TPU v7x, 512 devices: a whole 4x4x16 slice. The times are simulated.
512 devices in a mesh: gx: 16 (over z), gy: 16 (over x_lo, y, core), gz: 2 (over x_hi).
Axes of the slice: x: 4 (x_hi: 2, x_lo: 2; x = x_hi * 2 + x_lo), y: 4, z: 16, core: 2. Of those that a mesh axis runs over, the one named last changes fastest.
Arguments:
- features: bfloat16 [16, 16, 2, 1, 96, 512], P('gx', 'gy', 'gz'), may hold values from -6 to 6
- cotangent: bfloat16 [16, 16, 2, 1, 96, 512], P('gx', 'gy', 'gz'), may hold values from -6 to 6
- first_weight: bfloat16 [27, 96, 96], replicated, may hold values from -0.1875 to 0.1875
- second_weight: bfloat16 [27, 96, 96], replicated, may hold values from -0.1875 to 0.1875
- slot_position: int32 [16, 16, 2, 1], P('gx', 'gy', 'gz'), may hold values from 0 to 7, as said below
- brick_count: int32 [16, 16, 2], P('gx', 'gy', 'gz'), may hold values from 0 to 1, as said below
- column_code: int32 [16, 16, 2, 1, 64], P('gx', 'gy', 'gz'), may hold values from 0 to 63
Outputs:
- grad_input: bfloat16 [16, 16, 2, 1, 96, 512], P('gx', 'gy', 'gz')
- grad_first: float32 [27, 96, 96], replicated
- grad_second: float32 [27, 96, 96], replicated
Inputs may be any that keep to these rules, and one draw needn't show every extreme that they name: `slot_position`: within one device the slots hold distinct positions of 0 to 7. `brick_count`: slots from this number on are empty: their features, cotangents and codes carry no meaning; some device has 1.
All inputs are finite; a program needn't handle non-finite values.
Results may differ from a plain program's by a relative error of at most 0.0034.
Values may be sent and summed in bfloat16 or wider, within the bound.
A program may use at most 64 MiB of HBM per device.

v0:
```python
import jax
import jax.numpy as jnp
from jax import lax
from jax.sharding import PartitionSpec as P

RX = 2
RY = 2
RZ = 2


def padded_2(block, sides, width):
    for axis, dim in sides:
        count = lax.axis_size(axis)
        forward = [(i, i + 1) for i in range(count - 1)]
        backward = [(target, source) for source, target in forward]
        low = lax.ppermute(
            lax.slice_in_dim(block, block.shape[dim] - width, None, axis=dim), axis, forward
        )
        high = lax.ppermute(lax.slice_in_dim(block, 0, width, axis=dim), axis, backward)
        block = jnp.concatenate([low, block, high], axis=dim)
    return block


def voxel_mask(column_codes, live_count, slots):
    levels = jnp.arange(8, dtype=jnp.int32)
    lowest = column_codes // 8
    beyond = lowest + column_codes % 8 + 1
    inside = (levels[None, None, :] >= lowest[:, :, None]) & (
        levels[None, None, :] < beyond[:, :, None]
    )
    living = jnp.arange(slots, dtype=jnp.int32) < live_count
    return (inside & living[:, None, None]).reshape(slots, 512).astype(jnp.float32)


def to_region(bricks):
    channels = bricks.shape[1]
    blocks = bricks.reshape(RX, RY, RZ, channels, 8, 8, 8)
    blocks = blocks.transpose(3, 0, 4, 1, 5, 2, 6)
    return blocks.reshape(channels, RX * 8, RY * 8, RZ * 8)


def cut_patches(padded, positions):

    def single(position):
        corner_x = position // (RY * RZ) * 8
        corner_y = position // RZ % RY * 8
        corner_z = position % RZ * 8
        anchor = jnp.zeros((), jnp.int32)
        return lax.dynamic_slice(
            padded, (anchor, corner_x, corner_y, corner_z), (padded.shape[0], 10, 10, 10)
        )

    return jax.vmap(single)(positions)


def block_cols(patches, step_x, facing):
    gathered = []
    for step_y in (-1, 0, 1):
        for step_z in (-1, 0, 1):
            start_x = 1 + facing * step_x
            start_y = 1 + facing * step_y
            start_z = 1 + facing * step_z
            sliced = patches[
                :, :, start_x : start_x + 8, start_y : start_y + 8, start_z : start_z + 8
            ]
            gathered.append(sliced.reshape(patches.shape[0], patches.shape[1], 512))
    return jnp.concatenate(gathered, axis=1)


def shards(
    features, cotangent, first_weight, second_weight, slot_position, brick_count, column_code
):
    slots = features.shape[3]
    channels = features.shape[4]
    positions = slot_position.reshape(slots)
    occupied = voxel_mask(column_code.reshape(slots, 64), brick_count.reshape(()), slots)
    cut_mask = occupied[:, None, :].astype(jnp.bfloat16)
    inputs = features.reshape(slots, channels, 512) * cut_mask
    upstream = cotangent.reshape(slots, channels, 512) * cut_mask
    placing = (positions[:, None] == jnp.arange(RX * RY * RZ, dtype=jnp.int32)[None, :]).astype(
        jnp.bfloat16
    )
    total = slots * lax.axis_size("gx") * lax.axis_size("gy") * lax.axis_size("gz")
    scale = total ** (-0.5) / 8.0

    def regional(bricks):
        spread = jnp.einsum("sr,scv->rcv", placing, bricks, preferred_element_type=jnp.float32)
        return to_region(spread.astype(jnp.bfloat16))

    joined = regional(jnp.concatenate([inputs, upstream], axis=1))
    padded = padded_2(joined, (("gx", 1), ("gy", 2), ("gz", 3)), 1)
    patches = cut_patches(padded, positions)
    input_patch = patches[:, :channels]
    upstream_patch = patches[:, channels:]
    first_blocks = first_weight.reshape(3, 9 * channels, channels)
    second_back = second_weight.transpose(0, 2, 1).reshape(3, 9 * channels, channels)
    first_back = first_weight.transpose(0, 2, 1).reshape(3, 9 * channels, channels)
    pre_act = jnp.zeros((slots, channels, 512), jnp.float32)
    back_act = jnp.zeros((slots, channels, 512), jnp.float32)
    for step_x in (-1, 0, 1):
        pre_act = pre_act + jnp.einsum(
            "sjv,jo->sov",
            block_cols(input_patch, step_x, 1),
            first_blocks[step_x + 1],
            preferred_element_type=jnp.float32,
        )
        back_act = back_act + jnp.einsum(
            "sjv,jc->scv",
            block_cols(upstream_patch, step_x, -1),
            second_back[step_x + 1],
            preferred_element_type=jnp.float32,
        )
    sigma = jax.nn.sigmoid(pre_act)
    hidden = (pre_act * sigma * occupied[:, None, :]).astype(jnp.bfloat16)
    delta = (back_act * sigma * (1.0 + pre_act * (1.0 - sigma)) * occupied[:, None, :]).astype(
        jnp.bfloat16
    )
    second_parts = []
    hidden_pad = padded_2(regional(hidden), (("gx", 1), ("gy", 2), ("gz", 3)), 1)
    hidden_patch = cut_patches(hidden_pad, positions)
    for step_x in (-1, 0, 1):
        second_term = jnp.einsum(
            "sjv,sov->jo",
            block_cols(hidden_patch, step_x, 1),
            upstream,
            preferred_element_type=jnp.float32,
        )
        second_parts.append(second_term.reshape(9, channels, channels))
    second_local = jnp.concatenate(second_parts, axis=0)
    delta_pad = padded_2(regional(delta), (("gx", 1), ("gy", 2), ("gz", 3)), 1)
    delta_patch = cut_patches(delta_pad, positions)
    back_input = upstream.astype(jnp.float32)
    first_parts = []
    for step_x in (-1, 0, 1):
        back_input = back_input + jnp.einsum(
            "sjv,jc->scv",
            block_cols(delta_patch, step_x, -1),
            first_back[step_x + 1],
            preferred_element_type=jnp.float32,
        )
        first_term = jnp.einsum(
            "sjv,sov->jo",
            block_cols(input_patch, step_x, 1),
            delta,
            preferred_element_type=jnp.float32,
        )
        first_parts.append(first_term.reshape(9, channels, channels))
    first_local = jnp.concatenate(first_parts, axis=0)
    grad_input = (back_input * occupied[:, None, :]).astype(jnp.bfloat16)
    first_total, second_total = lax.psum((first_local, second_local), ("gx", "gy", "gz"))
    first_grad = first_total * scale
    second_grad = second_total * scale
    return (grad_input.reshape(1, 1, 1, slots, channels, 512), first_grad, second_grad)


def solution(mesh):
    placed = (
        P("gx", "gy", "gz", None, None, None),
        P("gx", "gy", "gz", None, None, None),
        P(),
        P(),
        P("gx", "gy", "gz", None),
        P("gx", "gy", "gz"),
        P("gx", "gy", "gz", None, None),
    )
    return jax.shard_map(
        shards,
        mesh=mesh,
        in_specs=placed,
        out_specs=(P("gx", "gy", "gz", None, None, None), P(), P()),
        check_vma=False,
    )
```

profile of v0, /device:TPU:1, one launch (start us, length us, event | category | flops | bytes accessed | tf_op | source)
XLA Modules:
  0.0 638.1 jit_solution(9033802837924944688)
XLA Ops:
  9.6 1.0 bitcast_multiply_fusion.1
  11.8 4.4 collective-permute-start
  16.1 1.3 collective-permute-start.1
  18.1 4.0 collective-permute-done.1
  22.1 5.2 collective-permute-start.2
  27.3 2.8 collective-permute-start.3
  30.1 0.9 fusion.75
  31.0 2.8 collective-permute-done.3
  33.8 1.6 pad_maximum_fusion.2
  35.3 5.4 collective-permute-start.4
  40.7 1.5 collective-permute-start.5
  42.2 0.7 fusion.74
  42.9 0.8 copy.12
  44.0 0.8 copy.14
  44.8 1.8 copy.18
  46.6 0.8 copy.19
  48.1 3.4 collective-permute-done.5
  51.5 3.0 fusion.25
  54.5 1.8 fusion.72
  56.3 2.2 fusion.73
  58.5 1.4 fusion.71
  59.9 1.6 concatenate.88
  61.5 1.3 copy.20
  62.8 1.1 fusion.17
  63.9 1.8 concatenate.89
  65.6 1.3 copy.21
  66.9 1.5 concatenate.90
  68.4 1.3 copy.22
  69.7 1.7 concatenate.85
  71.4 1.1 fusion.21
  72.5 2.2 convolution_add_fusion.1
  74.7 1.7 concatenate.86
  76.5 1.1 convolution_add_fusion.3
  77.6 1.5 fusion.45
  79.3 1.5 concatenate.87
  82.1 3.7 collective-permute-start.6
  85.8 1.3 collective-permute-start.7
  87.3 5.5 collective-permute-start.12
  92.8 1.3 collective-permute-start.13
  95.4 5.7 collective-permute-start.8
  101.0 1.9 collective-permute-start.9
  103.0 3.6 collective-permute-start.14
  106.7 1.9 collective-permute-start.15
  109.0 1.3 collective-permute-start.10
  110.3 1.5 collective-permute-start.11
  112.7 5.0 collective-permute-start.16
  117.7 1.3 collective-permute-start.17
  119.0 1.2 pad_maximum_fusion
  120.8 5.6 collective-permute-done.17
  126.4 2.1 fusion.32
  128.4 1.3 fusion.77
  129.8 0.9 fusion.78
  132.3 1.7 concatenate.102
  134.9 1.7 concatenate.103
  137.6 0.8 fusion.80
  138.4 1.2 pad_maximum_fusion.1
  139.6 1.2 fusion.79
  140.8 1.5 concatenate.94
  142.3 1.5 concatenate.95
  143.8 1.8 concatenate.96
  146.4 1.1 fusion.11
  147.5 479.9 %all-reduce.3.cloned.1.call-done = (f32[27,96,96]{2,1,0:T(8,128)}, f32[27,96,96]{2,1,0:T(8,128)}) async-done(((f32[27,96,96]{2,1,0:T(8,128)}, f32[27,96,96]{2,1,0:T(8,128)}), (f32[27,96,96]{2,1,0:T(8,128)}, f32[27,96,96]{2,1,0:T(8,128)})) %all-reduce.3.cloned.1.call-update) | async-done | bytes 1990672 | tf_op jit(solution)/shard_map/psum | solution.py:150
  627.5 2.6 broadcast_multiply_fusion
  630.1 1.2 broadcast_multiply_fusion.1
  (111 shorter events, 12.6 us)
Async XLA Ops:
  7.2 620.3 %all-reduce.3.cloned.1.call-start = ((), (), s32[]{:S(2)}) async-start(), calls=%async_computation | async-start | bytes 5308416 | tf_op jit(solution)/shard_map/psum | solution.py:150
  11.5 5.9 copy-start.11
  11.8 6.3 collective-permute-start
  16.1 5.9 collective-permute-start.1
  17.5 12.6 %copy-start.3 = (bf16[27,96,96]{2,1,0:T(8,128)(2,1)S(1)}, bf16[27,96,96]{2,1,0:T(8,128)(2,1)}, u32[]{:S(2)}) copy-start(bf16[27,96,96]{2,1,0:T(8,128)(2,1)} %param.9) | copy-start | bytes 1492996
  22.1 8.9 %collective-permute-start.2 = (bf16[192,18,1,16]{0,3,2,1:T(8,128)(2,1)S(1)}, bf16[192,18,1,16]{0,3,2,1:T(8,128)(2,1)S(1)}, u32[]{:S(2)}, u32[]{:S(2)}) collective-permute-start(bf16[192,18,1,16]{0,3,2,1:T(8,128)(2,1)S(1)} %get-tuple-element.44), channel_id=1, source_target_pairs={{0,2},{2,4},{4,6},{6,8},{8,10},{10,12},{12,14},{14,16},{16,18},{18... | collective-permute-start | bytes 331784 | tf_op jit(solution)/shard_map/ppermute | solution.py:16
  27.3 6.5 %collective-permute-start.3 = (bf16[192,18,1,16]{0,3,2,1:T(8,128)(2,1)S(1)}, bf16[192,18,1,16]{0,3,2,1:T(8,128)(2,1)S(1)}, u32[]{:S(2)}, u32[]{:S(2)}) collective-permute-start(bf16[192,18,1,16]{0,3,2,1:T(8,128)(2,1)S(1)} %get-tuple-element.45), channel_id=1, source_target_pairs={{2,0},{4,2},{6,4},{8,6},{10,8},{12,10},{14,12},{16,14},{18,16},{20... | collective-permute-start | bytes 331784 | tf_op jit(solution)/shard_map/ppermute | solution.py:19
  31.0 11.9 %copy-start.12 = (bf16[192,18,1,16]{0,3,2,1:T(8,128)(2,1)}, bf16[192,18,1,16]{0,3,2,1:T(8,128)(2,1)S(1)}, u32[]{:S(2)}) copy-start(bf16[192,18,1,16]{0,3,2,1:T(8,128)(2,1)S(1)} %collective-permute-done.2) | copy-start | bytes 331780
  33.8 9.2 %copy-start.13 = (bf16[192,18,1,16]{0,3,2,1:T(8,128)(2,1)}, bf16[192,18,1,16]{0,3,2,1:T(8,128)(2,1)S(1)}, u32[]{:S(2)}) copy-start(bf16[192,18,1,16]{0,3,2,1:T(8,128)(2,1)S(1)} %collective-permute-done.3) | copy-start | bytes 331780
  35.3 12.7 %collective-permute-start.4 = (bf16[192,18,18,1]{0,3,2,1:T(2,128)(2,1)}, bf16[192,18,18,1]{0,3,2,1:T(2,128)(2,1)}, u32[]{:S(2)}, u32[]{:S(2)}) collective-permute-start(bf16[192,18,18,1]{0,3,2,1:T(2,128)(2,1)} %get-tuple-element.43), channel_id=1, source_target_pairs={{0,1},{2,3},{4,5},{6,7},{8,9},{10,11},{12,13},{14,15},{16,17},{18,... | collective-permute-start | bytes 373256 | tf_op jit(solution)/shard_map/ppermute | solution.py:16
  40.7 10.8 %collective-permute-start.5 = (bf16[192,18,18,1]{0,3,2,1:T(2,128)(2,1)}, bf16[192,18,18,1]{0,3,2,1:T(2,128)(2,1)}, u32[]{:S(2)}, u32[]{:S(2)}) collective-permute-start(bf16[192,18,18,1]{0,3,2,1:T(2,128)(2,1)} %get-tuple-element.42), channel_id=1, source_target_pairs={{1,0},{3,2},{5,4},{7,6},{9,8},{11,10},{13,12},{15,14},{17,16},{19,... | collective-permute-start | bytes 373256 | tf_op jit(solution)/shard_map/ppermute | solution.py:19
  59.9 2.9 copy-start.9
  63.9 3.1 copy-start.21
  63.9 3.1 copy-start.22
  68.4 3.0 copy-start.8
  72.5 4.0 copy-start.10
  76.4 2.7 copy-start.14
  76.4 2.7 copy-start.15
  76.5 2.7 copy-start.16
  76.5 2.7 copy-start.17
  76.5 2.7 copy-start.18
  76.5 2.7 copy-start.19
  76.5 2.7 copy-start.20
  77.6 3.1 copy-start.23
  77.6 3.1 copy-start.24
  79.3 2.2 copy-start.25
  81.9 12.3 %copy-start.1 = (bf16[1,864,512]{2,1,0:T(8,128)(2,1)S(1)}, bf16[1,864,512]{2,1,0:T(8,128)(2,1)}, u32[]{:S(2)}) copy-start(bf16[1,864,512]{2,1,0:T(8,128)(2,1)} %copy.21) | copy-start | bytes 2654212
  82.1 12.5 %copy-start = (bf16[1,864,512]{2,1,0:T(8,128)(2,1)S(1)}, bf16[1,864,512]{2,1,0:T(8,128)(2,1)}, u32[]{:S(2)}) copy-start(bf16[1,864,512]{2,1,0:T(8,128)(2,1)} %copy.20) | copy-start | bytes 2654212
  82.1 13.2 %collective-permute-start.6 = (bf16[96,1,16,16]{0,3,2,1:T(8,128)(2,1)S(1)}, bf16[96,1,16,16]{0,3,2,1:T(8,128)(2,1)S(1)}, u32[]{:S(2)}, u32[]{:S(2)}) collective-permute-start(bf16[96,1,16,16]{0,3,2,1:T(8,128)(2,1)S(1)} %get-tuple-element.58), channel_id=1, source_target_pairs={{0,32},{32,64},{64,96},{96,128},{128,160},{160,192},{192,224},{224... | collective-permute-start | bytes 147464 | tf_op jit(solution)/shard_map/ppermute | solution.py:16
  85.8 9.5 %collective-permute-start.7 = (bf16[96,1,16,16]{0,3,2,1:T(8,128)(2,1)S(1)}, bf16[96,1,16,16]{0,3,2,1:T(8,128)(2,1)S(1)}, u32[]{:S(2)}, u32[]{:S(2)}) collective-permute-start(bf16[96,1,16,16]{0,3,2,1:T(8,128)(2,1)S(1)} %get-tuple-element.59), channel_id=1, source_target_pairs={{32,0},{64,32},{96,64},{128,96},{160,128},{192,160},{224,192},{256... | collective-permute-start | bytes 147464 | tf_op jit(solution)/shard_map/ppermute | solution.py:19
  87.3 7.6 %copy-start.2 = (bf16[1,864,512]{2,1,0:T(8,128)(2,1)S(1)}, bf16[1,864,512]{2,1,0:T(8,128)(2,1)}, u32[]{:S(2)}) copy-start(bf16[1,864,512]{2,1,0:T(8,128)(2,1)} %copy.22) | copy-start | bytes 2654212
  87.3 15.6 %collective-permute-start.12 = (bf16[96,1,16,16]{0,3,2,1:T(8,128)(2,1)S(1)}, bf16[96,1,16,16]{0,3,2,1:T(8,128)(2,1)S(1)}, u32[]{:S(2)}, u32[]{:S(2)}) collective-permute-start(bf16[96,1,16,16]{0,3,2,1:T(8,128)(2,1)S(1)} %get-tuple-element.56), channel_id=1, source_target_pairs={{0,32},{32,64},{64,96},{96,128},{128,160},{160,192},{192,224},{224... | collective-permute-start | bytes 147464 | tf_op jit(solution)/shard_map/ppermute | solution.py:16
  92.8 10.2 %collective-permute-start.13 = (bf16[96,1,16,16]{0,3,2,1:T(8,128)(2,1)S(1)}, bf16[96,1,16,16]{0,3,2,1:T(8,128)(2,1)S(1)}, u32[]{:S(2)}, u32[]{:S(2)}) collective-permute-start(bf16[96,1,16,16]{0,3,2,1:T(8,128)(2,1)S(1)} %get-tuple-element.57), channel_id=1, source_target_pairs={{32,0},{64,32},{96,64},{128,96},{160,128},{192,160},{224,192},{256... | collective-permute-start | bytes 147464 | tf_op jit(solution)/shard_map/ppermute | solution.py:19
  95.4 13.3 %collective-permute-start.8 = (bf16[96,18,1,16]{0,3,2,1:T(8,128)(2,1)S(1)}, bf16[96,18,1,16]{0,3,2,1:T(8,128)(2,1)S(1)}, u32[]{:S(2)}, u32[]{:S(2)}) collective-permute-start(bf16[96,18,1,16]{0,3,2,1:T(8,128)(2,1)S(1)} %get-tuple-element.54), channel_id=1, source_target_pairs={{0,2},{2,4},{4,6},{6,8},{8,10},{10,12},{12,14},{14,16},{16,18},{18... | collective-permute-start | bytes 165896 | tf_op jit(solution)/shard_map/ppermute | solution.py:16
  101.0 7.6 %collective-permute-start.9 = (bf16[96,18,1,16]{0,3,2,1:T(8,128)(2,1)S(1)}, bf16[96,18,1,16]{0,3,2,1:T(8,128)(2,1)S(1)}, u32[]{:S(2)}, u32[]{:S(2)}) collective-permute-start(bf16[96,18,1,16]{0,3,2,1:T(8,128)(2,1)S(1)} %get-tuple-element.55), channel_id=1, source_target_pairs={{2,0},{4,2},{6,4},{8,6},{10,8},{12,10},{14,12},{16,14},{18,16},{20... | collective-permute-start | bytes 165896 | tf_op jit(solution)/shard_map/ppermute | solution.py:19
  103.0 8.8 %collective-permute-start.14 = (bf16[96,18,1,16]{0,3,2,1:T(8,128)(2,1)S(1)}, bf16[96,18,1,16]{0,3,2,1:T(8,128)(2,1)S(1)}, u32[]{:S(2)}, u32[]{:S(2)}) collective-permute-start(bf16[96,18,1,16]{0,3,2,1:T(8,128)(2,1)S(1)} %get-tuple-element.52), channel_id=1, source_target_pairs={{0,2},{2,4},{4,6},{6,8},{8,10},{10,12},{12,14},{14,16},{16,18},{18... | collective-permute-start | bytes 165896 | tf_op jit(solution)/shard_map/ppermute | solution.py:16
  106.7 5.7 collective-permute-start.15
  109.0 11.2 %collective-permute-start.10 = (bf16[96,18,18,1]{0,3,2,1:T(2,128)(2,1)S(1)}, bf16[96,18,18,1]{0,3,2,1:T(2,128)(2,1)S(1)}, u32[]{:S(2)}, u32[]{:S(2)}) collective-permute-start(bf16[96,18,18,1]{0,3,2,1:T(2,128)(2,1)S(1)} %get-tuple-element.51), channel_id=1, source_target_pairs={{0,1},{2,3},{4,5},{6,7},{8,9},{10,11},{12,13},{14,15},{16,17},{18,... | collective-permute-start | bytes 186632 | tf_op jit(solution)/shard_map/ppermute | solution.py:16
  110.3 9.9 %collective-permute-start.11 = (bf16[96,18,18,1]{0,3,2,1:T(2,128)(2,1)S(1)}, bf16[96,18,18,1]{0,3,2,1:T(2,128)(2,1)S(1)}, u32[]{:S(2)}, u32[]{:S(2)}) collective-permute-start(bf16[96,18,18,1]{0,3,2,1:T(2,128)(2,1)S(1)} %get-tuple-element.50), channel_id=1, source_target_pairs={{1,0},{3,2},{5,4},{7,6},{9,8},{11,10},{13,12},{15,14},{17,16},{19,... | collective-permute-start | bytes 186632 | tf_op jit(solution)/shard_map/ppermute | solution.py:19
  112.7 8.1 %collective-permute-start.16 = (bf16[96,18,18,1]{0,3,2,1:T(2,128)(2,1)S(1)}, bf16[96,18,18,1]{0,3,2,1:T(2,128)(2,1)S(1)}, u32[]{:S(2)}, u32[]{:S(2)}) collective-permute-start(bf16[96,18,18,1]{0,3,2,1:T(2,128)(2,1)S(1)} %get-tuple-element.49), channel_id=1, source_target_pairs={{0,1},{2,3},{4,5},{6,7},{8,9},{10,11},{12,13},{14,15},{16,17},{18,... | collective-permute-start | bytes 186632 | tf_op jit(solution)/shard_map/ppermute | solution.py:16
  117.7 8.7 %collective-permute-start.17 = (bf16[96,18,18,1]{0,3,2,1:T(2,128)(2,1)S(1)}, bf16[96,18,18,1]{0,3,2,1:T(2,128)(2,1)S(1)}, u32[]{:S(2)}, u32[]{:S(2)}) collective-permute-start(bf16[96,18,18,1]{0,3,2,1:T(2,128)(2,1)S(1)} %get-tuple-element.48), channel_id=1, source_target_pairs={{1,0},{3,2},{5,4},{7,6},{9,8},{11,10},{13,12},{15,14},{17,16},{19,... | collective-permute-start | bytes 186632 | tf_op jit(solution)/shard_map/ppermute | solution.py:19
  130.7 1.2 copy-start.4
  142.3 3.3 copy-start.7
  143.8 2.2 copy-start.6
  627.5 2.6 copy-start.5
Sparse Core Ops, SparseCore 0:
  139.7 487.7 all-reduce.2
where the time goes:
time: 641 us; the launch traced here: 638 us
  waiting for transfers between devices  497 us (78%)
  starting transfers between devices  54.5 us (9%)
  local copies, waits for them, and re-layouts  41.5 us (6%)
  other arithmetic  16.8 us (3%)
  between operations  16.2 us (3%)
  matrix products  11.7 us (2%)
    psum x1, waiting for transfers between devices, shards(): lax.psum((first_local, second_local), ('gx', 'gy', 'gz'))  480 us
    ppermute x9, starting transfers between devices, padded_2(): lax.ppermute(lax.slice_in_dim(block, block.shape[dim] - width, None, axis...  39.7 us
    concatenate x18, local copies, waits for them, and re-layouts, block_cols(): return jnp.concatenate(gathered, axis=1)  24 us
    ppermute x9, waiting for transfers between devices, padded_2(): lax.ppermute(lax.slice_in_dim(block, 0, width, axis=dim), axis, backward)  16.3 us
    ppermute x9, starting transfers between devices, padded_2(): lax.ppermute(lax.slice_in_dim(block, 0, width, axis=dim), axis, backward)  14.8 us
  transfers between devices with their start and end apart: 19, of which 8 were waited for; matrix products, arithmetic and copies ran while one was open for 3% of the time, Pallas kernels for 0%

commit v1 on v0

--- a/solution.py
+++ b/solution.py
@@ -1,11 +1,209 @@
 import jax
 import jax.numpy as jnp
 from jax import lax
+from jax.experimental import pallas as pl
+from jax.experimental.pallas import tpu as pltpu
 from jax.sharding import PartitionSpec as P
 
 RX = 2
 RY = 2
 RZ = 2
+
+
+MESH = pl.DeviceIdType.MESH
+ROWS = 4096
+HALF = ROWS // 2
+PART = HALF // 16
+CELL = PART // 16
+
+
+def reduce_kernel(d_ref, out_ref, half_out, half_in, total, plane_out, plane_in, cell_src,
+                  line_in, line_all, own_part, gathered, pair_sem, plane_send, plane_recv,
+                  line_send, line_recv, line_send2, line_recv2, plane_send2, plane_recv2):
+    u = lax.axis_index("gx")
+    w = lax.axis_index("gy")
+    q = lax.axis_index("gz")
+    core = w % 2
+    y = w // 2 % 4
+    x = q * 2 + w // 8
+    chip = x * 4 + y
+    mate = (u, w + 1 - 2 * core, q)
+
+    def plane_peer(t):
+        px = (x + t // 4) % 4
+        py = (y + t % 4) % 4
+        return px * 4 + py, (u, ((px % 2) * 4 + py) * 2 + core, px // 2)
+
+    def line_peer(t):
+        z = (u + t) % 16
+        return z, (z, w, q)
+
+    barrier = pltpu.get_barrier_semaphore()
+    pl.semaphore_signal(barrier, inc=1, device_id=mate, device_id_type=MESH)
+
+    def greet(t, carry):
+        pl.semaphore_signal(barrier, inc=1, device_id=plane_peer(t)[1], device_id_type=MESH)
+        pl.semaphore_signal(barrier, inc=1, device_id=line_peer(t)[1], device_id_type=MESH)
+        return carry
+
+    lax.fori_loop(1, 16, greet, 0)
+    pl.semaphore_wait(barrier, 31)
+
+    other = pl.multiple_of((1 - core) * HALF, HALF)
+    own = pl.multiple_of(core * HALF, HALF)
+    half_out[...] = d_ref[pl.ds(other, HALF), :].astype(jnp.bfloat16)
+    swap = pltpu.make_async_remote_copy(
+        src_ref=half_out, dst_ref=half_in, send_sem=pair_sem.at[0], recv_sem=pair_sem.at[1],
+        device_id=mate, device_id_type=MESH)
+    swap.start()
+    swap.wait()
+    total[...] = d_ref[pl.ds(own, HALF), :] + half_in[...].astype(jnp.float32)
+    plane_out[...] = total[...].astype(jnp.bfloat16)
+
+    def plane_copy(t):
+        there, device = plane_peer(t)
+        return pltpu.make_async_remote_copy(
+            src_ref=plane_out.at[pl.ds(pl.multiple_of(there * PART, PART), PART), :],
+            dst_ref=plane_in.at[t], send_sem=plane_send.at[t], recv_sem=plane_recv.at[t],
+            device_id=device, device_id_type=MESH)
+
+    def plane_start(t, carry):
+        plane_copy(t).start()
+        return carry
+
+    lax.fori_loop(1, 16, plane_start, 0)
+    mine = pl.multiple_of(chip * PART, PART)
+
+    def plane_add(t, acc):
+        plane_copy(t).wait_recv()
+        return acc + plane_in[t].astype(jnp.float32)
+
+    cell_src[...] = lax.fori_loop(1, 16, plane_add, total[pl.ds(mine, PART), :])
+
+    def line_copy(t):
+        there, device = line_peer(t)
+        return pltpu.make_async_remote_copy(
+            src_ref=cell_src.at[pl.ds(pl.multiple_of(there * CELL, CELL), CELL), :],
+            dst_ref=line_in.at[t], send_sem=line_send.at[t], recv_sem=line_recv.at[t],
+            device_id=device, device_id_type=MESH)
+
+    def line_start(t, carry):
+        line_copy(t).start()
+        return carry
+
+    lax.fori_loop(1, 16, line_start, 0)
+    here = pl.multiple_of(u * CELL, CELL)
+
+    def line_add(t, acc):
+        line_copy(t).wait_recv()
+        return acc + line_in[t]
+
+    line_all[pl.ds(here, CELL), :] = lax.fori_loop(1, 16, line_add, cell_src[pl.ds(here, CELL), :])
+
+    def spread_copy(t):
+        there, device = line_peer(t)
+        return pltpu.make_async_remote_copy(
+            src_ref=line_all.at[pl.ds(here, CELL), :],
+            dst_ref=line_all.at[pl.ds(here, CELL), :], send_sem=line_send2.at[t], recv_sem=line_recv2.at[t],
+            device_id=device, device_id_type=MESH)
+
+    def arrive_copy(t):
+        z = (u - t + 16) % 16
+        rows = pl.ds(pl.multiple_of(z * CELL, CELL), CELL)
+        return pltpu.make_async_remote_copy(
+            src_ref=line_all.at[rows, :],
+            dst_ref=line_all.at[rows, :], send_sem=line_send2.at[t], recv_sem=line_recv2.at[t],
+            device_id=line_peer(t)[1], device_id_type=MESH)
+
+    def spread_start(t, carry):
+        spread_copy(t).start()
+        return carry
+
+    def spread_wait(t, carry):
+        arrive_copy(t).wait_recv()
+        return carry
+
+    lax.fori_loop(1, 16, spread_start, 0)
+    lax.fori_loop(1, 16, spread_wait, 0)
+    own_part[...] = line_all[...].astype(jnp.bfloat16)
+
+    place = pl.multiple_of(own + mine, PART)
+    gathered[pl.ds(place, PART), :] = own_part[...]
+
+    def back_copy(t):
+        there, device = plane_peer(t)
+        return pltpu.make_async_remote_copy(
+            src_ref=own_part,
+            dst_ref=gathered.at[pl.ds(place, PART), :], send_sem=plane_send2.at[t], recv_sem=plane_recv2.at[t],
+            device_id=device, device_id_type=MESH)
+
+    def back_arrive(t):
+        px = (x - t // 4 + 4) % 4
+        py = (y - t % 4 + 4) % 4
+        rows = pl.ds(pl.multiple_of(own + (px * 4 + py) * PART, PART), PART)
+        return pltpu.make_async_remote_copy(
+            src_ref=own_part,
+            dst_ref=gathered.at[rows, :], send_sem=plane_send2.at[t], recv_sem=plane_recv2.at[t],
+            device_id=plane_peer(t)[1], device_id_type=MESH)
+
+    def back_start(t, carry):
+        back_copy(t).start()
+        return carry
+
+    def back_wait(t, carry):
+        back_arrive(t).wait_recv()
+        return carry
+
+    lax.fori_loop(1, 16, back_start, 0)
+    lax.fori_loop(1, 16, back_wait, 0)
+
+    join = pltpu.make_async_remote_copy(
+        src_ref=gathered.at[pl.ds(own, HALF), :], dst_ref=gathered.at[pl.ds(own, HALF), :],
+        send_sem=pair_sem.at[2], recv_sem=pair_sem.at[3],
+        device_id=mate, device_id_type=MESH)
+    join.start()
+
+    def drain(t, carry):
+        plane_copy(t).wait_send()
+        line_copy(t).wait_send()
+        spread_copy(t).wait_send()
+        back_copy(t).wait_send()
+        return carry
+
+    lax.fori_loop(1, 16, drain, 0)
+    join.wait_send()
+    arrive = pltpu.make_async_remote_copy(
+        src_ref=gathered.at[pl.ds(other, HALF), :], dst_ref=gathered.at[pl.ds(other, HALF), :],
+        send_sem=pair_sem.at[2], recv_sem=pair_sem.at[3],
+        device_id=mate, device_id_type=MESH)
+    arrive.wait_recv()
+    out_ref[...] = gathered[...].astype(jnp.float32)
+
+
+def all_sum(data):
+    sems = lambda n: pltpu.SemaphoreType.DMA((n,))
+    return pl.pallas_call(
+        reduce_kernel,
+        out_shape=jax.ShapeDtypeStruct((ROWS, 128), jnp.float32),
+        in_specs=[pl.BlockSpec(memory_space=pltpu.VMEM)],
+        out_specs=pl.BlockSpec(memory_space=pltpu.VMEM),
+        scratch_shapes=[
+            pltpu.VMEM((HALF, 128), jnp.bfloat16),
+            pltpu.VMEM((HALF, 128), jnp.bfloat16),
+            pltpu.VMEM((HALF, 128), jnp.float32),
+            pltpu.VMEM((HALF, 128), jnp.bfloat16),
+            pltpu.VMEM((16, PART, 128), jnp.bfloat16),
+            pltpu.VMEM((PART, 128), jnp.float32),
+            pltpu.VMEM((16, CELL, 128), jnp.float32),
+            pltpu.VMEM((PART, 128), jnp.float32),
+            pltpu.VMEM((PART, 128), jnp.bfloat16),
+            pltpu.VMEM((ROWS, 128), jnp.bfloat16),
+            sems(4), sems(16), sems(16), sems(16), sems(16), sems(16), sems(16), sems(16), sems(16),
+        ],
+        compiler_params=pltpu.CompilerParams(
+            collective_id=3, has_side_effects=True, vmem_limit_bytes=32 * 2 ** 20),
+        name="all_sum",
+    )(data)
 
 
 def padded_2(block, sides, width):
@@ -147,9 +345,12 @@
         first_parts.append(first_term.reshape(9, channels, channels))
     first_local = jnp.concatenate(first_parts, axis=0)
     grad_input = (back_input * occupied[:, None, :]).astype(jnp.bfloat16)
-    first_total, second_total = lax.psum((first_local, second_local), ("gx", "gy", "gz"))
-    first_grad = first_total * scale
-    second_grad = second_total * scale
+    count = 27 * channels * channels
+    joined_grads = jnp.concatenate([first_local.reshape(-1), second_local.reshape(-1)]) * scale
+    padded_grads = jnp.pad(joined_grads, (0, ROWS * 128 - 2 * count)).reshape(ROWS, 128)
+    summed = all_sum(padded_grads).reshape(-1)
+    first_grad = summed[:count].reshape(27, channels, channels)
+    second_grad = summed[count : 2 * count].reshape(27, channels, channels)
     return (grad_input.reshape(1, 1, 1, slots, channels, 512), first_grad, second_grad)
 
 

time: 641 us -> 211 us (0.33)
  waiting for transfers between devices: 497 us -> 14.6 us
  Pallas kernels: 0 us -> 58.7 us
  between operations: 16.2 us -> 3.23 us
    psum x1 -> x0, waiting for transfers between devices: 480 us -> none  [shards(): lax.psum((first_local, second_local), ('gx', 'gy', 'gz'))]
    pallas_call x0 -> x1, Pallas kernels: none -> 58.7 us  [all_sum(): pl.pallas_call(reduce_kernel, out_shape=jax.ShapeDtypeStruct((ROWS, 128),...]
  transfers between devices with their start and end apart: 19 -> 18, of which waited for: 8 -> 5; matrix products, arithmetic and copies ran while one was open for 3% -> 6% of each run, Pallas kernels for 0% -> 0%
where the time goes in v1:
time: 211 us; the launch traced here: 210 us
  Pallas kernels  58.7 us (28%)
  starting transfers between devices  57.5 us (27%)
  local copies, waits for them, and re-layouts  47.5 us (23%)
  matrix products  15.8 us (7%)
  waiting for transfers between devices  14.6 us (7%)
  other arithmetic  13 us (6%)
  between operations  3.23 us (2%)
    pallas_call x1, Pallas kernels, all_sum(): pl.pallas_call(reduce_kernel, out_shape=jax.ShapeDtypeStruct((ROWS, 128),...  58.7 us
    ppermute x9, starting transfers between devices, padded_2(): lax.ppermute(lax.slice_in_dim(block, block.shape[dim] - width, None, axis...  43 us
    concatenate x18, local copies, waits for them, and re-layouts, block_cols(): return jnp.concatenate(gathered, axis=1)  21.4 us
    ppermute x9, starting transfers between devices, padded_2(): lax.ppermute(lax.slice_in_dim(block, 0, width, axis=dim), axis, backward)  14.5 us
    ppermute x9, waiting for transfers between devices, padded_2(): lax.ppermute(lax.slice_in_dim(block, 0, width, axis=dim), axis, backward)  14 us
    slice x7, local copies, waits for them, and re-layouts, block_cols(): patches[:, :, start_x:start_x + 8, start_y:start_y + 8, start_z:start_z + 8]  10.1 us
    slice x4, local copies, waits for them, and re-layouts, shards(): first_back[step_x + 1]  6.17 us
    gather x2, other arithmetic, single(): lax.dynamic_slice(padded, (anchor, corner_x, corner_y, corner_z), (padded...  5.92 us
  transfers between devices with their start and end apart: 18, of which 5 were waited for; matrix products, arithmetic and copies ran while one was open for 6% of the time, Pallas kernels for 0%

profile of v1, /device:TPU:1, one launch (start us, length us, event | category | flops | bytes accessed | tf_op | source)
XLA Modules:
  0.0 210.3 jit_solution(1963771876146365733)
XLA Ops:
  3.1 1.0 bitcast_multiply_fusion.1
  5.2 4.4 %collective-permute-start = (bf16[192,1,16,16]{0,3,2,1:T(8,128)(2,1)S(1)}, bf16[192,1,16,16]{0,3,2,1:T(8,128)(2,1)S(1)}, u32[]{:S(2)}, u32[]{:S(2)}) collective-permute-start(bf16[192,1,16,16]{0,3,2,1:T(8,128)(2,1)S(1)} %get-tuple-element.46), channel_id=1, source_target_pairs={{0,32},{32,64},{64,96},{96,128},{128,160},{160,192},{192,224},{224... | collective-permute-start | bytes 294920 | tf_op jit(solution)/shard_map/ppermute | solution.py:214
  9.6 1.3 collective-permute-start.1
  11.5 4.0 %collective-permute-done.1 = bf16[192,1,16,16]{0,3,2,1:T(8,128)(2,1)S(1)} collective-permute-done((bf16[192,1,16,16]{0,3,2,1:T(8,128)(2,1)S(1)}, bf16[192,1,16,16]{0,3,2,1:T(8,128)(2,1)S(1)}, u32[]{:S(2)}, u32[]{:S(2)}) %collective-permute-start.1) | collective-permute-done | bytes 98336 | tf_op jit(solution)/shard_map/ppermute | solution.py:217
  15.5 5.2 %collective-permute-start.2 = (bf16[192,18,1,16]{0,3,2,1:T(8,128)(2,1)S(1)}, bf16[192,18,1,16]{0,3,2,1:T(8,128)(2,1)S(1)}, u32[]{:S(2)}, u32[]{:S(2)}) collective-permute-start(bf16[192,18,1,16]{0,3,2,1:T(8,128)(2,1)S(1)} %get-tuple-element.42), channel_id=1, source_target_pairs={{0,2},{2,4},{4,6},{6,8},{8,10},{10,12},{12,14},{14,16},{16,18},{18... | collective-permute-start | bytes 331784 | tf_op jit(solution)/shard_map/ppermute | solution.py:214
  20.7 2.8 %collective-permute-start.3 = (bf16[192,18,1,16]{0,3,2,1:T(8,128)(2,1)S(1)}, bf16[192,18,1,16]{0,3,2,1:T(8,128)(2,1)S(1)}, u32[]{:S(2)}, u32[]{:S(2)}) collective-permute-start(bf16[192,18,1,16]{0,3,2,1:T(8,128)(2,1)S(1)} %get-tuple-element.43), channel_id=1, source_target_pairs={{2,0},{4,2},{6,4},{8,6},{10,8},{12,10},{14,12},{16,14},{18,16},{20... | collective-permute-start | bytes 331784 | tf_op jit(solution)/shard_map/ppermute | solution.py:217
  23.5 0.9 fusion.76
  24.4 2.8 %collective-permute-done.3 = bf16[192,18,1,16]{0,3,2,1:T(8,128)(2,1)S(1)} collective-permute-done((bf16[192,18,1,16]{0,3,2,1:T(8,128)(2,1)S(1)}, bf16[192,18,1,16]{0,3,2,1:T(8,128)(2,1)S(1)}, u32[]{:S(2)}, u32[]{:S(2)}) %collective-permute-start.3) | collective-permute-done | bytes 110624 | tf_op jit(solution)/shard_map/ppermute | solution.py:217
  27.2 1.6 pad_maximum_fusion.2
  28.8 5.4 %collective-permute-start.4 = (bf16[192,18,18,1]{0,3,2,1:T(2,128)(2,1)}, bf16[192,18,18,1]{0,3,2,1:T(2,128)(2,1)}, u32[]{:S(2)}, u32[]{:S(2)}) collective-permute-start(bf16[192,18,18,1]{0,3,2,1:T(2,128)(2,1)} %get-tuple-element.41), channel_id=1, source_target_pairs={{0,1},{2,3},{4,5},{6,7},{8,9},{10,11},{12,13},{14,15},{16,17},{18,... | collective-permute-start | bytes 373256 | tf_op jit(solution)/shard_map/ppermute | solution.py:214
  34.2 1.3 collective-permute-start.5
  37.5 1.8 copy.18
  39.3 1.8 copy.19
  41.1 1.8 copy.17
  42.8 2.1 collective-permute-done.5
  44.9 2.9 %fusion.25 = bf16[1,192,10,10,10]{1,4,3,2,0:T(8,128)(2,1)S(1)} fusion(s32[]{:T(128)} %bitcast.12, s32[]{:T(128)} %bitcast.13, s32[]{:T(128)} %bitcast.14, bf16[192,18,18,1]{0,3,2,1:T(2,128)(2,1)} %collective-permute-done.4, bf16[192,18,1,16]{0,3,2,1:T(8,128)(2,1)S(1)} %copy-done.19, bf16[192,1,16,16]{0,3,2,1:T(8,128)(2,1)S(1)} %collective-permute-done, ...), kind=kLoop, calls=%fused_computation.60 | loop fusion | flops 2688000 | bytes 2623500 | tf_op jit(solution)/shard_map/vmap()/gather | solution.py:247
  47.9 1.8 fusion.73
  49.7 2.2 %fusion.74 = (bf16[1,96,8,8,8]{1,4,3,2,0:T(8,128)(2,1)}, bf16[1,96,8,8,8]{1,4,3,2,0:T(8,128)(2,1)}, bf16[1,96,8,8,8]{1,4,3,2,0:T(8,128)(2,1)}, bf16[1,96,8,8,8]{...) fusion(bf16[1,192,10,10,10]{1,4,3,2,0:T(8,128)(2,1)S(1)} %fusion.25), kind=kLoop, calls=%fused_computation.148 | loop fusion | bytes 3145728 | tf_op jit(solution)/shard_map/slice | solution.py:261
  51.8 1.5 fusion.72
  54.0 1.3 copy.20
  55.3 1.1 fusion.17
  56.5 1.8 concatenate.93
  58.3 1.3 copy.22
  59.6 1.5 concatenate.92
  61.1 1.3 copy.21
  62.4 1.8 concatenate.88
  64.2 1.1 fusion.21
  65.3 2.1 convolution_add_fusion.1
  67.4 1.7 concatenate.89
  69.2 1.1 convolution_add_fusion.3
  70.3 2.2 %fusion.45 = (f32[96,512]{1,0:T(8,128)}, f32[96,512]{1,0:T(8,128)S(1)}) fusion(f32[512]{0:T(512)S(1)} %get-tuple-element.37, f32[512,96]{0,1:T(8,128)} %convolution_add_fusion.1, bf16[864,96]{1,0:T(8,128)(2,1)} %bitcast.423, bf16[1,864,512]{1,2,0:T(8,128)(2,1)S(1)} %concatenate.93), kind=kOutput, calls=%fused_computation.101 | convolution fusion | flops 85327872 | bytes 1642496 | tf_op jit(solution)/shard_map/sjv,jo->sov/dot_general | solution.py:299
  72.6 1.4 concatenate.90
  74.1 1.7 fusion.9
  75.9 1.1 fusion.52
  77.1 1.1 fusion.54
  78.2 1.2 fusion.56
  80.2 3.6 %collective-permute-start.6 = (bf16[96,1,16,16]{0,3,2,1:T(8,128)(2,1)S(1)}, bf16[96,1,16,16]{0,3,2,1:T(8,128)(2,1)S(1)}, u32[]{:S(2)}, u32[]{:S(2)}) collective-permute-start(bf16[96,1,16,16]{0,3,2,1:T(8,128)(2,1)S(1)} %get-tuple-element.58), channel_id=1, source_target_pairs={{0,32},{32,64},{64,96},{96,128},{128,160},{160,192},{192,224},{224... | collective-permute-start | bytes 147464 | tf_op jit(solution)/shard_map/ppermute | solution.py:214
  83.8 1.3 collective-permute-start.7
  85.3 5.4 %collective-permute-start.12 = (bf16[96,1,16,16]{0,3,2,1:T(8,128)(2,1)S(1)}, bf16[96,1,16,16]{0,3,2,1:T(8,128)(2,1)S(1)}, u32[]{:S(2)}, u32[]{:S(2)}) collective-permute-start(bf16[96,1,16,16]{0,3,2,1:T(8,128)(2,1)S(1)} %get-tuple-element.56), channel_id=1, source_target_pairs={{0,32},{32,64},{64,96},{96,128},{128,160},{160,192},{192,224},{224... | collective-permute-start | bytes 147464 | tf_op jit(solution)/shard_map/ppermute | solution.py:214
  90.7 1.3 collective-permute-start.13
  92.1 5.6 %collective-permute-start.8 = (bf16[96,18,1,16]{0,3,2,1:T(8,128)(2,1)S(1)}, bf16[96,18,1,16]{0,3,2,1:T(8,128)(2,1)S(1)}, u32[]{:S(2)}, u32[]{:S(2)}) collective-permute-start(bf16[96,18,1,16]{0,3,2,1:T(8,128)(2,1)S(1)} %get-tuple-element.54), channel_id=1, source_target_pairs={{0,2},{2,4},{4,6},{6,8},{8,10},{10,12},{12,14},{14,16},{16,18},{18... | collective-permute-start | bytes 165896 | tf_op jit(solution)/shard_map/ppermute | solution.py:214
  97.7 1.9 collective-permute-start.9
  99.8 3.9 %collective-permute-start.14 = (bf16[96,18,1,16]{0,3,2,1:T(8,128)(2,1)S(1)}, bf16[96,18,1,16]{0,3,2,1:T(8,128)(2,1)S(1)}, u32[]{:S(2)}, u32[]{:S(2)}) collective-permute-start(bf16[96,18,1,16]{0,3,2,1:T(8,128)(2,1)S(1)} %get-tuple-element.52), channel_id=1, source_target_pairs={{0,2},{2,4},{4,6},{6,8},{8,10},{10,12},{12,14},{14,16},{16,18},{18... | collective-permute-start | bytes 165896 | tf_op jit(solution)/shard_map/ppermute | solution.py:214
  103.7 2.1 collective-permute-start.15
  105.8 1.1 pad_maximum_fusion.12
  106.9 2.8 %collective-permute-start.10 = (bf16[96,18,18,1]{0,3,2,1:T(2,128)(2,1)}, bf16[96,18,18,1]{0,3,2,1:T(2,128)(2,1)}, u32[]{:S(2)}, u32[]{:S(2)}) collective-permute-start(bf16[96,18,18,1]{0,3,2,1:T(2,128)(2,1)} %get-tuple-element.51), channel_id=1, source_target_pairs={{0,1},{2,3},{4,5},{6,7},{8,9},{10,11},{12,13},{14,15},{16,17},{18,... | collective-permute-start | bytes 186632 | tf_op jit(solution)/shard_map/ppermute | solution.py:214
  109.6 1.3 collective-permute-start.11
  111.0 1.1 pad_maximum_fusion.7
  112.1 6.8 %collective-permute-start.16 = (bf16[96,18,18,1]{0,3,2,1:T(2,128)(2,1)}, bf16[96,18,18,1]{0,3,2,1:T(2,128)(2,1)}, u32[]{:S(2)}, u32[]{:S(2)}) collective-permute-start(bf16[96,18,18,1]{0,3,2,1:T(2,128)(2,1)} %get-tuple-element.49), channel_id=1, source_target_pairs={{0,1},{2,3},{4,5},{6,7},{8,9},{10,11},{12,13},{14,15},{16,17},{18,... | collective-permute-start | bytes 186632 | tf_op jit(solution)/shard_map/ppermute | solution.py:214
  118.9 1.3 collective-permute-start.17
  120.3 1.8 reshape.999
  122.1 5.2 %collective-permute-done.17 = bf16[96,18,18,1]{0,3,2,1:T(2,128)(2,1)} collective-permute-done((bf16[96,18,18,1]{0,3,2,1:T(2,128)(2,1)}, bf16[96,18,18,1]{0,3,2,1:T(2,128)(2,1)}, u32[]{:S(2)}, u32[]{:S(2)}) %collective-permute-start.17) | collective-permute-done | bytes 62240 | tf_op jit(solution)/shard_map/ppermute | solution.py:217
  127.2 3.0 %fusion.32 = (bf16[1,96,10,10,10]{1,4,3,2,0:T(8,128)(2,1)S(1)}, bf16[1,96,10,10,10]{1,4,3,2,0:T(8,128)(2,1)S(1)}) fusion(s32[]{:T(128)} %bitcast.12, s32[]{:T(128)} %bitcast.13, s32[]{:T(128)} %bitcast.14, bf16[96,18,18,1]{0,3,2,1:T(2,128)(2,1)} %collective-permute-done.16, bf16[96,18,1,16]{0,3,2,1:T(8,128)(2,1)} %copy-done.59, ...), kind=kLoop, calls=%fused_computation.67 | loop fusion | flops 2688000 | bytes 2623500 | tf_op jit(solution)/shard_map/vmap()/gather | solution.py:247
  130.2 1.2 fusion.78
  131.4 0.9 fusion.79
  132.3 1.5 fusion.80
  133.8 1.0 fusion.81
  136.5 1.6 concatenate.105
  139.0 1.6 concatenate.106
  143.1 58.7 %all_sum.1 = f32[4096,128]{1,0:T(8,128)S(1)} custom-call(f32[4096,128]{1,0:T(8,128)S(1)} %pad_bitcast_fusion.d_ref), custom_call_target="tpu_custom_call" | custom-call | tf_op jit(solution)/shard_map/all_sum/pallas_call | solution.py:185
  202.0 1.4 reshape.1031
  203.4 1.4 reshape.1032
  206.2 1.7 concatenate.99
  209.2 1.1 fusion.11
  (198 shorter events, 14.5 us)
Async XLA Ops:
  3.1 71.0 %copy-start.66 = (f32[512]{0:T(512)}, f32[512]{0:T(512)S(1)}, u32[]{:S(2)}) copy-start(f32[512]{0:T(512)S(1)} %get-tuple-element.37) | copy-start | bytes 6148
  5.0 5.9 %copy-start.15 = (bf16[27,96,96]{2,1,0:T(8,128)(2,1)S(1)}, bf16[27,96,96]{2,1,0:T(8,128)(2,1)}, u32[]{:S(2)}) copy-start(bf16[27,96,96]{2,1,0:T(8,128)(2,1)} %param.10) | copy-start | bytes 1492996
  5.2 6.3 %collective-permute-start = (bf16[192,1,16,16]{0,3,2,1:T(8,128)(2,1)S(1)}, bf16[192,1,16,16]{0,3,2,1:T(8,128)(2,1)S(1)}, u32[]{:S(2)}, u32[]{:S(2)}) collective-permute-start(bf16[192,1,16,16]{0,3,2,1:T(8,128)(2,1)S(1)} %get-tuple-element.46), channel_id=1, source_target_pairs={{0,32},{32,64},{64,96},{96,128},{128,160},{160,192},{192,224},{224... | collective-permute-start | bytes 294920 | tf_op jit(solution)/shard_map/ppermute | solution.py:214
  9.6 5.9 %collective-permute-start.1 = (bf16[192,1,16,16]{0,3,2,1:T(8,128)(2,1)S(1)}, bf16[192,1,16,16]{0,3,2,1:T(8,128)(2,1)S(1)}, u32[]{:S(2)}, u32[]{:S(2)}) collective-permute-start(bf16[192,1,16,16]{0,3,2,1:T(8,128)(2,1)S(1)} %get-tuple-element.47), channel_id=1, source_target_pairs={{32,0},{64,32},{96,64},{128,96},{160,128},{192,160},{224,192},{256... | collective-permute-start | bytes 294920 | tf_op jit(solution)/shard_map/ppermute | solution.py:217
  10.9 12.6 %copy-start.4 = (bf16[27,96,96]{2,1,0:T(8,128)(2,1)S(1)}, bf16[27,96,96]{2,1,0:T(8,128)(2,1)}, u32[]{:S(2)}) copy-start(bf16[27,96,96]{2,1,0:T(8,128)(2,1)} %param.9) | copy-start | bytes 1492996
  15.5 8.9 %collective-permute-start.2 = (bf16[192,18,1,16]{0,3,2,1:T(8,128)(2,1)S(1)}, bf16[192,18,1,16]{0,3,2,1:T(8,128)(2,1)S(1)}, u32[]{:S(2)}, u32[]{:S(2)}) collective-permute-start(bf16[192,18,1,16]{0,3,2,1:T(8,128)(2,1)S(1)} %get-tuple-element.42), channel_id=1, source_target_pairs={{0,2},{2,4},{4,6},{6,8},{8,10},{10,12},{12,14},{14,16},{16,18},{18... | collective-permute-start | bytes 331784 | tf_op jit(solution)/shard_map/ppermute | solution.py:214
  20.7 6.5 %collective-permute-start.3 = (bf16[192,18,1,16]{0,3,2,1:T(8,128)(2,1)S(1)}, bf16[192,18,1,16]{0,3,2,1:T(8,128)(2,1)S(1)}, u32[]{:S(2)}, u32[]{:S(2)}) collective-permute-start(bf16[192,18,1,16]{0,3,2,1:T(8,128)(2,1)S(1)} %get-tuple-element.43), channel_id=1, source_target_pairs={{2,0},{4,2},{6,4},{8,6},{10,8},{12,10},{14,12},{16,14},{18,16},{20... | collective-permute-start | bytes 331784 | tf_op jit(solution)/shard_map/ppermute | solution.py:217
  24.4 11.9 %copy-start.18 = (bf16[192,18,1,16]{0,3,2,1:T(8,128)(2,1)}, bf16[192,18,1,16]{0,3,2,1:T(8,128)(2,1)S(1)}, u32[]{:S(2)}) copy-start(bf16[192,18,1,16]{0,3,2,1:T(8,128)(2,1)S(1)} %collective-permute-done.2) | copy-start | bytes 331780
  27.2 9.1 %copy-start.20 = (bf16[192,18,1,16]{0,3,2,1:T(8,128)(2,1)}, bf16[192,18,1,16]{0,3,2,1:T(8,128)(2,1)S(1)}, u32[]{:S(2)}) copy-start(bf16[192,18,1,16]{0,3,2,1:T(8,128)(2,1)S(1)} %collective-permute-done.3) | copy-start | bytes 331780
  28.8 14.1 %collective-permute-start.4 = (bf16[192,18,18,1]{0,3,2,1:T(2,128)(2,1)}, bf16[192,18,18,1]{0,3,2,1:T(2,128)(2,1)}, u32[]{:S(2)}, u32[]{:S(2)}) collective-permute-start(bf16[192,18,18,1]{0,3,2,1:T(2,128)(2,1)} %get-tuple-element.41), channel_id=1, source_target_pairs={{0,1},{2,3},{4,5},{6,7},{8,9},{10,11},{12,13},{14,15},{16,17},{18,... | collective-permute-start | bytes 373256 | tf_op jit(solution)/shard_map/ppermute | solution.py:214
  34.2 10.8 %collective-permute-start.5 = (bf16[192,18,18,1]{0,3,2,1:T(2,128)(2,1)}, bf16[192,18,18,1]{0,3,2,1:T(2,128)(2,1)}, u32[]{:S(2)}, u32[]{:S(2)}) collective-permute-start(bf16[192,18,18,1]{0,3,2,1:T(2,128)(2,1)} %get-tuple-element.40), channel_id=1, source_target_pairs={{1,0},{3,2},{5,4},{7,6},{9,8},{11,10},{13,12},{15,14},{17,16},{19,... | collective-permute-start | bytes 373256 | tf_op jit(solution)/shard_map/ppermute | solution.py:217
  36.5 8.5 %copy-start.19 = (bf16[192,18,1,16]{0,3,2,1:T(8,128)(2,1)S(1)}, bf16[192,18,1,16]{0,3,2,1:T(8,128)(2,1)}, u32[]{:S(2)}) copy-start(bf16[192,18,1,16]{0,3,2,1:T(8,128)(2,1)} %copy-done.18) | copy-start | bytes 331780
  56.4 3.1 %copy-start.50 = (bf16[1,96,8,8,8]{1,4,3,2,0:T(8,128)(2,1)S(1)}, bf16[1,96,8,8,8]{1,4,3,2,0:T(8,128)(2,1)}, u32[]{:S(2)}) copy-start(bf16[1,96,8,8,8]{1,4,3,2,0:T(8,128)(2,1)} %get-tuple-element.68) | copy-start | bytes 294916
  56.5 3.1 %copy-start.51 = (bf16[1,96,8,8,8]{1,4,3,2,0:T(8,128)(2,1)S(1)}, bf16[1,96,8,8,8]{1,4,3,2,0:T(8,128)(2,1)}, u32[]{:S(2)}) copy-start(bf16[1,96,8,8,8]{1,4,3,2,0:T(8,128)(2,1)} %get-tuple-element.69) | copy-start | bytes 294916
  56.5 3.1 %copy-start.52 = (bf16[1,96,8,8,8]{1,4,3,2,0:T(8,128)(2,1)S(1)}, bf16[1,96,8,8,8]{1,4,3,2,0:T(8,128)(2,1)}, u32[]{:S(2)}) copy-start(bf16[1,96,8,8,8]{1,4,3,2,0:T(8,128)(2,1)} %get-tuple-element.70) | copy-start | bytes 294916
  56.5 3.1 %copy-start.53 = (bf16[1,96,8,8,8]{1,4,3,2,0:T(8,128)(2,1)S(1)}, bf16[1,96,8,8,8]{1,4,3,2,0:T(8,128)(2,1)}, u32[]{:S(2)}) copy-start(bf16[1,96,8,8,8]{1,4,3,2,0:T(8,128)(2,1)} %get-tuple-element.71) | copy-start | bytes 294916
  56.5 3.1 %copy-start.54 = (bf16[1,96,8,8,8]{1,4,3,2,0:T(8,128)(2,1)S(1)}, bf16[1,96,8,8,8]{1,4,3,2,0:T(8,128)(2,1)}, u32[]{:S(2)}) copy-start(bf16[1,96,8,8,8]{1,4,3,2,0:T(8,128)(2,1)} %get-tuple-element.72) | copy-start | bytes 294916
  56.5 3.1 %copy-start.55 = (bf16[1,96,8,8,8]{1,4,3,2,0:T(8,128)(2,1)S(1)}, bf16[1,96,8,8,8]{1,4,3,2,0:T(8,128)(2,1)}, u32[]{:S(2)}) copy-start(bf16[1,96,8,8,8]{1,4,3,2,0:T(8,128)(2,1)} %get-tuple-element.73) | copy-start | bytes 294916
  56.5 3.1 %copy-start.56 = (bf16[1,96,8,8,8]{1,4,3,2,0:T(8,128)(2,1)S(1)}, bf16[1,96,8,8,8]{1,4,3,2,0:T(8,128)(2,1)}, u32[]{:S(2)}) copy-start(bf16[1,96,8,8,8]{1,4,3,2,0:T(8,128)(2,1)} %get-tuple-element.74) | copy-start | bytes 294916
  62.4 2.9 %copy-start.12 = (bf16[9,96,96]{2,1,0:T(8,128)(2,1)S(1)}, bf16[9,96,96]{2,1,0:T(8,128)(2,1)}, u32[]{:S(2)}) copy-start(bf16[9,96,96]{2,1,0:T(8,128)(2,1)} %get-tuple-element.118) | copy-start | bytes 497668
  65.3 3.9 %copy-start.14 = (f32[512,96]{0,1:T(8,128)S(1)}, f32[512,96]{0,1:T(8,128)}, u32[]{:S(2)}) copy-start(f32[512,96]{0,1:T(8,128)} %fusion.21) | copy-start | bytes 589828
  69.1 3.4 %copy-start.21 = (bf16[1,96,8,8,8]{1,4,3,2,0:T(8,128)(2,1)S(1)}, bf16[1,96,8,8,8]{1,4,3,2,0:T(8,128)(2,1)}, u32[]{:S(2)}) copy-start(bf16[1,96,8,8,8]{1,4,3,2,0:T(8,128)(2,1)} %get-tuple-element.88) | copy-start | bytes 294916
  69.2 3.4 %copy-start.22 = (bf16[1,96,8,8,8]{1,4,3,2,0:T(8,128)(2,1)S(1)}, bf16[1,96,8,8,8]{1,4,3,2,0:T(8,128)(2,1)}, u32[]{:S(2)}) copy-start(bf16[1,96,8,8,8]{1,4,3,2,0:T(8,128)(2,1)} %get-tuple-element.89) | copy-start | bytes 294916
  69.2 3.4 %copy-start.23 = (bf16[1,96,8,8,8]{1,4,3,2,0:T(8,128)(2,1)S(1)}, bf16[1,96,8,8,8]{1,4,3,2,0:T(8,128)(2,1)}, u32[]{:S(2)}) copy-start(bf16[1,96,8,8,8]{1,4,3,2,0:T(8,128)(2,1)} %get-tuple-element.90) | copy-start | bytes 294916
  69.2 3.4 %copy-start.24 = (bf16[1,96,8,8,8]{1,4,3,2,0:T(8,128)(2,1)S(1)}, bf16[1,96,8,8,8]{1,4,3,2,0:T(8,128)(2,1)}, u32[]{:S(2)}) copy-start(bf16[1,96,8,8,8]{1,4,3,2,0:T(8,128)(2,1)} %get-tuple-element.91) | copy-start | bytes 294916
  69.2 3.4 %copy-start.25 = (bf16[1,96,8,8,8]{1,4,3,2,0:T(8,128)(2,1)S(1)}, bf16[1,96,8,8,8]{1,4,3,2,0:T(8,128)(2,1)}, u32[]{:S(2)}) copy-start(bf16[1,96,8,8,8]{1,4,3,2,0:T(8,128)(2,1)} %get-tuple-element.92) | copy-start | bytes 294916
  69.2 3.4 %copy-start.26 = (bf16[1,96,8,8,8]{1,4,3,2,0:T(8,128)(2,1)S(1)}, bf16[1,96,8,8,8]{1,4,3,2,0:T(8,128)(2,1)}, u32[]{:S(2)}) copy-start(bf16[1,96,8,8,8]{1,4,3,2,0:T(8,128)(2,1)} %get-tuple-element.93) | copy-start | bytes 294916
  69.2 3.4 %copy-start.27 = (bf16[1,96,8,8,8]{1,4,3,2,0:T(8,128)(2,1)S(1)}, bf16[1,96,8,8,8]{1,4,3,2,0:T(8,128)(2,1)}, u32[]{:S(2)}) copy-start(bf16[1,96,8,8,8]{1,4,3,2,0:T(8,128)(2,1)} %get-tuple-element.94) | copy-start | bytes 294916
  69.2 3.4 %copy-start.28 = (bf16[1,96,8,8,8]{1,4,3,2,0:T(8,128)(2,1)S(1)}, bf16[1,96,8,8,8]{1,4,3,2,0:T(8,128)(2,1)}, u32[]{:S(2)}) copy-start(bf16[1,96,8,8,8]{1,4,3,2,0:T(8,128)(2,1)} %get-tuple-element.95) | copy-start | bytes 294916
  70.3 3.7 %copy-start.61 = (bf16[9,96,96]{2,1,0:T(8,128)(2,1)S(1)}, bf16[9,96,96]{2,1,0:T(8,128)(2,1)}, u32[]{:S(2)}) copy-start(bf16[9,96,96]{2,1,0:T(8,128)(2,1)} %copy.14) | copy-start | bytes 497668
  70.3 3.7 %copy-start.63 = (f32[512,96]{0,1:T(8,128)S(1)}, f32[512,96]{0,1:T(8,128)}, u32[]{:S(2)}) copy-start(f32[512,96]{0,1:T(8,128)} %convolution_add_fusion.3) | copy-start | bytes 589828
  72.6 3.3 %copy-start.2 = (bf16[1,864,512]{2,1,0:T(8,128)(2,1)S(1)}, bf16[1,864,512]{2,1,0:T(8,128)(2,1)}, u32[]{:S(2)}) copy-start(bf16[1,864,512]{2,1,0:T(8,128)(2,1)} %copy.22) | copy-start | bytes 2654212
  74.1 3.0 %copy-start.3 = (bf16[1,864,512]{2,1,0:T(8,128)(2,1)S(1)}, bf16[1,864,512]{2,1,0:T(8,128)(2,1)}, u32[]{:S(2)}) copy-start(bf16[1,864,512]{2,1,0:T(8,128)(2,1)} %copy.21) | copy-start | bytes 2654212
  75.8 2.4 %copy-start.1 = (bf16[1,864,512]{2,1,0:T(8,128)(2,1)S(1)}, bf16[1,864,512]{2,1,0:T(8,128)(2,1)}, u32[]{:S(2)}) copy-start(bf16[1,864,512]{2,1,0:T(8,128)(2,1)} %copy.20) | copy-start | bytes 2654212
  75.9 3.5 %copy-start.62 = (f32[96,512]{1,0:T(8,128)S(1)}, f32[96,512]{1,0:T(8,128)}, u32[]{:S(2)}) copy-start(f32[96,512]{1,0:T(8,128)} %get-tuple-element.181) | copy-start | bytes 589828
  80.2 11.8 %collective-permute-start.6 = (bf16[96,1,16,16]{0,3,2,1:T(8,128)(2,1)S(1)}, bf16[96,1,16,16]{0,3,2,1:T(8,128)(2,1)S(1)}, u32[]{:S(2)}, u32[]{:S(2)}) collective-permute-start(bf16[96,1,16,16]{0,3,2,1:T(8,128)(2,1)S(1)} %get-tuple-element.58), channel_id=1, source_target_pairs={{0,32},{32,64},{64,96},{96,128},{128,160},{160,192},{192,224},{224... | collective-permute-start | bytes 147464 | tf_op jit(solution)/shard_map/ppermute | solution.py:214
  83.8 8.2 %collective-permute-start.7 = (bf16[96,1,16,16]{0,3,2,1:T(8,128)(2,1)S(1)}, bf16[96,1,16,16]{0,3,2,1:T(8,128)(2,1)S(1)}, u32[]{:S(2)}, u32[]{:S(2)}) collective-permute-start(bf16[96,1,16,16]{0,3,2,1:T(8,128)(2,1)S(1)} %get-tuple-element.59), channel_id=1, source_target_pairs={{32,0},{64,32},{96,64},{128,96},{160,128},{192,160},{224,192},{256... | collective-permute-start | bytes 147464 | tf_op jit(solution)/shard_map/ppermute | solution.py:217
  85.3 14.3 %collective-permute-start.12 = (bf16[96,1,16,16]{0,3,2,1:T(8,128)(2,1)S(1)}, bf16[96,1,16,16]{0,3,2,1:T(8,128)(2,1)S(1)}, u32[]{:S(2)}, u32[]{:S(2)}) collective-permute-start(bf16[96,1,16,16]{0,3,2,1:T(8,128)(2,1)S(1)} %get-tuple-element.56), channel_id=1, source_target_pairs={{0,32},{32,64},{64,96},{96,128},{128,160},{160,192},{192,224},{224... | collective-permute-start | bytes 147464 | tf_op jit(solution)/shard_map/ppermute | solution.py:214
  90.7 8.9 %collective-permute-start.13 = (bf16[96,1,16,16]{0,3,2,1:T(8,128)(2,1)S(1)}, bf16[96,1,16,16]{0,3,2,1:T(8,128)(2,1)S(1)}, u32[]{:S(2)}, u32[]{:S(2)}) collective-permute-start(bf16[96,1,16,16]{0,3,2,1:T(8,128)(2,1)S(1)} %get-tuple-element.57), channel_id=1, source_target_pairs={{32,0},{64,32},{96,64},{128,96},{160,128},{192,160},{224,192},{256... | collective-permute-start | bytes 147464 | tf_op jit(solution)/shard_map/ppermute | solution.py:217
  92.1 13.7 %collective-permute-start.8 = (bf16[96,18,1,16]{0,3,2,1:T(8,128)(2,1)S(1)}, bf16[96,18,1,16]{0,3,2,1:T(8,128)(2,1)S(1)}, u32[]{:S(2)}, u32[]{:S(2)}) collective-permute-start(bf16[96,18,1,16]{0,3,2,1:T(8,128)(2,1)S(1)} %get-tuple-element.54), channel_id=1, source_target_pairs={{0,2},{2,4},{4,6},{6,8},{8,10},{10,12},{12,14},{14,16},{16,18},{18... | collective-permute-start | bytes 165896 | tf_op jit(solution)/shard_map/ppermute | solution.py:214
  97.7 8.1 %collective-permute-start.9 = (bf16[96,18,1,16]{0,3,2,1:T(8,128)(2,1)S(1)}, bf16[96,18,1,16]{0,3,2,1:T(8,128)(2,1)S(1)}, u32[]{:S(2)}, u32[]{:S(2)}) collective-permute-start(bf16[96,18,1,16]{0,3,2,1:T(8,128)(2,1)S(1)} %get-tuple-element.55), channel_id=1, source_target_pairs={{2,0},{4,2},{6,4},{8,6},{10,8},{12,10},{14,12},{16,14},{18,16},{20... | collective-permute-start | bytes 165896 | tf_op jit(solution)/shard_map/ppermute | solution.py:217
  99.7 12.4 %copy-start.16 = (bf16[96,1,16,16]{0,3,2,1:T(8,128)(2,1)}, bf16[96,1,16,16]{0,3,2,1:T(8,128)(2,1)S(1)}, u32[]{:S(2)}) copy-start(bf16[96,1,16,16]{0,3,2,1:T(8,128)(2,1)S(1)} %collective-permute-done.12) | copy-start | bytes 147460
  99.7 12.4 %copy-start.17 = (bf16[96,1,16,16]{0,3,2,1:T(8,128)(2,1)}, bf16[96,1,16,16]{0,3,2,1:T(8,128)(2,1)S(1)}, u32[]{:S(2)}) copy-start(bf16[96,1,16,16]{0,3,2,1:T(8,128)(2,1)S(1)} %collective-permute-done.13) | copy-start | bytes 147460
  99.7 20.4 %copy-start.6 = (f32[9,96,96]{2,1,0:T(8,128)S(1)}, f32[9,96,96]{2,1,0:T(8,128)}, u32[]{:S(2)}) copy-start(f32[9,96,96]{2,1,0:T(8,128)} %fusion.52) | copy-start | bytes 995332
  99.7 20.4 %copy-start.7 = (f32[9,96,96]{2,1,0:T(8,128)S(1)}, f32[9,96,96]{2,1,0:T(8,128)}, u32[]{:S(2)}) copy-start(f32[9,96,96]{2,1,0:T(8,128)} %fusion.54) | copy-start | bytes 995332
  99.8 20.4 %copy-start.8 = (f32[9,96,96]{2,1,0:T(8,128)S(1)}, f32[9,96,96]{2,1,0:T(8,128)}, u32[]{:S(2)}) copy-start(f32[9,96,96]{2,1,0:T(8,128)} %fusion.56) | copy-start | bytes 995332
  99.8 11.2 %collective-permute-start.14 = (bf16[96,18,1,16]{0,3,2,1:T(8,128)(2,1)S(1)}, bf16[96,18,1,16]{0,3,2,1:T(8,128)(2,1)S(1)}, u32[]{:S(2)}, u32[]{:S(2)}) collective-permute-start(bf16[96,18,1,16]{0,3,2,1:T(8,128)(2,1)S(1)} %get-tuple-element.52), channel_id=1, source_target_pairs={{0,2},{2,4},{4,6},{6,8},{8,10},{10,12},{12,14},{14,16},{16,18},{18... | collective-permute-start | bytes 165896 | tf_op jit(solution)/shard_map/ppermute | solution.py:214
  103.7 7.3 %collective-permute-start.15 = (bf16[96,18,1,16]{0,3,2,1:T(8,128)(2,1)S(1)}, bf16[96,18,1,16]{0,3,2,1:T(8,128)(2,1)S(1)}, u32[]{:S(2)}, u32[]{:S(2)}) collective-permute-start(bf16[96,18,1,16]{0,3,2,1:T(8,128)(2,1)S(1)} %get-tuple-element.53), channel_id=1, source_target_pairs={{2,0},{4,2},{6,4},{8,6},{10,8},{12,10},{14,12},{16,14},{18,16},{20... | collective-permute-start | bytes 165896 | tf_op jit(solution)/shard_map/ppermute | solution.py:217
  105.8 13.1 %copy-start.57 = (bf16[96,18,1,16]{0,3,2,1:T(8,128)(2,1)}, bf16[96,18,1,16]{0,3,2,1:T(8,128)(2,1)S(1)}, u32[]{:S(2)}) copy-start(bf16[96,18,1,16]{0,3,2,1:T(8,128)(2,1)S(1)} %collective-permute-done.8) | copy-start | bytes 165892
  105.8 13.1 %copy-start.58 = (bf16[96,18,1,16]{0,3,2,1:T(8,128)(2,1)}, bf16[96,18,1,16]{0,3,2,1:T(8,128)(2,1)S(1)}, u32[]{:S(2)}) copy-start(bf16[96,18,1,16]{0,3,2,1:T(8,128)(2,1)S(1)} %collective-permute-done.9) | copy-start | bytes 165892
  106.9 15.2 %collective-permute-start.10 = (bf16[96,18,18,1]{0,3,2,1:T(2,128)(2,1)}, bf16[96,18,18,1]{0,3,2,1:T(2,128)(2,1)}, u32[]{:S(2)}, u32[]{:S(2)}) collective-permute-start(bf16[96,18,18,1]{0,3,2,1:T(2,128)(2,1)} %get-tuple-element.51), channel_id=1, source_target_pairs={{0,1},{2,3},{4,5},{6,7},{8,9},{10,11},{12,13},{14,15},{16,17},{18,... | collective-permute-start | bytes 186632 | tf_op jit(solution)/shard_map/ppermute | solution.py:214
  109.6 12.4 %collective-permute-start.11 = (bf16[96,18,18,1]{0,3,2,1:T(2,128)(2,1)}, bf16[96,18,18,1]{0,3,2,1:T(2,128)(2,1)}, u32[]{:S(2)}, u32[]{:S(2)}) collective-permute-start(bf16[96,18,18,1]{0,3,2,1:T(2,128)(2,1)} %get-tuple-element.50), channel_id=1, source_target_pairs={{1,0},{3,2},{5,4},{7,6},{9,8},{11,10},{13,12},{15,14},{17,16},{19,... | collective-permute-start | bytes 186632 | tf_op jit(solution)/shard_map/ppermute | solution.py:217
  110.9 7.9 %copy-start.59 = (bf16[96,18,1,16]{0,3,2,1:T(8,128)(2,1)}, bf16[96,18,1,16]{0,3,2,1:T(8,128)(2,1)S(1)}, u32[]{:S(2)}) copy-start(bf16[96,18,1,16]{0,3,2,1:T(8,128)(2,1)S(1)} %collective-permute-done.14) | copy-start | bytes 165892
  111.0 7.9 %copy-start.60 = (bf16[96,18,1,16]{0,3,2,1:T(8,128)(2,1)}, bf16[96,18,1,16]{0,3,2,1:T(8,128)(2,1)S(1)}, u32[]{:S(2)}) copy-start(bf16[96,18,1,16]{0,3,2,1:T(8,128)(2,1)S(1)} %collective-permute-done.15) | copy-start | bytes 165892
  112.1 10.0 %collective-permute-start.16 = (bf16[96,18,18,1]{0,3,2,1:T(2,128)(2,1)}, bf16[96,18,18,1]{0,3,2,1:T(2,128)(2,1)}, u32[]{:S(2)}, u32[]{:S(2)}) collective-permute-start(bf16[96,18,18,1]{0,3,2,1:T(2,128)(2,1)} %get-tuple-element.49), channel_id=1, source_target_pairs={{0,1},{2,3},{4,5},{6,7},{8,9},{10,11},{12,13},{14,15},{16,17},{18,... | collective-permute-start | bytes 186632 | tf_op jit(solution)/shard_map/ppermute | solution.py:214
  118.9 8.4 %collective-permute-start.17 = (bf16[96,18,18,1]{0,3,2,1:T(2,128)(2,1)}, bf16[96,18,18,1]{0,3,2,1:T(2,128)(2,1)}, u32[]{:S(2)}, u32[]{:S(2)}) collective-permute-start(bf16[96,18,18,1]{0,3,2,1:T(2,128)(2,1)} %get-tuple-element.48), channel_id=1, source_target_pairs={{1,0},{3,2},{5,4},{7,6},{9,8},{11,10},{13,12},{15,14},{17,16},{19,... | collective-permute-start | bytes 186632 | tf_op jit(solution)/shard_map/ppermute | solution.py:217
  201.9 2.9 %copy-start.41 = (bf16[1,96,8,8,8]{1,4,3,2,0:T(8,128)(2,1)S(1)}, bf16[1,96,8,8,8]{1,4,3,2,0:T(8,128)(2,1)}, u32[]{:S(2)}) copy-start(bf16[1,96,8,8,8]{1,4,3,2,0:T(8,128)(2,1)} %get-tuple-element.158) | copy-start | bytes 294916
  201.9 2.9 %copy-start.42 = (bf16[1,96,8,8,8]{1,4,3,2,0:T(8,128)(2,1)S(1)}, bf16[1,96,8,8,8]{1,4,3,2,0:T(8,128)(2,1)}, u32[]{:S(2)}) copy-start(bf16[1,96,8,8,8]{1,4,3,2,0:T(8,128)(2,1)} %get-tuple-element.159) | copy-start | bytes 294916
  202.0 2.9 %copy-start.43 = (bf16[1,96,8,8,8]{1,4,3,2,0:T(8,128)(2,1)S(1)}, bf16[1,96,8,8,8]{1,4,3,2,0:T(8,128)(2,1)}, u32[]{:S(2)}) copy-start(bf16[1,96,8,8,8]{1,4,3,2,0:T(8,128)(2,1)} %get-tuple-element.160) | copy-start | bytes 294916
  202.0 2.9 %copy-start.44 = (bf16[1,96,8,8,8]{1,4,3,2,0:T(8,128)(2,1)S(1)}, bf16[1,96,8,8,8]{1,4,3,2,0:T(8,128)(2,1)}, u32[]{:S(2)}) copy-start(bf16[1,96,8,8,8]{1,4,3,2,0:T(8,128)(2,1)} %get-tuple-element.161) | copy-start | bytes 294916
  202.0 2.9 %copy-start.45 = (bf16[1,96,8,8,8]{1,4,3,2,0:T(8,128)(2,1)S(1)}, bf16[1,96,8,8,8]{1,4,3,2,0:T(8,128)(2,1)}, u32[]{:S(2)}) copy-start(bf16[1,96,8,8,8]{1,4,3,2,0:T(8,128)(2,1)} %get-tuple-element.162) | copy-start | bytes 294916
  202.0 2.9 %copy-start.46 = (bf16[1,96,8,8,8]{1,4,3,2,0:T(8,128)(2,1)S(1)}, bf16[1,96,8,8,8]{1,4,3,2,0:T(8,128)(2,1)}, u32[]{:S(2)}) copy-start(bf16[1,96,8,8,8]{1,4,3,2,0:T(8,128)(2,1)} %get-tuple-element.163) | copy-start | bytes 294916
  205.7 2.3 %copy-start.10 = (bf16[9,96,96]{2,1,0:T(8,128)(2,1)S(1)}, bf16[9,96,96]{2,1,0:T(8,128)(2,1)}, u32[]{:S(2)}) copy-start(bf16[9,96,96]{2,1,0:T(8,128)(2,1)} %copy.19) | copy-start | bytes 497668
  206.1 2.3 %copy-start.29 = (bf16[1,96,8,8,8]{1,4,3,2,0:T(8,128)(2,1)S(1)}, bf16[1,96,8,8,8]{1,4,3,2,0:T(8,128)(2,1)}, u32[]{:S(2)}) copy-start(bf16[1,96,8,8,8]{1,4,3,2,0:T(8,128)(2,1)} %get-tuple-element.167) | copy-start | bytes 294916
  (22 other events, 37.6 us)

commit v2 on v1

--- a/solution.py
+++ b/solution.py
@@ -1,3 +1,5 @@
+import functools
+
 import jax
 import jax.numpy as jnp
 from jax import lax
@@ -5,12 +7,359 @@
 from jax.experimental.pallas import tpu as pltpu
 from jax.sharding import PartitionSpec as P
 
-RX = 2
-RY = 2
-RZ = 2
-
-
 MESH = pl.DeviceIdType.MESH
+VMEM = pl.BlockSpec(memory_space=pltpu.VMEM)
+SMEM = pl.BlockSpec(memory_space=pltpu.SMEM)
+C = 96
+WIDE = 128
+MSG = 512
+BF = jnp.bfloat16
+F32 = jnp.float32
+
+
+def message_plan():
+    plan = []
+    for ix in (0, 1):
+        plan.append((ix, 64, (1 - 2 * ix, 0, 0)))
+    for iy in (0, 1):
+        plan.append((2 + iy, 64, (0, 1 - 2 * iy, 0)))
+    plan.append((4, 64, (0, 0, 1)))
+    for ix in (0, 1):
+        for iy in (0, 1):
+            plan.append((5 + 2 * ix + iy, 16, (1 - 2 * ix, 1 - 2 * iy, 0)))
+    for ix in (0, 1):
+        plan.append((9 + ix, 16, (1 - 2 * ix, 0, 1)))
+    for iy in (0, 1):
+        plan.append((11 + iy, 16, (0, 1 - 2 * iy, 1)))
+    for ix in (0, 1):
+        for iy in (0, 1):
+            plan.append((13 + 2 * ix + iy, 16, (1 - 2 * ix, 1 - 2 * iy, 1)))
+    return plan
+
+
+def slot_row(slot):
+    return slot * 64 if slot < 5 else 320 + (slot - 5) * 16
+
+
+def pack_messages(wide_ref, msg_ref, q):
+    blank = jnp.zeros((8, WIDE), F32)
+    only = lax.broadcasted_iota(jnp.int32, (8, WIDE), 0) == 0
+    for part in range(wide_ref.shape[0]):
+
+        def rows(*spot, **stride):
+            return wide_ref[part, pl.ds(*spot, **stride), :]
+
+        def put(slot, value):
+            start = slot_row(slot)
+            msg_ref[pl.ds(start, value.shape[0]), pl.ds(part * WIDE, WIDE)] = value.astype(BF)
+
+        def side(low, high):
+            return jnp.where(q == 0, high, low)
+
+        for ix in (0, 1):
+            put(ix, rows(448 * (1 - ix), 64))
+        for iy in (0, 1):
+            edge = [rows(64 * i + 56 * (1 - iy), 8) for i in range(8)]
+            put(2 + iy, jnp.concatenate(edge, axis=0))
+        put(4, side(rows(0, 64, stride=8), rows(7, 64, stride=8)))
+        for ix in (0, 1):
+            x0 = 448 * (1 - ix)
+            for iy in (0, 1):
+                column = rows(x0 + 56 * (1 - iy), 8)
+                put(5 + 2 * ix + iy, jnp.concatenate([column, blank], axis=0))
+                corner = side(column, pltpu.roll(column, 1, 0))
+                put(13 + 2 * ix + iy, jnp.concatenate([jnp.where(only, corner, 0.0), blank], axis=0))
+            line = side(rows(x0, 8, stride=8), rows(x0 + 7, 8, stride=8))
+            put(9 + ix, jnp.concatenate([line, blank], axis=0))
+        for iy in (0, 1):
+            y0 = 56 * (1 - iy)
+            line = side(rows(y0, 8, stride=64), rows(y0 + 7, 8, stride=64))
+            put(11 + iy, jnp.concatenate([line, blank], axis=0))
+
+
+def pack_kernel(place_ref, x_ref, g_ref, code_ref, rows_ref, msg_ref, wide_ref):
+    position, count, q = place_ref[0], place_ref[1], place_ref[4]
+    column = lax.broadcasted_iota(jnp.int32, (64, 512), 0)
+    voxel = lax.broadcasted_iota(jnp.int32, (64, 512), 1)
+    spread = jnp.where(column == voxel // 8, 1.0, 0.0).astype(BF)
+    codes = jnp.broadcast_to(code_ref[...].astype(F32), (16, 64)).astype(BF)
+    code = jnp.dot(codes, spread, preferred_element_type=F32).astype(jnp.int32)[:8]
+    low = code // 8
+    level = lax.broadcasted_iota(jnp.int32, (8, 512), 1) % 8
+    live = (level >= low) & (level <= low + code % 8) & (count > 0)
+    mask = jnp.where(live, 1.0, 0.0)
+    first = lax.broadcasted_iota(jnp.int32, (8, 512), 0)
+    place = jnp.where(first == 0, position.astype(F32), jnp.where(first == 1, mask, 0.0))
+    blank = jnp.zeros((24, 512), F32)
+    inside = jnp.broadcast_to(mask[:1], (C, 512)) > 0.0
+    x = jnp.where(inside, x_ref[...].astype(F32), 0.0)
+    g = jnp.where(inside, g_ref[...].astype(F32), 0.0)
+    wide_ref[0] = jnp.concatenate([x, place, blank], axis=0).T
+    wide_ref[1] = jnp.concatenate([g, jnp.zeros((32, 512), F32)], axis=0).T
+    rows_ref[:, :WIDE] = wide_ref[0].astype(BF)
+    rows_ref[:, WIDE:] = wide_ref[1].astype(BF)
+    pack_messages(wide_ref, msg_ref, q)
+
+
+def pack(place, x, g, codes):
+    return pl.pallas_call(
+        pack_kernel,
+        out_shape=(jax.ShapeDtypeStruct((512, 2 * WIDE), BF), jax.ShapeDtypeStruct((MSG, 2 * WIDE), BF)),
+        in_specs=[SMEM, VMEM, VMEM, VMEM],
+        out_specs=(VMEM, VMEM),
+        scratch_shapes=[pltpu.VMEM((2, 512, WIDE), F32)],
+        name="pack",
+    )(place, x, g, codes)
+
+
+def neighbour(offset):
+    u, w, q = lax.axis_index("gx"), lax.axis_index("gy"), lax.axis_index("gz")
+    nx, ny = lax.axis_size("gx"), lax.axis_size("gy")
+    du, dv, dw = offset
+    return ((u + du + nx) % nx, (w + dv + ny) % ny, 1 - q if dw else q)
+
+
+def halo_copies(msg_ref, into_ref, send_sem, recv_sem):
+    copies = []
+    for slot, size, offset in message_plan():
+        rows = pl.ds(slot_row(slot), size)
+        copies.append(pltpu.make_async_remote_copy(
+            src_ref=msg_ref.at[rows, :], dst_ref=into_ref.at[rows, :],
+            send_sem=send_sem.at[slot], recv_sem=recv_sem.at[slot],
+            device_id=neighbour(offset), device_id_type=MESH))
+    return copies
+
+
+def greet_neighbours(barrier):
+    for _, _, offset in message_plan():
+        pl.semaphore_signal(barrier, inc=1, device_id=neighbour(offset), device_id_type=MESH)
+
+
+def exchange_kernel(msg_ref, out_ref, into, send_sem, recv_sem):
+    barrier = pltpu.get_barrier_semaphore()
+    greet_neighbours(barrier)
+    pl.semaphore_wait(barrier, 17)
+    copies = halo_copies(msg_ref, into, send_sem, recv_sem)
+    for copy in copies:
+        copy.start()
+    for copy in copies:
+        copy.wait()
+    out_ref[...] = into[...]
+
+
+def exchange(messages, number):
+    return pl.pallas_call(
+        exchange_kernel,
+        out_shape=jax.ShapeDtypeStruct(messages.shape, messages.dtype),
+        in_specs=[VMEM],
+        out_specs=VMEM,
+        scratch_shapes=[
+            pltpu.VMEM(messages.shape, messages.dtype),
+            pltpu.SemaphoreType.DMA((17,)), pltpu.SemaphoreType.DMA((17,))],
+        compiler_params=pltpu.CompilerParams(collective_id=number, has_side_effects=True),
+        name="exchange",
+    )(messages)
+
+
+def pick_messages(place_ref, into_ref):
+    position = place_ref[0]
+    a, b = position // 4, position // 2 % 2
+
+    def take(start, size):
+        return into_ref[pl.ds(pl.multiple_of(start, 16), size), :]
+
+    return jnp.concatenate([
+        take(a * 64, 64), take(128 + b * 64, 64), take(256, 64),
+        take(320 + (2 * a + b) * 16, 16), take(384 + a * 16, 16), take(416 + b * 16, 16),
+        take(448 + (2 * a + b) * 16, 16)], axis=0)
+
+
+def halo_codes(place_ref, sender):
+    position, u, w, q = place_ref[0], place_ref[2], place_ref[3], place_ref[4]
+    nx, ny = place_ref[5], place_ref[6]
+    own = (position // 4, position // 2 % 2, position % 2)
+    theirs = (sender // 4, sender // 2 % 2, sender % 2)
+    beyond = (u + 2 * own[0] - 1, w + 2 * own[1] - 1, q + 2 * own[2] - 1)
+    sizes = (nx, ny, 2)
+    r = lax.broadcasted_iota(jnp.int32, sender.shape, 1)
+    face = r < 192
+    t = jnp.where(face, r % 64, r % 16)
+    high, low = t // 8, t % 8
+    past = (
+        (r < 64) | ((r >= 192) & (r < 224)) | (r >= 240),
+        ((r >= 64) & (r < 128)) | ((r >= 192) & (r < 208)) | (r >= 224),
+        ((r >= 128) & (r < 192)) | (r >= 208))
+    index = (
+        jnp.where(face, high, t),
+        jnp.where(r < 64, high, jnp.where(face, low, t)),
+        jnp.where(face, low, t))
+    valid = face | (t < jnp.where(r < 240, 8, 1))
+    spot = []
+    for axis in range(3):
+        far = 9 * own[axis]
+        near = 9 - far
+        same = theirs[axis] == own[axis]
+        inner = jnp.where(same, 1 + index[axis], near)
+        inner_ok = same | (index[axis] == 7 * own[axis])
+        there = jnp.zeros_like(r) + beyond[axis]
+        outer_ok = (theirs[axis] != own[axis]) & (there >= 0) & (there < sizes[axis])
+        spot.append(jnp.where(past[axis], far, inner))
+        valid = valid & ((past[axis] & outer_ok) | (jnp.logical_not(past[axis]) & inner_ok))
+    return jnp.where(valid, (spot[0] * 10 + spot[1]) * 16 + spot[2], -1)
+
+
+def build_patch(place_ref, rows, picked, code, level_ref, all_ref, width):
+    n = lax.broadcasted_iota(jnp.int32, (800, 256), 0)
+    target = n // 8 * 16 + n % 8
+    level = lax.broadcasted_iota(jnp.int32, rows.shape, 0) % 8
+    for dz in (0, 1, 2):
+        pick = jnp.where(target + dz == code, 1.0, 0.0).astype(BF)
+        halo = jnp.dot(pick, picked, preferred_element_type=F32)
+        if dz == 0:
+            mine = jnp.where(level == 0, 0.0, pltpu.roll(rows, 1, 0))
+        elif dz == 1:
+            mine = rows
+        else:
+            mine = jnp.where(level == 7, 0.0, pltpu.roll(rows, 511, 0))
+        level_ref[...] = halo
+        for i in range(8):
+            spot = pl.ds(((i + 1) * 10 + 1) * 8, 64)
+            level_ref[spot, :] = level_ref[spot, :] + mine[64 * i : 64 * i + 64]
+        for dy in (0, 1, 2):
+            tap = dy * 3 + dz
+            for x in range(10):
+                all_ref[pl.ds(64 * x, 64), pl.ds(tap * width, width)] = (
+                    level_ref[pl.ds((x * 10 + dy) * 8, 64), :].astype(BF))
+
+
+def pack_grads(blocks, store):
+    lane = lax.broadcasted_iota(jnp.int32, (C, WIDE), 1)
+    for group in range(13):
+        last = blocks(4 * group + 3)
+        for t in range(3):
+            shifted = pltpu.roll(last, C - 32 * t, 1)
+            store(3 * group + t, jnp.where(lane < C, blocks(4 * group + t), shifted))
+    store(39, blocks(52))
+    store(40, blocks(53))
+
+
+def unpack_grads(load, store):
+    lane = lax.broadcasted_iota(jnp.int32, (C, WIDE), 1)
+    for group in range(13):
+        last = jnp.zeros((C, WIDE), F32)
+        for t in range(3):
+            tile = load(3 * group + t)
+            store(4 * group + t, tile)
+            moved = pltpu.roll(tile, 32 + 32 * t, 1)
+            last = jnp.where((lane >= 32 * t) & (lane < 32 * t + 32), moved, last)
+        store(4 * group + 3, last)
+    store(52, load(39))
+    store(53, load(40))
+
+
+def forward_kernel(scale, place_ref, rows_ref, into_ref, weight_ref, data_ref, delta_ref, msg_ref, code_out,
+                   level_ref, all_ref, grads_ref, wide_ref):
+    q = place_ref[4]
+    rows = rows_ref[...].astype(F32)
+    picked = pick_messages(place_ref, into_ref)
+    sender = picked[:, :WIDE].astype(F32).T[C : C + 8].astype(jnp.int32)
+    code = halo_codes(place_ref, sender)[:1]
+    code_out[...] = jnp.broadcast_to(code, (8, 256))
+    build_patch(place_ref, rows, picked, code, level_ref, all_ref, 2 * WIDE)
+    acc = jnp.zeros((512, 2 * WIDE), F32)
+    for dx in (0, 1, 2):
+        acc = acc + jnp.dot(all_ref[pl.ds(64 * dx, 512), :], weight_ref[dx], preferred_element_type=F32)
+    pre, back = acc[:, :WIDE], acc[:, WIDE:]
+    mask = jnp.broadcast_to(rows[:, C + 1 : C + 2], (512, WIDE))
+    sigma = jax.nn.sigmoid(pre)
+    hidden = pre * sigma * mask
+    delta = (back * sigma * (1.0 + pre * (1.0 - sigma)) * mask).astype(BF)
+    delta_ref[...] = delta
+    wide_ref[0] = delta.astype(F32)
+    pack_messages(wide_ref, msg_ref, q)
+    both = jnp.concatenate([hidden.T, delta.astype(F32).T], axis=0).astype(BF)
+    for dx in (0, 1, 2):
+        grads_ref[dx] = jnp.dot(both, all_ref[pl.ds(64 * dx, 512), :], preferred_element_type=F32)
+
+    def blocks(number):
+        if number < 27:
+            return grads_ref[number // 9, WIDE : WIDE + C, pl.ds(number % 9 * 2 * WIDE, WIDE)] * scale
+        turned = 53 - number
+        return grads_ref[turned // 9, 0:C, pl.ds(turned % 9 * 2 * WIDE + WIDE, WIDE)] * scale
+
+    def store(tile, value):
+        data_ref[pl.ds(tile * C, C), :] = value
+
+    pack_grads(blocks, store)
+    data_ref[pl.ds(41 * C, 4096 - 41 * C), :] = jnp.zeros((4096 - 41 * C, WIDE), F32)
+
+
+def forward(scale, place, rows, into, weights):
+    return pl.pallas_call(
+        functools.partial(forward_kernel, scale),
+        out_shape=(
+            jax.ShapeDtypeStruct((4096, WIDE), F32), jax.ShapeDtypeStruct((512, WIDE), BF),
+            jax.ShapeDtypeStruct((MSG, WIDE), BF), jax.ShapeDtypeStruct((8, 256), jnp.int32)),
+        in_specs=[SMEM, VMEM, VMEM, VMEM],
+        out_specs=(VMEM,) * 4,
+        scratch_shapes=[
+            pltpu.VMEM((800, 2 * WIDE), F32), pltpu.VMEM((640, 9 * 2 * WIDE), BF),
+            pltpu.VMEM((3, 2 * WIDE, 9 * 2 * WIDE), F32), pltpu.VMEM((1, 512, WIDE), F32)],
+        compiler_params=pltpu.CompilerParams(vmem_limit_bytes=50 * 2 ** 20),
+        name="forward",
+    )(place, rows, into, weights)
+
+
+def backward_kernel(place_ref, rows_ref, code_ref, delta_ref, into_ref, weight_ref, sum_ref,
+                    out_ref, first_ref, second_ref, level_ref, all_ref):
+    picked = pick_messages(place_ref, into_ref)
+    build_patch(place_ref, delta_ref[...].astype(F32), picked, code_ref[0:1, :], level_ref, all_ref, WIDE)
+    acc = rows_ref[:, WIDE:].astype(F32)
+    for dx in (0, 1, 2):
+        acc = acc + jnp.dot(all_ref[pl.ds(64 * dx, 512), :], weight_ref[dx], preferred_element_type=F32)
+    mask = jnp.broadcast_to(rows_ref[:, :WIDE].astype(F32)[:, C + 1 : C + 2], (512, WIDE))
+    out_ref[...] = (acc * mask).T[:C].astype(BF)
+
+    def load(tile):
+        return sum_ref[pl.ds(tile * C, C), :].astype(F32)
+
+    def store(number, value):
+        if number < 27:
+            first_ref[number] = value.T[:C]
+        else:
+            second_ref[number - 27] = value[:, :C]
+
+    unpack_grads(load, store)
+
+
+def backward(place, rows, code, delta, into, weights, summed):
+    return pl.pallas_call(
+        backward_kernel,
+        out_shape=(
+            jax.ShapeDtypeStruct((C, 512), BF),
+            jax.ShapeDtypeStruct((27, C, C), F32), jax.ShapeDtypeStruct((27, C, C), F32)),
+        in_specs=[SMEM] + [VMEM] * 6,
+        out_specs=(VMEM,) * 3,
+        scratch_shapes=[pltpu.VMEM((800, WIDE), F32), pltpu.VMEM((640, 9 * WIDE), BF)],
+        compiler_params=pltpu.CompilerParams(vmem_limit_bytes=50 * 2 ** 20),
+        name="backward",
+    )(place, rows, code, delta, into, weights, summed)
+
+
+def both_weights(first, second):
+    gap = WIDE - C
+    turned = second[::-1].transpose(0, 2, 1)
+    top = jnp.pad(first, ((0, 0), (0, gap), (0, WIDE + gap)))
+    bottom = jnp.pad(turned, ((0, 0), (0, gap), (WIDE, gap)))
+    return jnp.concatenate([top, bottom], axis=1).reshape(3, 9 * 2 * WIDE, 2 * WIDE)
+
+
+def back_weights(first):
+    gap = WIDE - C
+    turned = first[::-1].transpose(0, 2, 1)
+    return jnp.pad(turned, ((0, 0), (0, gap), (0, gap))).reshape(3, 9 * WIDE, WIDE)
+
+
 ROWS = 4096
 HALF = ROWS // 2
 PART = HALF // 16
@@ -206,152 +555,19 @@
     )(data)
 
 
-def padded_2(block, sides, width):
-    for axis, dim in sides:
-        count = lax.axis_size(axis)
-        forward = [(i, i + 1) for i in range(count - 1)]
-        backward = [(target, source) for source, target in forward]
-        low = lax.ppermute(
-            lax.slice_in_dim(block, block.shape[dim] - width, None, axis=dim), axis, forward
-        )
-        high = lax.ppermute(lax.slice_in_dim(block, 0, width, axis=dim), axis, backward)
-        block = jnp.concatenate([low, block, high], axis=dim)
-    return block
-
-
-def voxel_mask(column_codes, live_count, slots):
-    levels = jnp.arange(8, dtype=jnp.int32)
-    lowest = column_codes // 8
-    beyond = lowest + column_codes % 8 + 1
-    inside = (levels[None, None, :] >= lowest[:, :, None]) & (
-        levels[None, None, :] < beyond[:, :, None]
-    )
-    living = jnp.arange(slots, dtype=jnp.int32) < live_count
-    return (inside & living[:, None, None]).reshape(slots, 512).astype(jnp.float32)
-
-
-def to_region(bricks):
-    channels = bricks.shape[1]
-    blocks = bricks.reshape(RX, RY, RZ, channels, 8, 8, 8)
-    blocks = blocks.transpose(3, 0, 4, 1, 5, 2, 6)
-    return blocks.reshape(channels, RX * 8, RY * 8, RZ * 8)
-
-
-def cut_patches(padded, positions):
-
-    def single(position):
-        corner_x = position // (RY * RZ) * 8
-        corner_y = position // RZ % RY * 8
-        corner_z = position % RZ * 8
-        anchor = jnp.zeros((), jnp.int32)
-        return lax.dynamic_slice(
-            padded, (anchor, corner_x, corner_y, corner_z), (padded.shape[0], 10, 10, 10)
-        )
-
-    return jax.vmap(single)(positions)
-
-
-def block_cols(patches, step_x, facing):
-    gathered = []
-    for step_y in (-1, 0, 1):
-        for step_z in (-1, 0, 1):
-            start_x = 1 + facing * step_x
-            start_y = 1 + facing * step_y
-            start_z = 1 + facing * step_z
-            sliced = patches[
-                :, :, start_x : start_x + 8, start_y : start_y + 8, start_z : start_z + 8
-            ]
-            gathered.append(sliced.reshape(patches.shape[0], patches.shape[1], 512))
-    return jnp.concatenate(gathered, axis=1)
-
-
-def shards(
-    features, cotangent, first_weight, second_weight, slot_position, brick_count, column_code
-):
-    slots = features.shape[3]
-    channels = features.shape[4]
-    positions = slot_position.reshape(slots)
-    occupied = voxel_mask(column_code.reshape(slots, 64), brick_count.reshape(()), slots)
-    cut_mask = occupied[:, None, :].astype(jnp.bfloat16)
-    inputs = features.reshape(slots, channels, 512) * cut_mask
-    upstream = cotangent.reshape(slots, channels, 512) * cut_mask
-    placing = (positions[:, None] == jnp.arange(RX * RY * RZ, dtype=jnp.int32)[None, :]).astype(
-        jnp.bfloat16
-    )
-    total = slots * lax.axis_size("gx") * lax.axis_size("gy") * lax.axis_size("gz")
-    scale = total ** (-0.5) / 8.0
-
-    def regional(bricks):
-        spread = jnp.einsum("sr,scv->rcv", placing, bricks, preferred_element_type=jnp.float32)
-        return to_region(spread.astype(jnp.bfloat16))
-
-    joined = regional(jnp.concatenate([inputs, upstream], axis=1))
-    padded = padded_2(joined, (("gx", 1), ("gy", 2), ("gz", 3)), 1)
-    patches = cut_patches(padded, positions)
-    input_patch = patches[:, :channels]
-    upstream_patch = patches[:, channels:]
-    first_blocks = first_weight.reshape(3, 9 * channels, channels)
-    second_back = second_weight.transpose(0, 2, 1).reshape(3, 9 * channels, channels)
-    first_back = first_weight.transpose(0, 2, 1).reshape(3, 9 * channels, channels)
-    pre_act = jnp.zeros((slots, channels, 512), jnp.float32)
-    back_act = jnp.zeros((slots, channels, 512), jnp.float32)
-    for step_x in (-1, 0, 1):
-        pre_act = pre_act + jnp.einsum(
-            "sjv,jo->sov",
-            block_cols(input_patch, step_x, 1),
-            first_blocks[step_x + 1],
-            preferred_element_type=jnp.float32,
-        )
-        back_act = back_act + jnp.einsum(
-            "sjv,jc->scv",
-            block_cols(upstream_patch, step_x, -1),
-            second_back[step_x + 1],
-            preferred_element_type=jnp.float32,
-        )
-    sigma = jax.nn.sigmoid(pre_act)
-    hidden = (pre_act * sigma * occupied[:, None, :]).astype(jnp.bfloat16)
-    delta = (back_act * sigma * (1.0 + pre_act * (1.0 - sigma)) * occupied[:, None, :]).astype(
-        jnp.bfloat16
-    )
-    second_parts = []
-    hidden_pad = padded_2(regional(hidden), (("gx", 1), ("gy", 2), ("gz", 3)), 1)
-    hidden_patch = cut_patches(hidden_pad, positions)
-    for step_x in (-1, 0, 1):
-        second_term = jnp.einsum(
-            "sjv,sov->jo",
-            block_cols(hidden_patch, step_x, 1),
-            upstream,
-            preferred_element_type=jnp.float32,
-        )
-        second_parts.append(second_term.reshape(9, channels, channels))
-    second_local = jnp.concatenate(second_parts, axis=0)
-    delta_pad = padded_2(regional(delta), (("gx", 1), ("gy", 2), ("gz", 3)), 1)
-    delta_patch = cut_patches(delta_pad, positions)
-    back_input = upstream.astype(jnp.float32)
-    first_parts = []
-    for step_x in (-1, 0, 1):
-        back_input = back_input + jnp.einsum(
-            "sjv,jc->scv",
-            block_cols(delta_patch, step_x, -1),
-            first_back[step_x + 1],
-            preferred_element_type=jnp.float32,
-        )
-        first_term = jnp.einsum(
-            "sjv,sov->jo",
-            block_cols(input_patch, step_x, 1),
-            delta,
-            preferred_element_type=jnp.float32,
-        )
-        first_parts.append(first_term.reshape(9, channels, channels))
-    first_local = jnp.concatenate(first_parts, axis=0)
-    grad_input = (back_input * occupied[:, None, :]).astype(jnp.bfloat16)
-    count = 27 * channels * channels
-    joined_grads = jnp.concatenate([first_local.reshape(-1), second_local.reshape(-1)]) * scale
-    padded_grads = jnp.pad(joined_grads, (0, ROWS * 128 - 2 * count)).reshape(ROWS, 128)
-    summed = all_sum(padded_grads).reshape(-1)
-    first_grad = summed[:count].reshape(27, channels, channels)
-    second_grad = summed[count : 2 * count].reshape(27, channels, channels)
-    return (grad_input.reshape(1, 1, 1, slots, channels, 512), first_grad, second_grad)
+def shards(features, cotangent, first_weight, second_weight, slot_position, brick_count, column_code):
+    nx, ny, nz = (lax.axis_size(axis) for axis in ("gx", "gy", "gz"))
+    scale = float((nx * ny * nz) ** -0.5 / 8.0)
+    axes = [lax.axis_index(axis) for axis in ("gx", "gy", "gz")]
+    place = jnp.stack([slot_position.reshape(()), brick_count.reshape(()), *axes, nx, ny]).astype(jnp.int32)
+    rows, messages = pack(place, features.reshape(C, 512), cotangent.reshape(C, 512), column_code.reshape(1, 64))
+    into = exchange(messages, 1)
+    data, delta, delta_messages, code = forward(scale, place, rows, into, both_weights(first_weight, second_weight))
+    delta_into = exchange(delta_messages, 2)
+    summed = all_sum(data)
+    grad_input, first_grad, second_grad = backward(
+        place, rows, code, delta, delta_into, back_weights(first_weight), summed)
+    return grad_input.reshape(1, 1, 1, 1, C, 512), first_grad, second_grad
 
 
 def solution(mesh):

time: 211 us -> 111 us (0.53)
  starting transfers between devices: 57.5 us -> 0 us
  local copies, waits for them, and re-layouts: 47.5 us -> 11.5 us
  Pallas kernels: 58.7 us -> 94.3 us
  matrix products: 15.8 us -> 0 us
  waiting for transfers between devices: 14.6 us -> 0 us
  other arithmetic: 13 us -> 2.3 us
    ppermute x18 -> x0, starting transfers between devices: 57.5 us -> none  [the longest x9 43 us: padded_2(): lax.ppermute(lax.slice_in_dim(block, block.shape[dim] - width, None, axis...]
    pallas_call x0 -> x5, Pallas kernels: none -> 48 us  [the longest x2 32 us: exchange(): pl.pallas_call(exchange_kernel, out_shape=jax.ShapeDtypeStruct(messages.s...]
    slice x20 -> x0, local copies, waits for them, and re-layouts: 18.6 us -> none  [the longest x7 10.1 us: block_cols(): patches[:, :, start_x:start_x + 8, start_y:start_y + 8, start_z:start_z + 8]]
    dot_general x15 -> x0, matrix products: 15.8 us -> none  [the longest x3 5.41 us: shards(): jnp.einsum('sjv,jo->sov', block_cols(input_patch, step_x, 1), first_block...]
    concatenate x18 -> x1, local copies, waits for them, and re-layouts: 21.4 us -> 5.78 us  [both_weights(): jnp.concatenate([top, bottom], axis=1).reshape(3, 9 * 2 * WIDE, 2 * WIDE)]
    ppermute x18 -> x0, waiting for transfers between devices: 14.6 us -> none  [the longest x9 14 us: padded_2(): lax.ppermute(lax.slice_in_dim(block, 0, width, axis=dim), axis, backward)]
    pallas_call x1, Pallas kernels: 58.7 us -> 46.3 us  [all_sum(): pl.pallas_call(reduce_kernel, out_shape=jax.ShapeDtypeStruct((ROWS, 128),...]
    gather x2 -> x0, other arithmetic: 5.92 us -> none  [single(): lax.dynamic_slice(padded, (anchor, corner_x, corner_y, corner_z), (padded...]
  transfers between devices with their start and end apart: 18 -> 0, of which waited for: 5 -> 0; matrix products, arithmetic and copies ran while one was open for 6% -> 0% of each run, Pallas kernels for 0% -> 0%
where the time goes in v2:
time: 111 us; the launch traced here: 110 us
  Pallas kernels  94.3 us (85%)
  local copies, waits for them, and re-layouts  11.5 us (10%)
  other arithmetic  2.3 us (2%)
  between operations  2.04 us (2%)
    pallas_call x1, Pallas kernels, all_sum(): pl.pallas_call(reduce_kernel, out_shape=jax.ShapeDtypeStruct((ROWS, 128),...  46.3 us
    pallas_call x2, Pallas kernels, exchange(): pl.pallas_call(exchange_kernel, out_shape=jax.ShapeDtypeStruct(messages.s...  32 us
    pallas_call x1, Pallas kernels, forward(): pl.pallas_call(functools.partial(forward_kernel, scale), out_shape=(jax.S...  10 us
    concatenate x1, local copies, waits for them, and re-layouts, both_weights(): jnp.concatenate([top, bottom], axis=1).reshape(3, 9 * 2 * WIDE, 2 * WIDE)  5.78 us
    pallas_call x1, Pallas kernels, backward(): pl.pallas_call(backward_kernel, out_shape=(jax.ShapeDtypeStruct((C, 512),...  3.85 us
    unnamed x14, local copies, waits for them, and re-layouts  2.83 us
    concatenate x1, other arithmetic, both_weights(): jnp.concatenate([top, bottom], axis=1).reshape(3, 9 * 2 * WIDE, 2 * WIDE)  2.3 us

profile of v2, /device:TPU:1, one launch (start us, length us, event | category | flops | bytes accessed | tf_op | source)
XLA Modules:
  0.0 110.1 jit_solution(240406847376835521)
XLA Ops:
  1.9 0.6 stack.15.place_ref
  2.5 2.1 %pack.1 = (bf16[512,256]{1,0:T(8,128)(2,1)}, bf16[512,256]{1,0:T(8,128)(2,1)}) custom-call(s32[7]{0:T(128)} %stack.15.place_ref, bf16[96,512]{1,0:T(8,128)(2,1)} %bitcast.19, bf16[96,512]{1,0:T(8,128)(2,1)} %bitcast.20, s32[1,64]{1,0:T(1,128)} %bitcast.21), custom_call_target="tpu_custom_call" | custom-call | tf_op jit(solution)/shard_map/pack/pallas_call | solution.py:105
  4.6 21.5 %exchange.2.into_ref = bf16[512,256]{1,0:T(8,128)(2,1)} custom-call(bf16[512,256]{1,0:T(8,128)(2,1)} %get-tuple-element.13.msg_ref), custom_call_target="tpu_custom_call" | custom-call | tf_op jit(solution)/shard_map/exchange/pallas_call | solution.py:151
  26.2 1.4 %copy.10 = bf16[27,96,96]{1,2,0:T(8,128)(2,1)S(1)} copy(bf16[27,96,96]{2,1,0:T(8,128)(2,1)} %param.9) | data formatting | bytes 995328 | tf_op args[2]
  27.6 1.1 %reverse_bitcast_fusion.1 = bf16[27,96,96]{1,2,0:T(8,128)(2,1)S(1)} fusion(bf16[27,96,96]{2,1,0:T(8,128)(2,1)} %param.10), kind=kLoop, calls=%fused_computation.6 | loop fusion | bytes 995328 | tf_op jit(solution)/shard_map/transpose | solution.py:351
  28.7 2.3 %fusion.2 = bf16[27,256,256]{1,2,0:T(8,128)(2,1)} fusion(bf16[27,96,96]{1,2,0:T(8,128)(2,1)S(1)} %reverse_bitcast_fusion.1, bf16[27,96,96]{1,2,0:T(8,128)(2,1)S(1)} %copy.10), kind=kLoop, calls=%fused_computation.4 | loop fusion | flops 14155776 | bytes 4534272 | tf_op jit(solution)/shard_map/concatenate | solution.py:354
  31.0 0.0 copy-start
  31.0 0.0 copy-start.1
  31.0 0.0 copy-start.4
  31.0 5.8 %copy.11 = bf16[27,256,256]{2,1,0:T(8,128)(2,1)} copy(bf16[27,256,256]{1,2,0:T(8,128)(2,1)} %fusion.2) | data formatting | bytes 7077888 | tf_op jit(solution)/shard_map/concatenate | solution.py:354
  36.8 0.0 copy-done
  36.8 0.0 copy-done.1
  36.8 0.0 copy-done.4
  36.8 0.0 copy-start.5
  36.8 10.0 %forward.1 = (f32[4096,128]{1,0:T(8,128)S(1)}, bf16[512,128]{1,0:T(8,128)(2,1)S(1)}, bf16[512,128]{1,0:T(8,128)(2,1)S(1)}, s32[8,256]{1,0:T(8,128)S(1)}) custom-call(s32[7]{0:T(128)S(1)} %copy-done.4, bf16[512,256]{1,0:T(8,128)(2,1)S(1)} %copy-done, bf16[512,256]{1,0:T(8,128)(2,1)S(1)} %copy-done.1, bf16[3,2304,256]{2,1,0:T(8,128)(2,1)} %bitcast.18), custom_call_target="tpu_custom_call" | custom-call | tf_op jit(solution)/shard_map/forward/pallas_call | solution.py:298
  46.9 0.0 copy-start.3
  46.9 46.3 %all_sum.1.sum_ref = f32[4096,128]{1,0:T(8,128)S(1)} custom-call(f32[4096,128]{1,0:T(8,128)S(1)} %get-tuple-element.17.d_ref), custom_call_target="tpu_custom_call" | custom-call | tf_op jit(solution)/shard_map/all_sum/pallas_call | solution.py:534
  93.2 0.0 copy-done.3
  93.2 10.5 %exchange.3.into_ref = bf16[512,128]{1,0:T(8,128)(2,1)} custom-call(bf16[512,128]{1,0:T(8,128)(2,1)} %copy-done.3), custom_call_target="tpu_custom_call" | custom-call | tf_op jit(solution)/shard_map/exchange/pallas_call | solution.py:151
  103.7 0.0 copy-start.2
  103.7 0.0 copy-done.5
  103.7 0.9 reverse_bitcast_fusion
  104.6 1.4 %copy.13 = bf16[27,96,96]{2,1,0:T(8,128)(2,1)S(1)} copy(bf16[27,96,96]{1,2,0:T(8,128)(2,1)} %reverse_bitcast_fusion) | data formatting | bytes 995328
  106.0 0.2 pad.14.clone
  106.2 0.0 copy-done.2
  106.3 3.9 %backward.1 = (bf16[96,512]{1,0:T(8,128)(2,1)}, f32[27,96,96]{2,1,0:T(8,128)}, f32[27,96,96]{2,1,0:T(8,128)}) custom-call(s32[7]{0:T(128)S(1)} %copy-done.4, bf16[512,256]{1,0:T(8,128)(2,1)S(1)} %copy-done, s32[8,256]{1,0:T(8,128)S(1)} %get-tuple-element.14.code_ref, bf16[512,128]{1,0:T(8,128)(2,1)S(1)} %get-tuple-element.15.delta_ref, ...), custom_call_target="tpu_custom_call" | custom-call | tf_op jit(solution)/shard_map/backward/pallas_call | solution.py:336
  (1 shorter events, 0.0 us)
Async XLA Ops:
  31.0 5.8 %copy-start = (bf16[512,256]{1,0:T(8,128)(2,1)S(1)}, bf16[512,256]{1,0:T(8,128)(2,1)}, u32[]{:S(2)}) copy-start(bf16[512,256]{1,0:T(8,128)(2,1)} %get-tuple-element.12.rows_ref) | copy-start | bytes 786436
  31.0 5.8 %copy-start.1 = (bf16[512,256]{1,0:T(8,128)(2,1)S(1)}, bf16[512,256]{1,0:T(8,128)(2,1)}, u32[]{:S(2)}) copy-start(bf16[512,256]{1,0:T(8,128)(2,1)} %exchange.2.into_ref) | copy-start | bytes 786436
  31.0 5.8 %copy-start.4 = (s32[7]{0:T(128)S(1)}, s32[7]{0:T(128)}, u32[]{:S(2)}) copy-start(s32[7]{0:T(128)} %stack.15.place_ref) | copy-start | bytes 88
  36.8 66.9 %copy-start.5 = (bf16[27,96,96]{2,1,0:T(8,128)(2,1)S(1)}, bf16[27,96,96]{2,1,0:T(8,128)(2,1)}, u32[]{:S(2)}) copy-start(bf16[27,96,96]{2,1,0:T(8,128)(2,1)} %param.9) | copy-start | bytes 1492996
  46.9 46.3 %copy-start.3 = (bf16[512,128]{1,0:T(8,128)(2,1)}, bf16[512,128]{1,0:T(8,128)(2,1)S(1)}, u32[]{:S(2)}) copy-start(bf16[512,128]{1,0:T(8,128)(2,1)S(1)} %get-tuple-element.16.msg_ref) | copy-start | bytes 393220
  103.7 2.6 %copy-start.2 = (bf16[512,128]{1,0:T(8,128)(2,1)S(1)}, bf16[512,128]{1,0:T(8,128)(2,1)}, u32[]{:S(2)}) copy-start(bf16[512,128]{1,0:T(8,128)(2,1)} %exchange.3.into_ref) | copy-start | bytes 393220

commit v3 on v2

v3 whole, which is shorter than its diff:
```python
import functools

import jax
import jax.numpy as jnp
from jax import lax
from jax.experimental import pallas as pl
from jax.experimental.pallas import tpu as pltpu
from jax.sharding import PartitionSpec as P

MESH = pl.DeviceIdType.MESH
VMEM = pl.BlockSpec(memory_space=pltpu.VMEM)
SMEM = pl.BlockSpec(memory_space=pltpu.SMEM)
C = 96
WIDE = 128
MSG = 512
BF = jnp.bfloat16
F32 = jnp.float32


def message_plan():
    plan = []
    for ix in (0, 1):
        plan.append((ix, 64, (1 - 2 * ix, 0, 0)))
    for iy in (0, 1):
        plan.append((2 + iy, 64, (0, 1 - 2 * iy, 0)))
    plan.append((4, 64, (0, 0, 1)))
    for ix in (0, 1):
        for iy in (0, 1):
            plan.append((5 + 2 * ix + iy, 16, (1 - 2 * ix, 1 - 2 * iy, 0)))
    for ix in (0, 1):
        plan.append((9 + ix, 16, (1 - 2 * ix, 0, 1)))
    for iy in (0, 1):
        plan.append((11 + iy, 16, (0, 1 - 2 * iy, 1)))
    for ix in (0, 1):
        for iy in (0, 1):
            plan.append((13 + 2 * ix + iy, 16, (1 - 2 * ix, 1 - 2 * iy, 1)))
    return plan


def slot_row(slot):
    return slot * 64 if slot < 5 else 320 + (slot - 5) * 16


def pack_messages(wide_ref, msg_ref, q):
    blank = jnp.zeros((8, WIDE), F32)
    only = lax.broadcasted_iota(jnp.int32, (8, WIDE), 0) == 0
    for part in range(wide_ref.shape[0]):

        def rows(*spot, **stride):
            return wide_ref[part, pl.ds(*spot, **stride), :]

        def put(slot, value):
            start = slot_row(slot)
            msg_ref[pl.ds(start, value.shape[0]), pl.ds(part * WIDE, WIDE)] = value.astype(BF)

        def side(low, high):
            return jnp.where(q == 0, high, low)

        for ix in (0, 1):
            put(ix, rows(448 * (1 - ix), 64))
        for iy in (0, 1):
            edge = [rows(64 * i + 56 * (1 - iy), 8) for i in range(8)]
            put(2 + iy, jnp.concatenate(edge, axis=0))
        put(4, side(rows(0, 64, stride=8), rows(7, 64, stride=8)))
        for ix in (0, 1):
            x0 = 448 * (1 - ix)
            for iy in (0, 1):
                column = rows(x0 + 56 * (1 - iy), 8)
                put(5 + 2 * ix + iy, jnp.concatenate([column, blank], axis=0))
                corner = side(column, pltpu.roll(column, 1, 0))
                put(13 + 2 * ix + iy, jnp.concatenate([jnp.where(only, corner, 0.0), blank], axis=0))
            line = side(rows(x0, 8, stride=8), rows(x0 + 7, 8, stride=8))
            put(9 + ix, jnp.concatenate([line, blank], axis=0))
        for iy in (0, 1):
            y0 = 56 * (1 - iy)
            line = side(rows(y0, 8, stride=64), rows(y0 + 7, 8, stride=64))
            put(11 + iy, jnp.concatenate([line, blank], axis=0))


def pack_rows(position, count, x_ref, g_ref, code_ref, wide_ref, rows_ref):
    column = lax.broadcasted_iota(jnp.int32, (64, 512), 0)
    voxel = lax.broadcasted_iota(jnp.int32, (64, 512), 1)
    spread = jnp.where(column == voxel // 8, 1.0, 0.0).astype(BF)
    codes = jnp.broadcast_to(code_ref[...].astype(F32), (16, 64)).astype(BF)
    code = jnp.dot(codes, spread, preferred_element_type=F32).astype(jnp.int32)[:8]
    low = code // 8
    level = lax.broadcasted_iota(jnp.int32, (8, 512), 1) % 8
    live = (level >= low) & (level <= low + code % 8) & (count > 0)
    mask = jnp.where(live, 1.0, 0.0)
    first = lax.broadcasted_iota(jnp.int32, (8, 512), 0)
    place = jnp.where(first == 0, position.astype(F32), jnp.where(first == 1, mask, 0.0))
    blank = jnp.zeros((24, 512), F32)
    inside = jnp.broadcast_to(mask[:1], (C, 512)) > 0.0
    x = jnp.where(inside, x_ref[...].astype(F32), 0.0)
    g = jnp.where(inside, g_ref[...].astype(F32), 0.0)
    wide_ref[0] = jnp.concatenate([x, place, blank], axis=0).T
    wide_ref[1] = jnp.concatenate([g, jnp.zeros((32, 512), F32)], axis=0).T
    rows_ref[:, :WIDE] = wide_ref[0].astype(BF)
    rows_ref[:, WIDE:] = wide_ref[1].astype(BF)


def neighbour(offset):
    u, w, q = lax.axis_index("gx"), lax.axis_index("gy"), lax.axis_index("gz")
    nx, ny = lax.axis_size("gx"), lax.axis_size("gy")
    du, dv, dw = offset
    return ((u + du + nx) % nx, (w + dv + ny) % ny, 1 - q if dw else q)


def halo_copies(msg_ref, into_ref, send_sem, recv_sem):
    copies = []
    for slot, size, offset in message_plan():
        rows = pl.ds(slot_row(slot), size)
        copies.append(pltpu.make_async_remote_copy(
            src_ref=msg_ref.at[rows, :], dst_ref=into_ref.at[rows, :],
            send_sem=send_sem.at[slot], recv_sem=recv_sem.at[slot],
            device_id=neighbour(offset), device_id_type=MESH))
    return copies


def greet_neighbours(barrier):
    for _, _, offset in message_plan():
        pl.semaphore_signal(barrier, inc=1, device_id=neighbour(offset), device_id_type=MESH)


def pick_messages(position, into_ref):
    def bit(size, divisor):
        return jnp.zeros((size, into_ref.shape[1]), jnp.int32) + position // divisor % 2 == 0

    def at(slot):
        return into_ref[pl.ds(slot_row(slot), 64 if slot < 5 else 16), :].astype(F32)

    def two(slot, divisor):
        low = at(slot)
        return jnp.where(bit(low.shape[0], divisor), low, at(slot + 1))

    def four(slot):
        return jnp.where(bit(16, 4), two(slot, 2), two(slot + 2, 2))

    return jnp.concatenate(
        [two(0, 4), two(2, 2), at(4), four(5), two(9, 4), two(11, 2), four(13)], axis=0).astype(BF)


def halo_codes(position, sender):
    u, w, q = (lax.axis_index(axis) for axis in ("gx", "gy", "gz"))
    nx, ny = lax.axis_size("gx"), lax.axis_size("gy")
    own = (position // 4, position // 2 % 2, position % 2)
    theirs = (sender // 4, sender // 2 % 2, sender % 2)
    beyond = (u + 2 * own[0] - 1, w + 2 * own[1] - 1, q + 2 * own[2] - 1)
    sizes = (nx, ny, 2)
    r = lax.broadcasted_iota(jnp.int32, sender.shape, 1)
    face = r < 192
    t = jnp.where(face, r % 64, r % 16)
    high, low = t // 8, t % 8
    past = (
        (r < 64) | ((r >= 192) & (r < 224)) | (r >= 240),
        ((r >= 64) & (r < 128)) | ((r >= 192) & (r < 208)) | (r >= 224),
        ((r >= 128) & (r < 192)) | (r >= 208))
    index = (
        jnp.where(face, high, t),
        jnp.where(r < 64, high, jnp.where(face, low, t)),
        jnp.where(face, low, t))
    valid = face | (t < jnp.where(r < 240, 8, 1))
    spot = []
    for axis in range(3):
        far = 9 * own[axis]
        near = 9 - far
        same = theirs[axis] == own[axis]
        inner = jnp.where(same, 1 + index[axis], near)
        inner_ok = same | (index[axis] == 7 * own[axis])
        there = jnp.zeros_like(r) + beyond[axis]
        outer_ok = (theirs[axis] != own[axis]) & (there >= 0) & (there < sizes[axis])
        spot.append(jnp.where(past[axis], far, inner))
        valid = valid & ((past[axis] & outer_ok) | (jnp.logical_not(past[axis]) & inner_ok))
    return jnp.where(valid, (spot[0] * 10 + spot[1]) * 16 + spot[2], -1)


def build_patch(rows, picked, code, level_ref, all_ref, width):
    n = lax.broadcasted_iota(jnp.int32, (800, 256), 0)
    target = n // 8 * 16 + n % 8
    level = lax.broadcasted_iota(jnp.int32, rows.shape, 0) % 8
    for dz in (0, 1, 2):
        pick = jnp.where(target + dz == code, 1.0, 0.0).astype(BF)
        halo = jnp.dot(pick, picked, preferred_element_type=F32)
        if dz == 0:
            mine = jnp.where(level == 0, 0.0, pltpu.roll(rows, 1, 0))
        elif dz == 1:
            mine = rows
        else:
            mine = jnp.where(level == 7, 0.0, pltpu.roll(rows, 511, 0))
        level_ref[...] = halo
        for i in range(8):
            spot = pl.ds(((i + 1) * 10 + 1) * 8, 64)
            level_ref[spot, :] = level_ref[spot, :] + mine[64 * i : 64 * i + 64]
        for dy in (0, 1, 2):
            tap = dy * 3 + dz
            for x in range(10):
                all_ref[pl.ds(64 * x, 64), pl.ds(tap * width, width)] = (
                    level_ref[pl.ds((x * 10 + dy) * 8, 64), :].astype(BF))


def pack_grads(block, store):
    lane = lax.broadcasted_iota(jnp.int32, (C, WIDE), 1)
    for group in range(6):
        last = block(4 * group + 3)
        for t in range(3):
            shifted = pltpu.roll(last, C - 32 * t, 1)
            store(3 * group + t, jnp.where(lane < C, block(4 * group + t), shifted))
    for t in range(3):
        store(18 + t, block(24 + t))


def unpack_grads(load, store):
    lane = lax.broadcasted_iota(jnp.int32, (C, WIDE), 1)
    for group in range(6):
        last = jnp.zeros((C, WIDE), F32)
        for t in range(3):
            tile = load(3 * group + t)
            store(4 * group + t, tile)
            moved = pltpu.roll(tile, 32 + 32 * t, 1)
            last = jnp.where((lane >= 32 * t) & (lane < 32 * t + 32), moved, last)
        store(4 * group + 3, last)
    for t in range(3):
        store(24 + t, load(18 + t))


def square(block):
    gap = WIDE - C
    wide = jnp.concatenate([block.astype(F32), jnp.zeros((C, gap), F32)], axis=1)
    return jnp.concatenate([wide, jnp.zeros((gap, WIDE), F32)], axis=0)


def lay_weights(first_ref, second_ref, weight_ref):
    none = jnp.zeros((WIDE, WIDE), BF)

    def step(k, carry):
        top = pl.ds(pl.multiple_of(k % 9 * 2 * WIDE, WIDE), WIDE)
        bottom = pl.ds(pl.multiple_of(k % 9 * 2 * WIDE + WIDE, WIDE), WIDE)
        weight_ref[k // 9, top, :WIDE] = square(first_ref[k]).astype(BF)
        weight_ref[k // 9, top, WIDE:] = none
        weight_ref[k // 9, bottom, :WIDE] = none
        weight_ref[k // 9, bottom, WIDE:] = square(second_ref[26 - k]).T.astype(BF)
        return carry

    lax.fori_loop(0, 27, step, 0)


def lay_back_weights(first_ref, weight_ref):
    def step(k, carry):
        rows = pl.ds(pl.multiple_of(k % 9 * WIDE, WIDE), WIDE)
        weight_ref[k // 9, rows, :] = square(first_ref[26 - k]).T.astype(BF)
        return carry

    lax.fori_loop(0, 27, step, 0)


ROWS = 4096
HALF = ROWS // 2
PART = HALF // 16
CELL = PART // 16


def places():
    u = lax.axis_index("gx")
    w = lax.axis_index("gy")
    q = lax.axis_index("gz")
    core = w % 2
    y = w // 2 % 4
    x = q * 2 + w // 8
    mate = (u, w + 1 - 2 * core, q)

    def plane_peer(t):
        px = (x + t // 4) % 4
        py = (y + t % 4) % 4
        return px * 4 + py, (u, ((px % 2) * 4 + py) * 2 + core, px // 2)

    def line_peer(t):
        z = (u + t) % 16
        return z, (z, w, q)
    return u, w, q, core, x, y, x * 4 + y, mate, plane_peer, line_peer


def greet_sharers(barrier):
    u, w, q, core, x, y, chip, mate, plane_peer, line_peer = places()
    pl.semaphore_signal(barrier, inc=1, device_id=mate, device_id_type=MESH)

    def greet(t, carry):
        pl.semaphore_signal(barrier, inc=1, device_id=plane_peer(t)[1], device_id_type=MESH)
        pl.semaphore_signal(barrier, inc=1, device_id=line_peer(t)[1], device_id_type=MESH)
        return carry

    lax.fori_loop(1, 16, greet, 0)


def all_sum(between, data_ref, sum_ref, gathered, half_out, half_in, total, plane_out, plane_in,
            cell_src, line_in, line_all, own_part, pair_sem, plane_send, plane_recv,
            line_send, line_recv, line_send2, line_recv2, plane_send2, plane_recv2):
    u, w, q, core, x, y, chip, mate, plane_peer, line_peer = places()
    other = pl.multiple_of((1 - core) * HALF, HALF)
    own = pl.multiple_of(core * HALF, HALF)
    half_out[...] = data_ref[pl.ds(other, HALF), :].astype(jnp.bfloat16)
    swap = pltpu.make_async_remote_copy(
        src_ref=half_out, dst_ref=half_in, send_sem=pair_sem.at[0], recv_sem=pair_sem.at[1],
        device_id=mate, device_id_type=MESH)
    swap.start()
    swap.wait()
    total[...] = data_ref[pl.ds(own, HALF), :] + half_in[...].astype(jnp.float32)
    plane_out[...] = total[...].astype(jnp.bfloat16)

    def plane_copy(t):
        there, device = plane_peer(t)
        return pltpu.make_async_remote_copy(
            src_ref=plane_out.at[pl.ds(pl.multiple_of(there * PART, PART), PART), :],
            dst_ref=plane_in.at[t], send_sem=plane_send.at[t], recv_sem=plane_recv.at[t],
            device_id=device, device_id_type=MESH)

    def plane_start(t, carry):
        plane_copy(t).start()
        return carry

    lax.fori_loop(1, 16, plane_start, 0)
    between()
    mine = pl.multiple_of(chip * PART, PART)

    def plane_add(t, acc):
        plane_copy(t).wait_recv()
        return acc + plane_in[t].astype(jnp.float32)

    cell_src[...] = lax.fori_loop(1, 16, plane_add, total[pl.ds(mine, PART), :])

    def line_copy(t):
        there, device = line_peer(t)
        return pltpu.make_async_remote_copy(
            src_ref=cell_src.at[pl.ds(pl.multiple_of(there * CELL, CELL), CELL), :],
            dst_ref=line_in.at[t], send_sem=line_send.at[t], recv_sem=line_recv.at[t],
            device_id=device, device_id_type=MESH)

    def line_start(t, carry):
        line_copy(t).start()
        return carry

    lax.fori_loop(1, 16, line_start, 0)
    here = pl.multiple_of(u * CELL, CELL)

    def line_add(t, acc):
        line_copy(t).wait_recv()
        return acc + line_in[t]

    line_all[pl.ds(here, CELL), :] = lax.fori_loop(1, 16, line_add, cell_src[pl.ds(here, CELL), :])

    def spread_copy(t):
        there, device = line_peer(t)
        return pltpu.make_async_remote_copy(
            src_ref=line_all.at[pl.ds(here, CELL), :],
            dst_ref=line_all.at[pl.ds(here, CELL), :], send_sem=line_send2.at[t], recv_sem=line_recv2.at[t],
            device_id=device, device_id_type=MESH)

    def arrive_copy(t):
        z = (u - t + 16) % 16
        rows = pl.ds(pl.multiple_of(z * CELL, CELL), CELL)
        return pltpu.make_async_remote_copy(
            src_ref=line_all.at[rows, :],
            dst_ref=line_all.at[rows, :], send_sem=line_send2.at[t], recv_sem=line_recv2.at[t],
            device_id=line_peer(t)[1], device_id_type=MESH)

    def spread_start(t, carry):
        spread_copy(t).start()
        return carry

    def spread_wait(t, carry):
        arrive_copy(t).wait_recv()
        return carry

    lax.fori_loop(1, 16, spread_start, 0)
    lax.fori_loop(1, 16, spread_wait, 0)
    own_part[...] = line_all[...].astype(jnp.bfloat16)

    place = pl.multiple_of(own + mine, PART)
    gathered[pl.ds(place, PART), :] = own_part[...]

    def back_copy(t):
        there, device = plane_peer(t)
        return pltpu.make_async_remote_copy(
            src_ref=own_part,
            dst_ref=gathered.at[pl.ds(place, PART), :], send_sem=plane_send2.at[t], recv_sem=plane_recv2.at[t],
            device_id=device, device_id_type=MESH)

    def back_arrive(t):
        px = (x - t // 4 + 4) % 4
        py = (y - t % 4 + 4) % 4
        rows = pl.ds(pl.multiple_of(own + (px * 4 + py) * PART, PART), PART)
        return pltpu.make_async_remote_copy(
            src_ref=own_part,
            dst_ref=gathered.at[rows, :], send_sem=plane_send2.at[t], recv_sem=plane_recv2.at[t],
            device_id=plane_peer(t)[1], device_id_type=MESH)

    def back_start(t, carry):
        back_copy(t).start()
        return carry

    def back_wait(t, carry):
        back_arrive(t).wait_recv()
        return carry

    lax.fori_loop(1, 16, back_start, 0)
    lax.fori_loop(1, 16, back_wait, 0)

    join = pltpu.make_async_remote_copy(
        src_ref=gathered.at[pl.ds(own, HALF), :], dst_ref=gathered.at[pl.ds(own, HALF), :],
        send_sem=pair_sem.at[2], recv_sem=pair_sem.at[3],
        device_id=mate, device_id_type=MESH)
    join.start()

    def drain(t, carry):
        plane_copy(t).wait_send()
        line_copy(t).wait_send()
        spread_copy(t).wait_send()
        back_copy(t).wait_send()
        return carry

    lax.fori_loop(1, 16, drain, 0)
    join.wait_send()
    arrive = pltpu.make_async_remote_copy(
        src_ref=gathered.at[pl.ds(other, HALF), :], dst_ref=gathered.at[pl.ds(other, HALF), :],
        send_sem=pair_sem.at[2], recv_sem=pair_sem.at[3],
        device_id=mate, device_id_type=MESH)
    arrive.wait_recv()
    sum_ref[...] = gathered[...]


def whole_kernel(scale, position_ref, count_ref, x_ref, g_ref, code_ref, first_ref, second_ref,
                 out_ref, sum_ref, wide_ref, rows_ref, msg_ref, into_ref, back_msg_ref, back_into_ref,
                 weight_ref, back_weight_ref, level_ref, all_ref, back_level_ref, back_all_ref,
                 grads_ref, data_ref, delta_ref, send_sem, recv_sem, back_send_sem, back_recv_sem, *reduce_refs):
    q = lax.axis_index("gz")
    position = position_ref[0]
    barrier = pltpu.get_barrier_semaphore()
    greet_neighbours(barrier)
    greet_sharers(barrier)

    pack_rows(position, count_ref[0], x_ref, g_ref, code_ref, wide_ref, rows_ref)
    pack_messages(wide_ref, msg_ref, q)
    pl.semaphore_wait(barrier, 17 + 31)
    copies = halo_copies(msg_ref, into_ref, send_sem, recv_sem)
    for copy in copies:
        copy.start()
    lay_weights(first_ref, second_ref, weight_ref)
    for copy in copies:
        copy.wait()

    rows = rows_ref[...].astype(F32)
    picked = pick_messages(position, into_ref)
    sender = picked[:, :WIDE].astype(F32).T[C : C + 8].astype(jnp.int32)
    code = halo_codes(position, sender)[:1]
    build_patch(rows, picked, code, level_ref, all_ref, 2 * WIDE)
    acc = jnp.zeros((512, 2 * WIDE), F32)
    for dx in (0, 1, 2):
        acc = acc + jnp.dot(all_ref[pl.ds(64 * dx, 512), :], weight_ref[dx], preferred_element_type=F32)
    pre, back = acc[:, :WIDE], acc[:, WIDE:]
    mask = jnp.broadcast_to(rows[:, C + 1 : C + 2], (512, WIDE))
    sigma = jax.nn.sigmoid(pre)
    hidden = pre * sigma * mask
    delta = (back * sigma * (1.0 + pre * (1.0 - sigma)) * mask).astype(BF)
    delta_ref[...] = delta
    wide_ref[0] = delta.astype(F32)
    pack_messages(wide_ref.at[pl.ds(0, 1)], back_msg_ref, q)
    back_copies = halo_copies(back_msg_ref, back_into_ref, back_send_sem, back_recv_sem)
    for copy in back_copies:
        copy.start()
    both = jnp.concatenate([hidden.T, delta.astype(F32).T], axis=0).astype(BF)
    for dx in (0, 1, 2):
        grads_ref[dx] = jnp.dot(both, all_ref[pl.ds(64 * dx, 512), :], preferred_element_type=F32)

    def first_block(k):
        return grads_ref[k // 9, WIDE : WIDE + C, pl.ds(k % 9 * 2 * WIDE, WIDE)] * scale

    def second_block(k):
        turned = 26 - k
        return grads_ref[turned // 9, 0:C, pl.ds(turned % 9 * 2 * WIDE + WIDE, WIDE)] * scale

    for half, block in ((0, first_block), (1, second_block)):

        def store(tile, value):
            data_ref[pl.ds(half * HALF + tile * C, C), :] = value

        pack_grads(block, store)
        data_ref[pl.ds(half * HALF + 21 * C, HALF - 21 * C), :] = jnp.zeros((HALF - 21 * C, WIDE), F32)

    def backward():
        lay_back_weights(first_ref, back_weight_ref)
        for copy in back_copies:
            copy.wait()
        back_picked = pick_messages(position, back_into_ref)
        build_patch(delta_ref[...].astype(F32), back_picked, code, back_level_ref, back_all_ref, WIDE)
        grad = rows_ref[:, WIDE:].astype(F32)
        for dx in (0, 1, 2):
            grad = grad + jnp.dot(
                back_all_ref[pl.ds(64 * dx, 512), :], back_weight_ref[dx], preferred_element_type=F32)
        out_ref[...] = (grad * mask).T[:C].astype(BF)

    all_sum(backward, data_ref, sum_ref, *reduce_refs)


def whole(scale, position, count, x, g, codes, first, second):
    sems = lambda n: pltpu.SemaphoreType.DMA((n,))
    return pl.pallas_call(
        functools.partial(whole_kernel, scale),
        out_shape=(jax.ShapeDtypeStruct((C, 512), BF), jax.ShapeDtypeStruct((ROWS, WIDE), BF)),
        in_specs=[SMEM, SMEM] + [VMEM] * 5,
        out_specs=(VMEM, VMEM),
        scratch_shapes=[
            pltpu.VMEM((2, 512, WIDE), F32), pltpu.VMEM((512, 2 * WIDE), BF),
            pltpu.VMEM((MSG, 2 * WIDE), BF), pltpu.VMEM((MSG, 2 * WIDE), BF),
            pltpu.VMEM((MSG, WIDE), BF), pltpu.VMEM((MSG, WIDE), BF),
            pltpu.VMEM((3, 9 * 2 * WIDE, 2 * WIDE), BF), pltpu.VMEM((3, 9 * WIDE, WIDE), BF),
            pltpu.VMEM((800, 2 * WIDE), F32), pltpu.VMEM((640, 9 * 2 * WIDE), BF),
            pltpu.VMEM((800, WIDE), F32), pltpu.VMEM((640, 9 * WIDE), BF),
            pltpu.VMEM((3, 2 * WIDE, 9 * 2 * WIDE), F32), pltpu.VMEM((ROWS, WIDE), F32),
            pltpu.VMEM((512, WIDE), BF),
            sems(17), sems(17), sems(17), sems(17),
            pltpu.VMEM((ROWS, WIDE), BF),
            pltpu.VMEM((HALF, WIDE), BF), pltpu.VMEM((HALF, WIDE), BF),
            pltpu.VMEM((HALF, WIDE), F32), pltpu.VMEM((HALF, WIDE), BF),
            pltpu.VMEM((16, PART, WIDE), BF), pltpu.VMEM((PART, WIDE), F32),
            pltpu.VMEM((16, CELL, WIDE), F32), pltpu.VMEM((PART, WIDE), F32),
            pltpu.VMEM((PART, WIDE), BF),
            sems(4), sems(16), sems(16), sems(16), sems(16), sems(16), sems(16), sems(16), sems(16),
        ],
        compiler_params=pltpu.CompilerParams(
            collective_id=1, has_side_effects=True, vmem_limit_bytes=56 * 2 ** 20),
        name="whole",
    )(position, count, x, g, codes, first, second)


def finish_kernel(grad_ref, sum_ref, out_ref, first_ref, second_ref):
    out_ref[...] = grad_ref[...]

    def load_first(tile):
        return sum_ref[pl.ds(tile * C, C), :].astype(F32)

    def load_second(tile):
        return sum_ref[pl.ds(HALF + tile * C, C), :].astype(F32)

    def store_first(k, value):
        first_ref[k] = value.T[:C]

    def store_second(k, value):
        second_ref[k] = value[:, :C]

    unpack_grads(load_first, store_first)
    unpack_grads(load_second, store_second)


def finish(grad, summed):
    return pl.pallas_call(
        finish_kernel,
        out_shape=(
            jax.ShapeDtypeStruct((C, 512), BF),
            jax.ShapeDtypeStruct((27, C, C), F32), jax.ShapeDtypeStruct((27, C, C), F32)),
        in_specs=[VMEM, VMEM],
        out_specs=(VMEM,) * 3,
        compiler_params=pltpu.CompilerParams(vmem_limit_bytes=32 * 2 ** 20),
        name="finish",
    )(grad, summed)


def shards(features, cotangent, first_weight, second_weight, slot_position, brick_count, column_code):
    devices = lax.axis_size("gx") * lax.axis_size("gy") * lax.axis_size("gz")
    scale = float(devices ** -0.5 / 8.0)
    grad, summed = whole(
        scale, slot_position.reshape(1), brick_count.reshape(1), features.reshape(C, 512),
        cotangent.reshape(C, 512), column_code.reshape(1, 64), first_weight, second_weight)
    grad_input, first_grad, second_grad = finish(grad, summed)
    return grad_input.reshape(1, 1, 1, 1, C, 512), first_grad, second_grad


def solution(mesh):
    placed = (
        P("gx", "gy", "gz", None, None, None),
        P("gx", "gy", "gz", None, None, None),
        P(),
        P(),
        P("gx", "gy", "gz", None),
        P("gx", "gy", "gz"),
        P("gx", "gy", "gz", None, None),
    )
    return jax.shard_map(
        shards,
        mesh=mesh,
        in_specs=placed,
        out_specs=(P("gx", "gy", "gz", None, None, None), P(), P()),
        check_vma=False,
    )
```

time: 111 us -> 77.6 us (0.70)
  Pallas kernels: 94.3 us -> 73.3 us
  local copies, waits for them, and re-layouts: 11.5 us -> 2.11 us
  other arithmetic: 2.3 us -> 0 us
    pallas_call x6 -> x2, Pallas kernels: 94.3 us -> 73.3 us  [the longest x1 71.3 us: whole(): pl.pallas_call(functools.partial(whole_kernel, scale), out_shape=(jax.Sha...]
    concatenate x1 -> x0, local copies, waits for them, and re-layouts: 5.78 us -> none  [both_weights(): jnp.concatenate([top, bottom], axis=1).reshape(3, 9 * 2 * WIDE, 2 * WIDE)]
    concatenate x1 -> x0, other arithmetic: 2.3 us -> none  [both_weights(): jnp.concatenate([top, bottom], axis=1).reshape(3, 9 * 2 * WIDE, 2 * WIDE)]
    transpose x2 -> x0, local copies, waits for them, and re-layouts: 2.02 us -> none  [the longest x1 1.14 us: both_weights(): turned = second[::-1].transpose(0, 2, 1)]
    unnamed x14 -> x4, local copies, waits for them, and re-layouts: 2.83 us -> 2.11 us
where the time goes in v3:
time: 77.6 us; the launch traced here: 77.4 us
  Pallas kernels  73.3 us (94%)
  local copies, waits for them, and re-layouts  2.11 us (3%)
  between operations  1.94 us (2%)
    pallas_call x1, Pallas kernels, whole(): pl.pallas_call(functools.partial(whole_kernel, scale), out_shape=(jax.Sha...  71.3 us
    unnamed x4, local copies, waits for them, and re-layouts  2.11 us
    pallas_call x1, Pallas kernels, finish(): pl.pallas_call(finish_kernel, out_shape=(jax.ShapeDtypeStruct((C, 512), B...  2.01 us

profile of v3, /device:TPU:1, one launch (start us, length us, event | category | flops | bytes accessed | tf_op | source)
XLA Modules:
  0.0 77.4 jit_solution(14859129588024249031)
XLA Ops:
  1.9 71.3 %whole.1 = (bf16[96,512]{1,0:T(8,128)(2,1)}, bf16[4096,128]{1,0:T(8,128)(2,1)}) custom-call(s32[1]{0:T(128)} %bitcast.6.position_ref, s32[1]{0:T(128)} %bitcast.7.count_ref, bf16[96,512]{1,0:T(8,128)(2,1)} %bitcast.8, bf16[96,512]{1,0:T(8,128)(2,1)} %bitcast.9, s32[1,64]{1,0:T(1,128)} %bitcast.10, bf16[27,96,96]{2,1,0:T(8,128)(2,1)} %first_ref.1, ...), custom_call_target="tpu_custom_call" | custom-call | tf_op jit(solution)/shard_map/whole/pallas_call | solution.py:505
  73.3 0.0 copy-start
  73.3 1.2 %copy-done = bf16[4096,128]{1,0:T(8,128)(2,1)S(1)} copy-done((bf16[4096,128]{1,0:T(8,128)(2,1)S(1)}, bf16[4096,128]{1,0:T(8,128)(2,1)}, u32[]{:S(2)}) %copy-start) | copy-done | bytes 1048600
  74.5 0.0 copy-start.1
  74.5 0.9 %copy-done.1 = bf16[96,512]{1,0:T(8,128)(2,1)S(1)} copy-done((bf16[96,512]{1,0:T(8,128)(2,1)S(1)}, bf16[96,512]{1,0:T(8,128)(2,1)}, u32[]{:S(2)}) %copy-start.1) | copy-done | bytes 98328
  75.4 2.0 %finish.1 = (bf16[96,512]{1,0:T(8,128)(2,1)}, f32[27,96,96]{2,1,0:T(8,128)}, f32[27,96,96]{2,1,0:T(8,128)}) custom-call(bf16[96,512]{1,0:T(8,128)(2,1)S(1)} %copy-done.1, bf16[4096,128]{1,0:T(8,128)(2,1)S(1)} %copy-done), custom_call_target="tpu_custom_call" | custom-call | tf_op jit(solution)/shard_map/finish/pallas_call | solution.py:554
Async XLA Ops:
  73.3 1.2 %copy-start = (bf16[4096,128]{1,0:T(8,128)(2,1)S(1)}, bf16[4096,128]{1,0:T(8,128)(2,1)}, u32[]{:S(2)}) copy-start(bf16[4096,128]{1,0:T(8,128)(2,1)} %get-tuple-element.9.sum_ref) | copy-start | bytes 3145732
  74.5 0.9 %copy-start.1 = (bf16[96,512]{1,0:T(8,128)(2,1)S(1)}, bf16[96,512]{1,0:T(8,128)(2,1)}, u32[]{:S(2)}) copy-start(bf16[96,512]{1,0:T(8,128)(2,1)} %get-tuple-element.8.grad_ref) | copy-start | bytes 294916

commit v4 on v3

v4 whole, which is shorter than its diff:
```python
import functools

import jax
import jax.numpy as jnp
from jax import lax
from jax.experimental import pallas as pl
from jax.experimental.pallas import tpu as pltpu
from jax.sharding import PartitionSpec as P

MESH = pl.DeviceIdType.MESH
VMEM = pl.BlockSpec(memory_space=pltpu.VMEM)
SMEM = pl.BlockSpec(memory_space=pltpu.SMEM)
C = 96
WIDE = 128
MSG = 512
BF = jnp.bfloat16
F32 = jnp.float32


def message_plan():
    plan = []
    for ix in (0, 1):
        plan.append((ix, 64, (1 - 2 * ix, 0, 0)))
    for iy in (0, 1):
        plan.append((2 + iy, 64, (0, 1 - 2 * iy, 0)))
    plan.append((4, 64, (0, 0, 1)))
    for ix in (0, 1):
        for iy in (0, 1):
            plan.append((5 + 2 * ix + iy, 16, (1 - 2 * ix, 1 - 2 * iy, 0)))
    for ix in (0, 1):
        plan.append((9 + ix, 16, (1 - 2 * ix, 0, 1)))
    for iy in (0, 1):
        plan.append((11 + iy, 16, (0, 1 - 2 * iy, 1)))
    for ix in (0, 1):
        for iy in (0, 1):
            plan.append((13 + 2 * ix + iy, 16, (1 - 2 * ix, 1 - 2 * iy, 1)))
    return plan


def slot_row(slot):
    return slot * 64 if slot < 5 else 320 + (slot - 5) * 16


def pack_messages(wide_ref, msg_ref, q):
    blank = jnp.zeros((8, WIDE), F32)
    only = lax.broadcasted_iota(jnp.int32, (8, WIDE), 0) == 0
    for part in range(wide_ref.shape[0]):

        def rows(*spot, **stride):
            return wide_ref[part, pl.ds(*spot, **stride), :]

        def put(slot, value):
            start = slot_row(slot)
            msg_ref[pl.ds(start, value.shape[0]), pl.ds(part * WIDE, WIDE)] = value.astype(BF)

        def side(low, high):
            return jnp.where(q == 0, high, low)

        for ix in (0, 1):
            put(ix, rows(448 * (1 - ix), 64))
        for iy in (0, 1):
            edge = [rows(64 * i + 56 * (1 - iy), 8) for i in range(8)]
            put(2 + iy, jnp.concatenate(edge, axis=0))
        put(4, side(rows(0, 64, stride=8), rows(7, 64, stride=8)))
        for ix in (0, 1):
            x0 = 448 * (1 - ix)
            for iy in (0, 1):
                column = rows(x0 + 56 * (1 - iy), 8)
                put(5 + 2 * ix + iy, jnp.concatenate([column, blank], axis=0))
                corner = side(column, pltpu.roll(column, 1, 0))
                put(13 + 2 * ix + iy, jnp.concatenate([jnp.where(only, corner, 0.0), blank], axis=0))
            line = side(rows(x0, 8, stride=8), rows(x0 + 7, 8, stride=8))
            put(9 + ix, jnp.concatenate([line, blank], axis=0))
        for iy in (0, 1):
            y0 = 56 * (1 - iy)
            line = side(rows(y0, 8, stride=64), rows(y0 + 7, 8, stride=64))
            put(11 + iy, jnp.concatenate([line, blank], axis=0))


def pack_rows(position, count, x_ref, g_ref, code_ref, wide_ref, rows_ref):
    column = lax.broadcasted_iota(jnp.int32, (64, 512), 0)
    voxel = lax.broadcasted_iota(jnp.int32, (64, 512), 1)
    spread = jnp.where(column == voxel // 8, 1.0, 0.0).astype(BF)
    codes = jnp.broadcast_to(code_ref[...].astype(F32), (16, 64)).astype(BF)
    code = jnp.dot(codes, spread, preferred_element_type=F32).astype(jnp.int32)[:8]
    low = code // 8
    level = lax.broadcasted_iota(jnp.int32, (8, 512), 1) % 8
    live = (level >= low) & (level <= low + code % 8) & (count > 0)
    mask = jnp.where(live, 1.0, 0.0)
    first = lax.broadcasted_iota(jnp.int32, (8, 512), 0)
    place = jnp.where(first == 0, position.astype(F32), jnp.where(first == 1, mask, 0.0))
    blank = jnp.zeros((24, 512), F32)
    inside = jnp.broadcast_to(mask[:1], (C, 512)) > 0.0
    x = jnp.where(inside, x_ref[...].astype(F32), 0.0)
    g = jnp.where(inside, g_ref[...].astype(F32), 0.0)
    wide_ref[0] = jnp.concatenate([x, place, blank], axis=0).T
    wide_ref[1] = jnp.concatenate([g, jnp.zeros((32, 512), F32)], axis=0).T
    rows_ref[:, :WIDE] = wide_ref[0].astype(BF)
    rows_ref[:, WIDE:] = wide_ref[1].astype(BF)


def neighbour(offset):
    u, w, q = lax.axis_index("gx"), lax.axis_index("gy"), lax.axis_index("gz")
    nx, ny = lax.axis_size("gx"), lax.axis_size("gy")
    du, dv, dw = offset
    return ((u + du + nx) % nx, (w + dv + ny) % ny, 1 - q if dw else q)


def halo_copies(msg_ref, into_ref, send_sem, recv_sem):
    copies = []
    for slot, size, offset in message_plan():
        rows = pl.ds(slot_row(slot), size)
        copies.append(pltpu.make_async_remote_copy(
            src_ref=msg_ref.at[rows, :], dst_ref=into_ref.at[rows, :],
            send_sem=send_sem.at[slot], recv_sem=recv_sem.at[slot],
            device_id=neighbour(offset), device_id_type=MESH))
    return copies


def greet_neighbours(barrier):
    for _, _, offset in message_plan():
        pl.semaphore_signal(barrier, inc=1, device_id=neighbour(offset), device_id_type=MESH)


def pick_messages(position, into_ref):
    def bit(size, divisor):
        return jnp.zeros((size, into_ref.shape[1]), jnp.int32) + position // divisor % 2 == 0

    def at(slot):
        return into_ref[pl.ds(slot_row(slot), 64 if slot < 5 else 16), :].astype(F32)

    def two(slot, divisor):
        low = at(slot)
        return jnp.where(bit(low.shape[0], divisor), low, at(slot + 1))

    def four(slot):
        return jnp.where(bit(16, 4), two(slot, 2), two(slot + 2, 2))

    return jnp.concatenate(
        [two(0, 4), two(2, 2), at(4), four(5), two(9, 4), two(11, 2), four(13)], axis=0).astype(BF)


def halo_codes(position, sender):
    u, w, q = (lax.axis_index(axis) for axis in ("gx", "gy", "gz"))
    nx, ny = lax.axis_size("gx"), lax.axis_size("gy")
    own = (position // 4, position // 2 % 2, position % 2)
    theirs = (sender // 4, sender // 2 % 2, sender % 2)
    beyond = (u + 2 * own[0] - 1, w + 2 * own[1] - 1, q + 2 * own[2] - 1)
    sizes = (nx, ny, 2)
    r = lax.broadcasted_iota(jnp.int32, sender.shape, 1)
    face = r < 192
    t = jnp.where(face, r % 64, r % 16)
    high, low = t // 8, t % 8
    past = (
        (r < 64) | ((r >= 192) & (r < 224)) | (r >= 240),
        ((r >= 64) & (r < 128)) | ((r >= 192) & (r < 208)) | (r >= 224),
        ((r >= 128) & (r < 192)) | (r >= 208))
    index = (
        jnp.where(face, high, t),
        jnp.where(r < 64, high, jnp.where(face, low, t)),
        jnp.where(face, low, t))
    valid = face | (t < jnp.where(r < 240, 8, 1))
    spot = []
    for axis in range(3):
        far = 9 * own[axis]
        near = 9 - far
        same = theirs[axis] == own[axis]
        inner = jnp.where(same, 1 + index[axis], near)
        inner_ok = same | (index[axis] == 7 * own[axis])
        there = jnp.zeros_like(r) + beyond[axis]
        outer_ok = (theirs[axis] != own[axis]) & (there >= 0) & (there < sizes[axis])
        spot.append(jnp.where(past[axis], far, inner))
        valid = valid & ((past[axis] & outer_ok) | (jnp.logical_not(past[axis]) & inner_ok))
    return jnp.where(valid, (spot[0] * 10 + spot[1]) * 16 + spot[2], -1)


def build_patch(rows, picked, code, level_ref, patch_refs):
    n = lax.broadcasted_iota(jnp.int32, (800, 256), 0)
    target = n // 8 * 16 + n % 8
    level = lax.broadcasted_iota(jnp.int32, rows.shape, 0) % 8
    for dz in (0, 1, 2):
        pick = jnp.where(target + dz == code, 1.0, 0.0).astype(BF)
        halo = jnp.dot(pick, picked, preferred_element_type=F32)
        if dz == 0:
            mine = jnp.where(level == 0, 0.0, pltpu.roll(rows, 1, 0))
        elif dz == 1:
            mine = rows
        else:
            mine = jnp.where(level == 7, 0.0, pltpu.roll(rows, 511, 0))
        level_ref[...] = halo
        for i in range(8):
            spot = pl.ds(((i + 1) * 10 + 1) * 8, 64)
            level_ref[spot, :] = level_ref[spot, :] + mine[64 * i : 64 * i + 64]
        for part, patch_ref in enumerate(patch_refs):
            for dy in (0, 1, 2):
                tap = dy * 3 + dz
                for x in range(10):
                    patch_ref[pl.ds(64 * x, 64), pl.ds(tap * WIDE, WIDE)] = (
                        level_ref[pl.ds((x * 10 + dy) * 8, 64), pl.ds(part * WIDE, WIDE)].astype(BF))


def convolve(start, patch_ref, weight_ref):
    total = start
    for dx in (0, 1, 2):
        total = total + jnp.dot(patch_ref[pl.ds(64 * dx, 512), :], weight_ref[dx], preferred_element_type=F32)
    return total


def pack_grads(block, store):
    lane = lax.broadcasted_iota(jnp.int32, (C, WIDE), 1)
    for group in range(2):
        last = block(4 * group + 3)
        for t in range(3):
            shifted = pltpu.roll(last, C - 32 * t, 1)
            store(3 * group + t, jnp.where(lane < C, block(4 * group + t), shifted))
    store(6, block(8))


def unpack_grads(load, store):
    lane = lax.broadcasted_iota(jnp.int32, (C, WIDE), 1)
    for group in range(2):
        last = jnp.zeros((C, WIDE), F32)
        for t in range(3):
            tile = load(3 * group + t)
            store(4 * group + t, tile)
            moved = pltpu.roll(tile, 32 + 32 * t, 1)
            last = jnp.where((lane >= 32 * t) & (lane < 32 * t + 32), moved, last)
        store(4 * group + 3, last)
    store(8, load(6))


def square(block):
    gap = WIDE - C
    wide = jnp.concatenate([block.astype(F32), jnp.zeros((C, gap), F32)], axis=1)
    return jnp.concatenate([wide, jnp.zeros((gap, WIDE), F32)], axis=0)


def lay_weights(kernel_ref, weight_ref, turned):
    def step(k, carry):
        rows = pl.ds(pl.multiple_of(k % 9 * WIDE, WIDE), WIDE)
        block = square(kernel_ref[26 - k]).T if turned else square(kernel_ref[k])
        weight_ref[k // 9, rows, :] = block.astype(BF)
        return carry

    lax.fori_loop(0, 27, step, 0)


ROWS = 4096
HALF = ROWS // 2
STRIP = 7 * C
PART = HALF // 16
CELL = PART // 4


def places():
    u = lax.axis_index("gx")
    w = lax.axis_index("gy")
    q = lax.axis_index("gz")
    core = w % 2
    y = w // 2 % 4
    x = q * 2 + w // 8
    mate = (u, w + 1 - 2 * core, q)

    def plane_peer(t):
        px = (x + t // 4) % 4
        py = (y + t % 4) % 4
        return px * 4 + py, (u, ((px % 2) * 4 + py) * 2 + core, px // 2)

    def near_peer(t):
        r = (u % 4 + t) % 4
        return r, (u // 4 * 4 + r, w, q)

    def far_peer(t):
        g = (u // 4 + t) % 4
        return g, (g * 4 + u % 4, w, q)

    return core, x, y, mate, plane_peer, near_peer, far_peer


def greet_sharers(barrier):
    core, x, y, mate, plane_peer, near_peer, far_peer = places()

    def greet(t, carry):
        pl.semaphore_signal(barrier, inc=1, device_id=plane_peer(t)[1], device_id_type=MESH)
        return carry

    def greet_line(t, carry):
        pl.semaphore_signal(barrier, inc=1, device_id=far_peer(t)[1], device_id_type=MESH)
        pl.semaphore_signal(barrier, inc=1, device_id=near_peer(t)[1], device_id_type=MESH)
        return carry

    lax.fori_loop(1, 4, greet_line, 0)
    lax.fori_loop(1, 16, greet, 0)
    pl.semaphore_signal(barrier, inc=1, device_id=mate, device_id_type=MESH)


def remote(src, dst, sends, recvs, index, device):
    return pltpu.make_async_remote_copy(
        src_ref=src, dst_ref=dst, send_sem=sends.at[index], recv_sem=recvs.at[index],
        device_id=device, device_id_type=MESH)


def swap_copy(strip, half_out, half_in, swap_send, swap_recv):
    rows = pl.ds(strip * STRIP, STRIP)
    return remote(half_out.at[rows, :], half_in.at[rows, :], swap_send, swap_recv, strip, places()[3])


def start_swap(strip, data_ref, half_out, half_in, swap_send, swap_recv):
    core = places()[0]
    theirs = pl.multiple_of((1 - core) * HALF + strip * STRIP, 16)
    half_out[pl.ds(strip * STRIP, STRIP), :] = data_ref[pl.ds(theirs, STRIP), :].astype(BF)
    swap_copy(strip, half_out, half_in, swap_send, swap_recv).start()


def all_sum(fill_plane, fill_line, data_ref, sum_ref, gathered, half_out, half_in, total, plane_out, plane_in,
            near_src, near_in, far_all, own_part, swap_send, swap_recv, plane_send, plane_recv,
            near_send, near_recv, far_send, far_recv, near_send2, near_recv2, plane_send2, plane_recv2,
            join_send, join_recv, out_sem):
    core, x, y, mate, plane_peer, near_peer, far_peer = places()
    u = lax.axis_index("gx")
    chip = x * 4 + y
    own = pl.multiple_of(core * HALF, HALF)
    other = pl.multiple_of((1 - core) * HALF, HALF)

    for strip in range(3):
        rows = pl.ds(strip * STRIP, STRIP)
        swap_copy(strip, half_out, half_in, swap_send, swap_recv).wait()
        mine = data_ref[pl.ds(pl.multiple_of(own + strip * STRIP, 16), STRIP), :]
        both = mine + half_in[rows, :].astype(F32)
        total[rows, :] = both
        plane_out[rows, :] = both.astype(BF)
    rest = pl.ds(3 * STRIP, HALF - 3 * STRIP)
    total[rest, :] = jnp.zeros((HALF - 3 * STRIP, WIDE), F32)
    plane_out[rest, :] = jnp.zeros((HALF - 3 * STRIP, WIDE), BF)

    def plane_copy(t):
        there, device = plane_peer(t)
        rows = pl.ds(pl.multiple_of(there * PART, PART), PART)
        return remote(plane_out.at[rows, :], plane_in.at[t], plane_send, plane_recv, t, device)

    def plane_start(t, carry):
        plane_copy(t).start()
        return carry

    lax.fori_loop(1, 16, plane_start, 0)
    fill_plane()

    def plane_add(t, acc):
        plane_copy(t).wait_recv()
        return acc + plane_in[t].astype(F32)

    part = pl.multiple_of(chip * PART, PART)
    near_src[...] = lax.fori_loop(1, 16, plane_add, total[pl.ds(part, PART), :])

    def near_copy(t):
        there, device = near_peer(t)
        rows = pl.ds(pl.multiple_of(there * CELL, CELL), CELL)
        return remote(near_src.at[rows, :], near_in.at[t], near_send, near_recv, t, device)

    for t in (1, 2, 3):
        near_copy(t).start()
    cell = pl.multiple_of(u % 4 * CELL, CELL)
    cell_sum = near_src[pl.ds(cell, CELL), :]
    for t in (1, 2, 3):
        near_copy(t).wait_recv()
        cell_sum = cell_sum + near_in[t]

    group = u // 4
    far_all[group] = cell_sum

    def far_copy(t, slot):
        return remote(far_all.at[group], far_all.at[slot], far_send, far_recv, t, far_peer(t)[1])

    for t in (1, 2, 3):
        far_copy(t, group).start()
    fill_line()
    for t in (1, 2, 3):
        far_copy(t, (group - t + 4) % 4).wait_recv()
    final = (far_all[0] + far_all[1]) + (far_all[2] + far_all[3])
    own_part[pl.ds(cell, CELL), :] = final.astype(BF)

    def near_back(t, owner):
        rows = pl.ds(pl.multiple_of(owner * CELL, CELL), CELL)
        return remote(own_part.at[rows, :], own_part.at[rows, :], near_send2, near_recv2, t, near_peer(t)[1])

    for t in (1, 2, 3):
        near_back(t, u % 4).start()
    for t in (1, 2, 3):
        near_back(t, (u % 4 - t + 4) % 4).wait_recv()

    place = pl.multiple_of(own + part, PART)

    def plane_back(t):
        return remote(own_part, gathered.at[pl.ds(place, PART), :], plane_send2, plane_recv2, t, plane_peer(t)[1])

    def plane_back_start(t, carry):
        plane_back(t).start()
        return carry

    def source_rows(t, base):
        px = (x - t // 4 + 4) % 4
        py = (y - t % 4 + 4) % 4
        return pl.ds(pl.multiple_of(base + (px * 4 + py) * PART, PART), PART)

    def join_copy(t, base):
        rows = source_rows(t, base)
        return remote(gathered.at[rows, :], gathered.at[rows, :], join_send, join_recv, t, mate)

    lax.fori_loop(1, 16, plane_back_start, 0)
    gathered[pl.ds(place, PART), :] = own_part[...]
    join_copy(0, own).start()

    def plane_back_wait(t, carry):
        remote(own_part, gathered.at[source_rows(t, own), :], plane_send2, plane_recv2, t,
               plane_peer(t)[1]).wait_recv()
        join_copy(t, own).start()
        return carry

    lax.fori_loop(1, 16, plane_back_wait, 0)
    first_out = pltpu.make_async_copy(
        gathered.at[pl.ds(own, HALF), :], sum_ref.at[pl.ds(own, HALF), :], out_sem.at[0])
    first_out.start()

    def join_wait(t, carry):
        join_copy(t, other).wait_recv()
        return carry

    lax.fori_loop(0, 16, join_wait, 0)
    second_out = pltpu.make_async_copy(
        gathered.at[pl.ds(other, HALF), :], sum_ref.at[pl.ds(other, HALF), :], out_sem.at[1])
    second_out.start()

    def drain(t, carry):
        plane_copy(t).wait_send()
        plane_back(t).wait_send()
        join_copy(t, own).wait_send()
        return carry

    lax.fori_loop(1, 16, drain, 0)
    join_copy(0, own).wait_send()
    for t in (1, 2, 3):
        near_copy(t).wait_send()
        far_copy(t, group).wait_send()
        near_back(t, u % 4).wait_send()
    first_out.wait()
    second_out.wait()


SHARERS = 1 + 15 + 3 + 3


def whole_kernel(scale, position_ref, count_ref, x_hbm, g_hbm, code_hbm, first_hbm, second_hbm,
                 out_ref, sum_ref, x_ref, g_ref, code_ref, first_ref, second_ref, load_sem,
                 wide_ref, rows_ref, msg_ref, into_ref, back_msg_ref, back_into_ref,
                 x_weight_ref, g_weight_ref, back_weight_ref, level_ref, x_patch_ref, g_patch_ref,
                 back_level_ref, back_patch_ref, grads_ref, data_ref, delta_ref,
                 send_sem, recv_sem, back_send_sem, back_recv_sem, *reduce_refs):
    q = lax.axis_index("gz")
    position = position_ref[0]
    barrier = pltpu.get_barrier_semaphore()
    greet_sharers(barrier)
    greet_neighbours(barrier)
    loads = [
        pltpu.make_async_copy(src, dst, load_sem.at[i])
        for i, (src, dst) in enumerate((
            (x_hbm, x_ref), (g_hbm, g_ref), (code_hbm, code_ref), (first_hbm, first_ref), (second_hbm, second_ref)))]
    for load in loads:
        load.start()
    for load in loads[:3]:
        load.wait()
    pack_rows(position, count_ref[0], x_ref, g_ref, code_ref, wide_ref, rows_ref)
    pack_messages(wide_ref, msg_ref, q)
    pl.semaphore_wait(barrier, 17 + SHARERS)
    copies = halo_copies(msg_ref, into_ref, send_sem, recv_sem)
    for copy in copies:
        copy.start()
    for load in loads[3:]:
        load.wait()
    lay_weights(first_ref, x_weight_ref, False)
    lay_weights(second_ref, g_weight_ref, True)
    for copy in copies:
        copy.wait()

    rows = rows_ref[...].astype(F32)
    picked = pick_messages(position, into_ref)
    sender = picked[:, :WIDE].astype(F32).T[C : C + 8].astype(jnp.int32)
    code = halo_codes(position, sender)[:1]
    build_patch(rows, picked, code, level_ref, (x_patch_ref, g_patch_ref))
    nothing = jnp.zeros((512, WIDE), F32)
    pre = convolve(nothing, x_patch_ref, x_weight_ref)
    back = convolve(nothing, g_patch_ref, g_weight_ref)
    mask = jnp.broadcast_to(rows[:, C + 1 : C + 2], (512, WIDE))
    sigma = jax.nn.sigmoid(pre)
    hidden = pre * sigma * mask
    delta = (back * sigma * (1.0 + pre * (1.0 - sigma)) * mask).astype(BF)
    delta_ref[...] = delta
    wide_ref[0] = delta.astype(F32)
    pack_messages(wide_ref.at[pl.ds(0, 1)], back_msg_ref, q)
    back_copies = halo_copies(back_msg_ref, back_into_ref, back_send_sem, back_recv_sem)
    for copy in back_copies:
        copy.start()

    turned = (delta.astype(F32).T[:C].astype(BF), hidden.T[:C].astype(BF))
    for dx in (0, 1, 2):
        for half, patch_ref in ((0, x_patch_ref), (1, g_patch_ref)):
            grads_ref[half] = jnp.dot(
                turned[half], patch_ref[pl.ds(64 * dx, 512), :], preferred_element_type=F32)

            def block(tap):
                return grads_ref[half, :, pl.ds(tap * WIDE, WIDE)] * scale

            def store(tile, value):
                data_ref[pl.ds(half * HALF + dx * STRIP + tile * C, C), :] = value

            pack_grads(block, store)
        start_swap(dx, data_ref, *reduce_refs[1:3], *reduce_refs[10:12])

    def fill_plane():
        lay_weights(first_ref, back_weight_ref, True)

    def fill_line():
        for copy in back_copies:
            copy.wait()
        back_picked = pick_messages(position, back_into_ref)
        build_patch(delta_ref[...].astype(F32), back_picked, code, back_level_ref, (back_patch_ref,))
        grad = convolve(rows_ref[:, WIDE:].astype(F32), back_patch_ref, back_weight_ref)
        out_ref[...] = (grad * mask).T[:C].astype(BF)

    all_sum(fill_plane, fill_line, data_ref, sum_ref, *reduce_refs)


def whole(scale, position, count, x, g, codes, first, second):
    sems = lambda n: pltpu.SemaphoreType.DMA((n,))
    taps = 9 * WIDE
    anywhere = pl.BlockSpec(memory_space=pl.ANY)
    return pl.pallas_call(
        functools.partial(whole_kernel, scale),
        out_shape=(jax.ShapeDtypeStruct((C, 512), BF), jax.ShapeDtypeStruct((ROWS, WIDE), BF)),
        in_specs=[SMEM, SMEM] + [anywhere] * 5,
        out_specs=(VMEM, anywhere),
        scratch_shapes=[
            pltpu.VMEM((C, 512), BF), pltpu.VMEM((C, 512), BF), pltpu.VMEM((1, 64), jnp.int32),
            pltpu.VMEM((27, C, C), BF), pltpu.VMEM((27, C, C), BF), sems(5),
            pltpu.VMEM((2, 512, WIDE), F32), pltpu.VMEM((512, 2 * WIDE), BF),
            pltpu.VMEM((MSG, 2 * WIDE), BF), pltpu.VMEM((MSG, 2 * WIDE), BF),
            pltpu.VMEM((MSG, WIDE), BF), pltpu.VMEM((MSG, WIDE), BF),
            pltpu.VMEM((3, taps, WIDE), BF), pltpu.VMEM((3, taps, WIDE), BF), pltpu.VMEM((3, taps, WIDE), BF),
            pltpu.VMEM((800, 2 * WIDE), F32), pltpu.VMEM((640, taps), BF), pltpu.VMEM((640, taps), BF),
            pltpu.VMEM((800, WIDE), F32), pltpu.VMEM((640, taps), BF),
            pltpu.VMEM((2, C, taps), F32), pltpu.VMEM((ROWS, WIDE), F32), pltpu.VMEM((512, WIDE), BF),
            sems(17), sems(17), sems(17), sems(17),
            pltpu.VMEM((ROWS, WIDE), BF),
            pltpu.VMEM((HALF, WIDE), BF), pltpu.VMEM((HALF, WIDE), BF),
            pltpu.VMEM((HALF, WIDE), F32), pltpu.VMEM((HALF, WIDE), BF),
            pltpu.VMEM((16, PART, WIDE), BF), pltpu.VMEM((PART, WIDE), F32),
            pltpu.VMEM((4, CELL, WIDE), F32), pltpu.VMEM((4, CELL, WIDE), F32),
            pltpu.VMEM((PART, WIDE), BF),
            sems(3), sems(3), sems(16), sems(16), sems(4), sems(4), sems(4), sems(4), sems(4), sems(4),
            sems(16), sems(16), sems(16), sems(16), sems(2),
        ],
        compiler_params=pltpu.CompilerParams(
            collective_id=1, has_side_effects=True, vmem_limit_bytes=60 * 2 ** 20),
        name="whole",
    )(position, count, x, g, codes, first, second)


def finish_kernel(grad_ref, first_sum_ref, second_sum_ref, out_ref, first_ref, second_ref):
    out_ref[...] = grad_ref[...]

    def load_first(tile):
        return first_sum_ref[0, pl.ds(tile * C, C), :].astype(F32)

    def load_second(tile):
        return second_sum_ref[0, pl.ds(tile * C, C), :].astype(F32)

    def store_first(tap, value):
        first_ref[tap] = value.T[:C]

    def store_second(tap, value):
        second_ref[8 - tap] = value[:, :C]

    unpack_grads(load_first, store_first)
    unpack_grads(load_second, store_second)


def finish(grad, summed):
    halves = summed.reshape(2, HALF, WIDE)
    return pl.pallas_call(
        finish_kernel,
        grid=(3,),
        out_shape=(
            jax.ShapeDtypeStruct((C, 512), BF),
            jax.ShapeDtypeStruct((27, C, C), F32), jax.ShapeDtypeStruct((27, C, C), F32)),
        in_specs=[
            pl.BlockSpec((C, 512), lambda i: (0, 0)),
            pl.BlockSpec((1, STRIP, WIDE), lambda i: (0, i, 0)),
            pl.BlockSpec((1, STRIP, WIDE), lambda i: (1, 2 - i, 0))],
        out_specs=(
            pl.BlockSpec((C, 512), lambda i: (0, 0)),
            pl.BlockSpec((9, C, C), lambda i: (i, 0, 0)),
            pl.BlockSpec((9, C, C), lambda i: (i, 0, 0))),
        compiler_params=pltpu.CompilerParams(vmem_limit_bytes=60 * 2 ** 20),
        name="finish",
    )(grad, halves, halves)


def shards(features, cotangent, first_weight, second_weight, slot_position, brick_count, column_code):
    devices = lax.axis_size("gx") * lax.axis_size("gy") * lax.axis_size("gz")
    scale = float(devices ** -0.5 / 8.0)
    grad, summed = whole(
        scale, slot_position.reshape(1), brick_count.reshape(1), features.reshape(C, 512),
        cotangent.reshape(C, 512), column_code.reshape(1, 64), first_weight, second_weight)
    grad_input, first_grad, second_grad = finish(grad, summed)
    return grad_input.reshape(1, 1, 1, 1, C, 512), first_grad, second_grad


def solution(mesh):
    placed = (
        P("gx", "gy", "gz", None, None, None),
        P("gx", "gy", "gz", None, None, None),
        P(),
        P(),
        P("gx", "gy", "gz", None),
        P("gx", "gy", "gz"),
        P("gx", "gy", "gz", None, None),
    )
    return jax.shard_map(
        shards,
        mesh=mesh,
        in_specs=placed,
        out_specs=(P("gx", "gy", "gz", None, None, None), P(), P()),
        check_vma=False,
    )
```

time: 77.6 us -> 71.5 us (0.921)
  Pallas kernels: 73.3 us -> 69.3 us
  local copies, waits for them, and re-layouts: 2.11 us -> 0 us
    pallas_call x1, Pallas kernels: 71.3 us -> 65.4 us  [whole(): pl.pallas_call(functools.partial(whole_kernel, scale), out_shape=(jax.Sha...]
    unnamed x4 -> x0, local copies, waits for them, and re-layouts: 2.11 us -> none
    pallas_call x1, Pallas kernels: 2.01 us -> 3.97 us  [finish(): pl.pallas_call(finish_kernel, grid=(3,), out_shape=(jax.ShapeDtypeStruct(...]
where the time goes in v4:
time: 71.5 us; the launch traced here: 71.3 us
  Pallas kernels  69.3 us (97%)
  between operations  1.93 us (3%)
    pallas_call x1, Pallas kernels, whole(): pl.pallas_call(functools.partial(whole_kernel, scale), out_shape=(jax.Sha...  65.4 us
    pallas_call x1, Pallas kernels, finish(): pl.pallas_call(finish_kernel, grid=(3,), out_shape=(jax.ShapeDtypeStruct(...  3.97 us

profile of v4, /device:TPU:1, one launch (start us, length us, event | category | flops | bytes accessed | tf_op | source)
XLA Modules:
  0.0 71.3 jit_solution(12495471850489176319)
XLA Ops:
  1.9 65.4 %whole.1 = (bf16[96,512]{1,0:T(8,128)(2,1)}, bf16[4096,128]{1,0:T(8,128)(2,1)}) custom-call(s32[1]{0:T(128)} %bitcast.7.position_ref, s32[1]{0:T(128)} %bitcast.8.count_ref, bf16[96,512]{1,0:T(8,128)(2,1)} %bitcast.11, bf16[96,512]{1,0:T(8,128)(2,1)} %bitcast.12, s32[1,64]{1,0:T(1,128)} %bitcast.13, bf16[27,96,96]{2,1,0:T(8,128)(2,1)} %first_hbm.1, ...), custom_call_target="tpu_custom_call" | custom-call | tf_op jit(solution)/shard_map/whole/pallas_call | solution.py:536
  67.3 4.0 %finish.1 = (bf16[96,512]{1,0:T(8,128)(2,1)}, f32[27,96,96]{2,1,0:T(8,128)}, f32[27,96,96]{2,1,0:T(8,128)}) custom-call(bf16[96,512]{1,0:T(8,128)(2,1)} %get-tuple-element.8.grad_ref, bf16[2,2048,128]{2,1,0:T(8,128)(2,1)} %bitcast.9, bf16[2,2048,128]{2,1,0:T(8,128)(2,1)} %bitcast.10), custom_call_target="tpu_custom_call" | custom-call | tf_op jit(solution)/shard_map/finish/pallas_call | solution.py:588

commit v5 on v4

--- a/solution.py
+++ b/solution.py
@@ -20,20 +20,20 @@
 def message_plan():
     plan = []
     for ix in (0, 1):
-        plan.append((ix, 64, (1 - 2 * ix, 0, 0)))
+        for iy in (0, 1):
+            plan.append((13 + 2 * ix + iy, 16, (1 - 2 * ix, 1 - 2 * iy, 1)))
     for iy in (0, 1):
-        plan.append((2 + iy, 64, (0, 1 - 2 * iy, 0)))
-    plan.append((4, 64, (0, 0, 1)))
+        plan.append((11 + iy, 16, (0, 1 - 2 * iy, 1)))
+    for ix in (0, 1):
+        plan.append((9 + ix, 16, (1 - 2 * ix, 0, 1)))
     for ix in (0, 1):
         for iy in (0, 1):
             plan.append((5 + 2 * ix + iy, 16, (1 - 2 * ix, 1 - 2 * iy, 0)))
+    plan.append((4, 64, (0, 0, 1)))
+    for iy in (0, 1):
+        plan.append((2 + iy, 64, (0, 1 - 2 * iy, 0)))
     for ix in (0, 1):
-        plan.append((9 + ix, 16, (1 - 2 * ix, 0, 1)))
-    for iy in (0, 1):
-        plan.append((11 + iy, 16, (0, 1 - 2 * iy, 1)))
-    for ix in (0, 1):
-        for iy in (0, 1):
-            plan.append((13 + 2 * ix + iy, 16, (1 - 2 * ix, 1 - 2 * iy, 1)))
+        plan.append((ix, 64, (1 - 2 * ix, 0, 0)))
     return plan
 
 
@@ -252,6 +252,14 @@
 CELL = PART // 4
 
 
+def ring(distance, size):
+    return min(distance, size - distance)
+
+
+PLANE = sorted(range(1, 16), key=lambda t: -ring(t // 4, 4) - ring(t % 4, 4))
+LINE = sorted(range(1, 16), key=lambda t: -ring(t, 16))
+
+
 def places():
     u = lax.axis_index("gx")
     w = lax.axis_index("gy")
@@ -270,27 +278,18 @@
         r = (u % 4 + t) % 4
         return r, (u // 4 * 4 + r, w, q)
 
-    def far_peer(t):
-        g = (u // 4 + t) % 4
-        return g, (g * 4 + u % 4, w, q)
-
-    return core, x, y, mate, plane_peer, near_peer, far_peer
+    def line_peer(t):
+        return (u + t) % 16, w, q
+
+    return core, x, y, mate, plane_peer, near_peer, line_peer
 
 
 def greet_sharers(barrier):
-    core, x, y, mate, plane_peer, near_peer, far_peer = places()
-
-    def greet(t, carry):
+    core, x, y, mate, plane_peer, near_peer, line_peer = places()
+    for t in LINE:
+        pl.semaphore_signal(barrier, inc=1, device_id=line_peer(t), device_id_type=MESH)
+    for t in PLANE:
         pl.semaphore_signal(barrier, inc=1, device_id=plane_peer(t)[1], device_id_type=MESH)
-        return carry
-
-    def greet_line(t, carry):
-        pl.semaphore_signal(barrier, inc=1, device_id=far_peer(t)[1], device_id_type=MESH)
-        pl.semaphore_signal(barrier, inc=1, device_id=near_peer(t)[1], device_id_type=MESH)
-        return carry
-
-    lax.fori_loop(1, 4, greet_line, 0)
-    lax.fori_loop(1, 16, greet, 0)
     pl.semaphore_signal(barrier, inc=1, device_id=mate, device_id_type=MESH)
 
 
@@ -308,25 +307,26 @@
 def start_swap(strip, data_ref, half_out, half_in, swap_send, swap_recv):
     core = places()[0]
     theirs = pl.multiple_of((1 - core) * HALF + strip * STRIP, 16)
-    half_out[pl.ds(strip * STRIP, STRIP), :] = data_ref[pl.ds(theirs, STRIP), :].astype(BF)
+    half_out[pl.ds(strip * STRIP, STRIP), :] = data_ref[pl.ds(theirs, STRIP), :]
     swap_copy(strip, half_out, half_in, swap_send, swap_recv).start()
 
 
 def all_sum(fill_plane, fill_line, data_ref, sum_ref, gathered, half_out, half_in, total, plane_out, plane_in,
-            near_src, near_in, far_all, own_part, swap_send, swap_recv, plane_send, plane_recv,
-            near_send, near_recv, far_send, far_recv, near_send2, near_recv2, plane_send2, plane_recv2,
+            near_src, near_in, line_in, own_part, swap_send, swap_recv, plane_send, plane_recv,
+            near_send, near_recv, line_send, line_recv, plane_send2, plane_recv2,
             join_send, join_recv, out_sem):
-    core, x, y, mate, plane_peer, near_peer, far_peer = places()
+    core, x, y, mate, plane_peer, near_peer, line_peer = places()
     u = lax.axis_index("gx")
     chip = x * 4 + y
     own = pl.multiple_of(core * HALF, HALF)
     other = pl.multiple_of((1 - core) * HALF, HALF)
 
+    swaps = [swap_copy(strip, half_out, half_in, swap_send, swap_recv) for strip in range(3)]
     for strip in range(3):
         rows = pl.ds(strip * STRIP, STRIP)
-        swap_copy(strip, half_out, half_in, swap_send, swap_recv).wait()
+        swaps[strip].wait_recv()
         mine = data_ref[pl.ds(pl.multiple_of(own + strip * STRIP, 16), STRIP), :]
-        both = mine + half_in[rows, :].astype(F32)
+        both = mine + half_in[rows, :]
         total[rows, :] = both
         plane_out[rows, :] = both.astype(BF)
     rest = pl.ds(3 * STRIP, HALF - 3 * STRIP)
@@ -338,115 +338,87 @@
         rows = pl.ds(pl.multiple_of(there * PART, PART), PART)
         return remote(plane_out.at[rows, :], plane_in.at[t], plane_send, plane_recv, t, device)
 
-    def plane_start(t, carry):
-        plane_copy(t).start()
-        return carry
-
-    lax.fori_loop(1, 16, plane_start, 0)
+    plane_copies = [plane_copy(t) for t in PLANE]
+    for copy in plane_copies:
+        copy.start()
     fill_plane()
-
-    def plane_add(t, acc):
-        plane_copy(t).wait_recv()
-        return acc + plane_in[t].astype(F32)
-
     part = pl.multiple_of(chip * PART, PART)
-    near_src[...] = lax.fori_loop(1, 16, plane_add, total[pl.ds(part, PART), :])
+    part_sum = total[pl.ds(part, PART), :]
+    for t, copy in zip(reversed(PLANE), reversed(plane_copies)):
+        copy.wait_recv()
+        part_sum = part_sum + plane_in[t].astype(F32)
+    near_src[...] = part_sum
 
     def near_copy(t):
         there, device = near_peer(t)
         rows = pl.ds(pl.multiple_of(there * CELL, CELL), CELL)
         return remote(near_src.at[rows, :], near_in.at[t], near_send, near_recv, t, device)
 
-    for t in (1, 2, 3):
-        near_copy(t).start()
-    cell = pl.multiple_of(u % 4 * CELL, CELL)
-    cell_sum = near_src[pl.ds(cell, CELL), :]
-    for t in (1, 2, 3):
-        near_copy(t).wait_recv()
+    near_copies = [near_copy(t) for t in (1, 2, 3)]
+    for copy in near_copies:
+        copy.start()
+    cell_sum = near_src[pl.ds(pl.multiple_of(u % 4 * CELL, CELL), CELL), :]
+    for t, copy in zip((1, 2, 3), near_copies):
+        copy.wait_recv()
         cell_sum = cell_sum + near_in[t]
 
-    group = u // 4
-    far_all[group] = cell_sum
-
-    def far_copy(t, slot):
-        return remote(far_all.at[group], far_all.at[slot], far_send, far_recv, t, far_peer(t)[1])
-
-    for t in (1, 2, 3):
-        far_copy(t, group).start()
+    line_in[u] = cell_sum.astype(BF)
+
+    def line_copy(t, slot):
+        return remote(line_in.at[u], line_in.at[slot], line_send, line_recv, t, line_peer(t))
+
+    line_copies = [line_copy(t, u) for t in LINE]
+    for copy in line_copies:
+        copy.start()
     fill_line()
-    for t in (1, 2, 3):
-        far_copy(t, (group - t + 4) % 4).wait_recv()
-    final = (far_all[0] + far_all[1]) + (far_all[2] + far_all[3])
-    own_part[pl.ds(cell, CELL), :] = final.astype(BF)
-
-    def near_back(t, owner):
-        rows = pl.ds(pl.multiple_of(owner * CELL, CELL), CELL)
-        return remote(own_part.at[rows, :], own_part.at[rows, :], near_send2, near_recv2, t, near_peer(t)[1])
-
-    for t in (1, 2, 3):
-        near_back(t, u % 4).start()
-    for t in (1, 2, 3):
-        near_back(t, (u % 4 - t + 4) % 4).wait_recv()
+    for t in reversed(LINE):
+        line_copy(t, (u - t + 16) % 16).wait_recv()
+    for r in range(4):
+        cells = [line_in[4 * group + r].astype(F32) for group in range(4)]
+        own_part[pl.ds(r * CELL, CELL), :] = ((cells[0] + cells[1]) + (cells[2] + cells[3])).astype(BF)
 
     place = pl.multiple_of(own + part, PART)
 
     def plane_back(t):
         return remote(own_part, gathered.at[pl.ds(place, PART), :], plane_send2, plane_recv2, t, plane_peer(t)[1])
-
-    def plane_back_start(t, carry):
-        plane_back(t).start()
-        return carry
 
     def source_rows(t, base):
         px = (x - t // 4 + 4) % 4
         py = (y - t % 4 + 4) % 4
         return pl.ds(pl.multiple_of(base + (px * 4 + py) * PART, PART), PART)
 
+    def plane_arrive(t):
+        return remote(own_part, gathered.at[source_rows(t, own), :], plane_send2, plane_recv2, t, plane_peer(t)[1])
+
     def join_copy(t, base):
         rows = source_rows(t, base)
         return remote(gathered.at[rows, :], gathered.at[rows, :], join_send, join_recv, t, mate)
 
-    lax.fori_loop(1, 16, plane_back_start, 0)
+    backs = [plane_back(t) for t in PLANE]
+    for copy in backs:
+        copy.start()
     gathered[pl.ds(place, PART), :] = own_part[...]
-    join_copy(0, own).start()
-
-    def plane_back_wait(t, carry):
-        remote(own_part, gathered.at[source_rows(t, own), :], plane_send2, plane_recv2, t,
-               plane_peer(t)[1]).wait_recv()
-        join_copy(t, own).start()
-        return carry
-
-    lax.fori_loop(1, 16, plane_back_wait, 0)
+    joins = [join_copy(0, own)]
+    joins[0].start()
+    for t in reversed(PLANE):
+        plane_arrive(t).wait_recv()
+        joins.append(join_copy(t, own))
+        joins[-1].start()
     first_out = pltpu.make_async_copy(
         gathered.at[pl.ds(own, HALF), :], sum_ref.at[pl.ds(own, HALF), :], out_sem.at[0])
     first_out.start()
-
-    def join_wait(t, carry):
+    for t in [0, *reversed(PLANE)]:
         join_copy(t, other).wait_recv()
-        return carry
-
-    lax.fori_loop(0, 16, join_wait, 0)
     second_out = pltpu.make_async_copy(
         gathered.at[pl.ds(other, HALF), :], sum_ref.at[pl.ds(other, HALF), :], out_sem.at[1])
     second_out.start()
-
-    def drain(t, carry):
-        plane_copy(t).wait_send()
-        plane_back(t).wait_send()
-        join_copy(t, own).wait_send()
-        return carry
-
-    lax.fori_loop(1, 16, drain, 0)
-    join_copy(0, own).wait_send()
-    for t in (1, 2, 3):
-        near_copy(t).wait_send()
-        far_copy(t, group).wait_send()
-        near_back(t, u % 4).wait_send()
+    for copy in [*swaps, *plane_copies, *near_copies, *line_copies, *backs, *joins]:
+        copy.wait_send()
     first_out.wait()
     second_out.wait()
 
 
-SHARERS = 1 + 15 + 3 + 3
+SHARERS = 1 + 15 + 15
 
 
 def whole_kernel(scale, position_ref, count_ref, x_hbm, g_hbm, code_hbm, first_hbm, second_hbm,
@@ -495,10 +467,7 @@
     delta = (back * sigma * (1.0 + pre * (1.0 - sigma)) * mask).astype(BF)
     delta_ref[...] = delta
     wide_ref[0] = delta.astype(F32)
-    pack_messages(wide_ref.at[pl.ds(0, 1)], back_msg_ref, q)
     back_copies = halo_copies(back_msg_ref, back_into_ref, back_send_sem, back_recv_sem)
-    for copy in back_copies:
-        copy.start()
 
     turned = (delta.astype(F32).T[:C].astype(BF), hidden.T[:C].astype(BF))
     for dx in (0, 1, 2):
@@ -516,6 +485,9 @@
         start_swap(dx, data_ref, *reduce_refs[1:3], *reduce_refs[10:12])
 
     def fill_plane():
+        pack_messages(wide_ref.at[pl.ds(0, 1)], back_msg_ref, q)
+        for copy in back_copies:
+            copy.start()
         lay_weights(first_ref, back_weight_ref, True)
 
     def fill_line():
@@ -550,12 +522,12 @@
             pltpu.VMEM((2, C, taps), F32), pltpu.VMEM((ROWS, WIDE), F32), pltpu.VMEM((512, WIDE), BF),
             sems(17), sems(17), sems(17), sems(17),
             pltpu.VMEM((ROWS, WIDE), BF),
-            pltpu.VMEM((HALF, WIDE), BF), pltpu.VMEM((HALF, WIDE), BF),
+            pltpu.VMEM((HALF, WIDE), F32), pltpu.VMEM((HALF, WIDE), F32),
             pltpu.VMEM((HALF, WIDE), F32), pltpu.VMEM((HALF, WIDE), BF),
             pltpu.VMEM((16, PART, WIDE), BF), pltpu.VMEM((PART, WIDE), F32),
-            pltpu.VMEM((4, CELL, WIDE), F32), pltpu.VMEM((4, CELL, WIDE), F32),
+            pltpu.VMEM((4, CELL, WIDE), F32), pltpu.VMEM((16, CELL, WIDE), BF),
             pltpu.VMEM((PART, WIDE), BF),
-            sems(3), sems(3), sems(16), sems(16), sems(4), sems(4), sems(4), sems(4), sems(4), sems(4),
+            sems(3), sems(3), sems(16), sems(16), sems(4), sems(4), sems(16), sems(16),
             sems(16), sems(16), sems(16), sems(16), sems(2),
         ],
         compiler_params=pltpu.CompilerParams(
@@ -564,44 +536,53 @@
     )(position, count, x, g, codes, first, second)
 
 
-def finish_kernel(grad_ref, first_sum_ref, second_sum_ref, out_ref, first_ref, second_ref):
-    out_ref[...] = grad_ref[...]
-
-    def load_first(tile):
-        return first_sum_ref[0, pl.ds(tile * C, C), :].astype(F32)
-
-    def load_second(tile):
-        return second_sum_ref[0, pl.ds(tile * C, C), :].astype(F32)
-
-    def store_first(tap, value):
-        first_ref[tap] = value.T[:C]
-
-    def store_second(tap, value):
-        second_ref[8 - tap] = value[:, :C]
-
-    unpack_grads(load_first, store_first)
-    unpack_grads(load_second, store_second)
+def finish_kernel(grad_hbm, sum_hbm, out_hbm, first_hbm, second_hbm, sum_ref, first_ref, second_ref, in_sem, out_sem):
+    keep = pltpu.make_async_copy(grad_hbm, out_hbm, out_sem.at[6])
+    keep.start()
+    strips = [(half, dx) for dx in (0, 1, 2) for half in (0, 1)]
+    loads = []
+    for i, (half, dx) in enumerate(strips):
+        rows = pl.ds(half * HALF + dx * STRIP, STRIP)
+        loads.append(pltpu.make_async_copy(sum_hbm.at[rows, :], sum_ref.at[i], in_sem.at[i]))
+        loads[-1].start()
+    stores = []
+    for i, (half, dx) in enumerate(strips):
+        loads[i].wait()
+
+        def load(tile):
+            return sum_ref[i, pl.ds(tile * C, C), :].astype(F32)
+
+        def store(tap, value):
+            if half == 0:
+                first_ref[9 * dx + tap] = value.T[:C]
+            else:
+                second_ref[26 - 9 * dx - tap] = value[:, :C]
+
+        unpack_grads(load, store)
+        done = (first_ref, first_hbm, 9 * dx) if half == 0 else (second_ref, second_hbm, 18 - 9 * dx)
+        taps = pl.ds(done[2], 9)
+        stores.append(pltpu.make_async_copy(done[0].at[taps], done[1].at[taps], out_sem.at[i]))
+        stores[-1].start()
+    for copy in stores:
+        copy.wait()
+    keep.wait()
 
 
 def finish(grad, summed):
-    halves = summed.reshape(2, HALF, WIDE)
+    anywhere = pl.BlockSpec(memory_space=pl.ANY)
     return pl.pallas_call(
         finish_kernel,
-        grid=(3,),
         out_shape=(
             jax.ShapeDtypeStruct((C, 512), BF),
             jax.ShapeDtypeStruct((27, C, C), F32), jax.ShapeDtypeStruct((27, C, C), F32)),
-        in_specs=[
-            pl.BlockSpec((C, 512), lambda i: (0, 0)),
-            pl.BlockSpec((1, STRIP, WIDE), lambda i: (0, i, 0)),
-            pl.BlockSpec((1, STRIP, WIDE), lambda i: (1, 2 - i, 0))],
-        out_specs=(
-            pl.BlockSpec((C, 512), lambda i: (0, 0)),
-            pl.BlockSpec((9, C, C), lambda i: (i, 0, 0)),
-            pl.BlockSpec((9, C, C), lambda i: (i, 0, 0))),
+        in_specs=[anywhere, anywhere],
+        out_specs=(anywhere,) * 3,
+        scratch_shapes=[
+            pltpu.VMEM((6, STRIP, WIDE), BF), pltpu.VMEM((27, C, C), F32), pltpu.VMEM((27, C, C), F32),
+            pltpu.SemaphoreType.DMA((6,)), pltpu.SemaphoreType.DMA((7,))],
         compiler_params=pltpu.CompilerParams(vmem_limit_bytes=60 * 2 ** 20),
         name="finish",
-    )(grad, halves, halves)
+    )(grad, summed)
 
 
 def shards(features, cotangent, first_weight, second_weight, slot_position, brick_count, column_code):

time: 71.5 us -> 67.9 us (0.950)
  Pallas kernels: 69.3 us -> 65.8 us
    pallas_call x1, Pallas kernels: 65.4 us -> 61.6 us  [whole(): pl.pallas_call(functools.partial(whole_kernel, scale), out_shape=(jax.Sha...]
where the time goes in v5:
time: 67.9 us; the launch traced here: 67.7 us
  Pallas kernels  65.8 us (97%)
  between operations  1.93 us (3%)
    pallas_call x1, Pallas kernels, whole(): pl.pallas_call(functools.partial(whole_kernel, scale), out_shape=(jax.Sha...  61.6 us
    pallas_call x1, Pallas kernels, finish(): pl.pallas_call(finish_kernel, out_shape=(jax.ShapeDtypeStruct((C, 512), B...  4.2 us

profile of v5, /device:TPU:1, one launch (start us, length us, event | category | flops | bytes accessed | tf_op | source)
XLA Modules:
  0.0 67.7 jit_solution(14275390103124431662)
XLA Ops:
  1.9 61.6 %whole.1 = (bf16[96,512]{1,0:T(8,128)(2,1)}, bf16[4096,128]{1,0:T(8,128)(2,1)}) custom-call(s32[1]{0:T(128)} %bitcast.6.position_ref, s32[1]{0:T(128)} %bitcast.7.count_ref, bf16[96,512]{1,0:T(8,128)(2,1)} %bitcast.8, bf16[96,512]{1,0:T(8,128)(2,1)} %bitcast.9, s32[1,64]{1,0:T(1,128)} %bitcast.10, bf16[27,96,96]{2,1,0:T(8,128)(2,1)} %first_hbm.1, ...), custom_call_target="tpu_custom_call" | custom-call | tf_op jit(solution)/shard_map/whole/pallas_call | solution.py:508
  63.5 4.2 %finish.1 = (bf16[96,512]{1,0:T(8,128)(2,1)}, f32[27,96,96]{2,1,0:T(8,128)}, f32[27,96,96]{2,1,0:T(8,128)}) custom-call(bf16[96,512]{1,0:T(8,128)(2,1)} %get-tuple-element.8.grad_hbm, bf16[4096,128]{1,0:T(8,128)(2,1)} %get-tuple-element.9.sum_hbm), custom_call_target="tpu_custom_call" | custom-call | tf_op jit(solution)/shard_map/finish/pallas_call | solution.py:573

commit v6 on v5

--- a/solution.py
+++ b/solution.py
@@ -248,7 +248,10 @@
 ROWS = 4096
 HALF = ROWS // 2
 STRIP = 7 * C
-PART = HALF // 16
+SIDE = HALF // 2
+SLAB = SIDE // 4
+PIECE = SLAB // 4
+PART = 2 * PIECE
 CELL = PART // 4
 
 
@@ -256,7 +259,7 @@
     return min(distance, size - distance)
 
 
-PLANE = sorted(range(1, 16), key=lambda t: -ring(t // 4, 4) - ring(t % 4, 4))
+ROW = (2, 1, 3)
 LINE = sorted(range(1, 16), key=lambda t: -ring(t, 16))
 
 
@@ -269,10 +272,14 @@
     x = q * 2 + w // 8
     mate = (u, w + 1 - 2 * core, q)
 
-    def plane_peer(t):
-        px = (x + t // 4) % 4
-        py = (y + t % 4) % 4
-        return px * 4 + py, (u, ((px % 2) * 4 + py) * 2 + core, px // 2)
+    def at(px, py):
+        return u, ((px % 2) * 4 + py) * 2 + core, px // 2
+
+    def x_peer(t):
+        return (x + t) % 4, at((x + t) % 4, y)
+
+    def y_peer(t):
+        return (y + t) % 4, at(x, (y + t) % 4)
 
     def near_peer(t):
         r = (u % 4 + t) % 4
@@ -281,15 +288,16 @@
     def line_peer(t):
         return (u + t) % 16, w, q
 
-    return core, x, y, mate, plane_peer, near_peer, line_peer
+    return core, x, y, mate, x_peer, y_peer, near_peer, line_peer
 
 
 def greet_sharers(barrier):
-    core, x, y, mate, plane_peer, near_peer, line_peer = places()
+    core, x, y, mate, x_peer, y_peer, near_peer, line_peer = places()
     for t in LINE:
         pl.semaphore_signal(barrier, inc=1, device_id=line_peer(t), device_id_type=MESH)
-    for t in PLANE:
-        pl.semaphore_signal(barrier, inc=1, device_id=plane_peer(t)[1], device_id_type=MESH)
+    for t in ROW:
+        pl.semaphore_signal(barrier, inc=1, device_id=x_peer(t)[1], device_id_type=MESH)
+        pl.semaphore_signal(barrier, inc=1, device_id=y_peer(t)[1], device_id_type=MESH)
     pl.semaphore_signal(barrier, inc=1, device_id=mate, device_id_type=MESH)
 
 
@@ -311,13 +319,16 @@
     swap_copy(strip, half_out, half_in, swap_send, swap_recv).start()
 
 
-def all_sum(fill_plane, fill_line, data_ref, sum_ref, gathered, half_out, half_in, total, plane_out, plane_in,
-            near_src, near_in, line_in, own_part, swap_send, swap_recv, plane_send, plane_recv,
-            near_send, near_recv, line_send, line_recv, plane_send2, plane_recv2,
-            join_send, join_recv, out_sem):
-    core, x, y, mate, plane_peer, near_peer, line_peer = places()
+def block(start, size):
+    return pl.ds(pl.multiple_of(start, 16), size)
+
+
+def all_sum(fill_plane, fill_line, data_ref, sum_ref, gathered, half_out, half_in, total, plane_out, slab_in,
+            slab_sum, piece_in, near_src, near_in, line_in, own_part, swap_send, swap_recv, slab_send, slab_recv,
+            piece_send, piece_recv, near_send, near_recv, line_send, line_recv, piece_send2, piece_recv2,
+            slab_send2, slab_recv2, join_send, join_recv):
+    core, x, y, mate, x_peer, y_peer, near_peer, line_peer = places()
     u = lax.axis_index("gx")
-    chip = x * 4 + y
     own = pl.multiple_of(core * HALF, HALF)
     other = pl.multiple_of((1 - core) * HALF, HALF)
 
@@ -333,21 +344,35 @@
     total[rest, :] = jnp.zeros((HALF - 3 * STRIP, WIDE), F32)
     plane_out[rest, :] = jnp.zeros((HALF - 3 * STRIP, WIDE), BF)
 
-    def plane_copy(t):
-        there, device = plane_peer(t)
-        rows = pl.ds(pl.multiple_of(there * PART, PART), PART)
-        return remote(plane_out.at[rows, :], plane_in.at[t], plane_send, plane_recv, t, device)
-
-    plane_copies = [plane_copy(t) for t in PLANE]
-    for copy in plane_copies:
-        copy.start()
+    ways = ((y, y_peer, x, x_peer), (x, x_peer, y, y_peer))
+    slab_copies, piece_copies = [], []
+    for t in ROW:
+        for side, (_, first_peer, _, _) in enumerate(ways):
+            there, device = first_peer(t)
+            slab_copies.append((side, t, remote(
+                plane_out.at[block(side * SIDE + there * SLAB, SLAB), :], slab_in.at[side, t],
+                slab_send, slab_recv, (side, t), device)))
+            slab_copies[-1][2].start()
     fill_plane()
-    part = pl.multiple_of(chip * PART, PART)
-    part_sum = total[pl.ds(part, PART), :]
-    for t, copy in zip(reversed(PLANE), reversed(plane_copies)):
+    slab_sums = [total[block(side * SIDE + ways[side][0] * SLAB, SLAB), :] for side in (0, 1)]
+    for side, t, copy in reversed(slab_copies):
         copy.wait_recv()
-        part_sum = part_sum + plane_in[t].astype(F32)
-    near_src[...] = part_sum
+        slab_sums[side] = slab_sums[side] + slab_in[side, t].astype(F32)
+    for side in (0, 1):
+        slab_sum[side] = slab_sums[side]
+    for t in ROW:
+        for side, (_, _, _, second_peer) in enumerate(ways):
+            there, device = second_peer(t)
+            piece_copies.append((side, t, remote(
+                slab_sum.at[side, block(there * PIECE, PIECE), :], piece_in.at[side, t],
+                piece_send, piece_recv, (side, t), device)))
+            piece_copies[-1][2].start()
+    pieces = [slab_sum[side, block(ways[side][2] * PIECE, PIECE), :] for side in (0, 1)]
+    for side, t, copy in reversed(piece_copies):
+        copy.wait_recv()
+        pieces[side] = pieces[side] + piece_in[side, t]
+    for side in (0, 1):
+        near_src[pl.ds(side * PIECE, PIECE), :] = pieces[side]
 
     def near_copy(t):
         there, device = near_peer(t)
@@ -377,48 +402,57 @@
         cells = [line_in[4 * group + r].astype(F32) for group in range(4)]
         own_part[pl.ds(r * CELL, CELL), :] = ((cells[0] + cells[1]) + (cells[2] + cells[3])).astype(BF)
 
-    place = pl.multiple_of(own + part, PART)
-
-    def plane_back(t):
-        return remote(own_part, gathered.at[pl.ds(place, PART), :], plane_send2, plane_recv2, t, plane_peer(t)[1])
-
-    def source_rows(t, base):
-        px = (x - t // 4 + 4) % 4
-        py = (y - t % 4 + 4) % 4
-        return pl.ds(pl.multiple_of(base + (px * 4 + py) * PART, PART), PART)
-
-    def plane_arrive(t):
-        return remote(own_part, gathered.at[source_rows(t, own), :], plane_send2, plane_recv2, t, plane_peer(t)[1])
-
-    def join_copy(t, base):
-        rows = source_rows(t, base)
-        return remote(gathered.at[rows, :], gathered.at[rows, :], join_send, join_recv, t, mate)
-
-    backs = [plane_back(t) for t in PLANE]
-    for copy in backs:
-        copy.start()
-    gathered[pl.ds(place, PART), :] = own_part[...]
-    joins = [join_copy(0, own)]
-    joins[0].start()
-    for t in reversed(PLANE):
-        plane_arrive(t).wait_recv()
-        joins.append(join_copy(t, own))
+    def slab_rows(base, side, place):
+        return block(base + side * SIDE + place * SLAB, SLAB)
+
+    def piece_rows(side, place, inner):
+        return block(own + side * SIDE + place * SLAB + inner * PIECE, PIECE)
+
+    def join_copy(rows, index):
+        return remote(gathered.at[rows, :], gathered.at[rows, :], join_send, join_recv, index, mate)
+
+    backs, joins = [], []
+    for side, (place, _, inner, _) in enumerate(ways):
+        gathered[piece_rows(side, place, inner), :] = own_part[pl.ds(side * PIECE, PIECE), :]
+    for t in ROW:
+        for side, (place, _, inner, second_peer) in enumerate(ways):
+            rows = piece_rows(side, place, inner)
+            backs.append(remote(own_part.at[pl.ds(side * PIECE, PIECE), :], gathered.at[rows, :],
+                                piece_send2, piece_recv2, (side, t), second_peer(t)[1]))
+            backs[-1].start()
+    for t in reversed(ROW):
+        for side, (place, _, inner, second_peer) in enumerate(ways):
+            rows = piece_rows(side, place, (inner - t + 4) % 4)
+            remote(own_part.at[pl.ds(side * PIECE, PIECE), :], gathered.at[rows, :],
+                   piece_send2, piece_recv2, (side, t), second_peer(t)[1]).wait_recv()
+    for t in ROW:
+        for side, (place, first_peer, _, _) in enumerate(ways):
+            rows = slab_rows(own, side, place)
+            backs.append(remote(gathered.at[rows, :], gathered.at[rows, :],
+                                slab_send2, slab_recv2, (side, t), first_peer(t)[1]))
+            backs[-1].start()
+    for side in (0, 1):
+        joins.append(join_copy(slab_rows(own, side, ways[side][0]), (side, 0)))
         joins[-1].start()
-    first_out = pltpu.make_async_copy(
-        gathered.at[pl.ds(own, HALF), :], sum_ref.at[pl.ds(own, HALF), :], out_sem.at[0])
-    first_out.start()
-    for t in [0, *reversed(PLANE)]:
-        join_copy(t, other).wait_recv()
-    second_out = pltpu.make_async_copy(
-        gathered.at[pl.ds(other, HALF), :], sum_ref.at[pl.ds(other, HALF), :], out_sem.at[1])
-    second_out.start()
-    for copy in [*swaps, *plane_copies, *near_copies, *line_copies, *backs, *joins]:
+    for t in reversed(ROW):
+        for side, (place, first_peer, _, _) in enumerate(ways):
+            rows = slab_rows(own, side, (place - t + 4) % 4)
+            remote(gathered.at[rows, :], gathered.at[rows, :],
+                   slab_send2, slab_recv2, (side, t), first_peer(t)[1]).wait_recv()
+            joins.append(join_copy(rows, (side, t)))
+            joins[-1].start()
+    sum_ref[pl.ds(own, HALF), :] = gathered[pl.ds(own, HALF), :]
+    for t in (0, *reversed(ROW)):
+        for side in (0, 1):
+            rows = slab_rows(other, side, (ways[side][0] - t + 4) % 4)
+            join_copy(rows, (side, t)).wait_recv()
+            sum_ref[rows, :] = gathered[rows, :]
+    reduced = [copy for _, _, copy in slab_copies + piece_copies]
+    for copy in [*swaps, *reduced, *near_copies, *line_copies, *backs, *joins]:
         copy.wait_send()
-    first_out.wait()
-    second_out.wait()
-
-
-SHARERS = 1 + 15 + 15
+
+
+SHARERS = 1 + 6 + 15
 
 
 def whole_kernel(scale, position_ref, count_ref, x_hbm, g_hbm, code_hbm, first_hbm, second_hbm,
@@ -482,7 +516,7 @@
                 data_ref[pl.ds(half * HALF + dx * STRIP + tile * C, C), :] = value
 
             pack_grads(block, store)
-        start_swap(dx, data_ref, *reduce_refs[1:3], *reduce_refs[10:12])
+        start_swap(dx, data_ref, *reduce_refs[1:3], *reduce_refs[12:14])
 
     def fill_plane():
         pack_messages(wide_ref.at[pl.ds(0, 1)], back_msg_ref, q)
@@ -502,14 +536,14 @@
 
 
 def whole(scale, position, count, x, g, codes, first, second):
-    sems = lambda n: pltpu.SemaphoreType.DMA((n,))
+    sems = lambda *n: pltpu.SemaphoreType.DMA(n)
     taps = 9 * WIDE
     anywhere = pl.BlockSpec(memory_space=pl.ANY)
     return pl.pallas_call(
         functools.partial(whole_kernel, scale),
-        out_shape=(jax.ShapeDtypeStruct((C, 512), BF), jax.ShapeDtypeStruct((ROWS, WIDE), BF)),
+        out_shape=(pltpu.VMEM((C, 512), BF), pltpu.VMEM((ROWS, WIDE), BF)),
         in_specs=[SMEM, SMEM] + [anywhere] * 5,
-        out_specs=(VMEM, anywhere),
+        out_specs=(VMEM, VMEM),
         scratch_shapes=[
             pltpu.VMEM((C, 512), BF), pltpu.VMEM((C, 512), BF), pltpu.VMEM((1, 64), jnp.int32),
             pltpu.VMEM((27, C, C), BF), pltpu.VMEM((27, C, C), BF), sems(5),
@@ -524,48 +558,41 @@
             pltpu.VMEM((ROWS, WIDE), BF),
             pltpu.VMEM((HALF, WIDE), F32), pltpu.VMEM((HALF, WIDE), F32),
             pltpu.VMEM((HALF, WIDE), F32), pltpu.VMEM((HALF, WIDE), BF),
-            pltpu.VMEM((16, PART, WIDE), BF), pltpu.VMEM((PART, WIDE), F32),
+            pltpu.VMEM((2, 4, SLAB, WIDE), BF), pltpu.VMEM((2, SLAB, WIDE), F32),
+            pltpu.VMEM((2, 4, PIECE, WIDE), F32), pltpu.VMEM((PART, WIDE), F32),
             pltpu.VMEM((4, CELL, WIDE), F32), pltpu.VMEM((16, CELL, WIDE), BF),
             pltpu.VMEM((PART, WIDE), BF),
-            sems(3), sems(3), sems(16), sems(16), sems(4), sems(4), sems(16), sems(16),
-            sems(16), sems(16), sems(16), sems(16), sems(2),
+            sems(3), sems(3), sems(2, 4), sems(2, 4), sems(2, 4), sems(2, 4), sems(4), sems(4), sems(16), sems(16),
+            sems(2, 4), sems(2, 4), sems(2, 4), sems(2, 4), sems(2, 4), sems(2, 4),
         ],
         compiler_params=pltpu.CompilerParams(
-            collective_id=1, has_side_effects=True, vmem_limit_bytes=60 * 2 ** 20),
+            collective_id=1, has_side_effects=True, vmem_limit_bytes=48 * 2 ** 20),
         name="whole",
-    )(position, count, x, g, codes, first, second)
-
-
-def finish_kernel(grad_hbm, sum_hbm, out_hbm, first_hbm, second_hbm, sum_ref, first_ref, second_ref, in_sem, out_sem):
-    keep = pltpu.make_async_copy(grad_hbm, out_hbm, out_sem.at[6])
-    keep.start()
-    strips = [(half, dx) for dx in (0, 1, 2) for half in (0, 1)]
-    loads = []
-    for i, (half, dx) in enumerate(strips):
-        rows = pl.ds(half * HALF + dx * STRIP, STRIP)
-        loads.append(pltpu.make_async_copy(sum_hbm.at[rows, :], sum_ref.at[i], in_sem.at[i]))
-        loads[-1].start()
-    stores = []
-    for i, (half, dx) in enumerate(strips):
-        loads[i].wait()
-
-        def load(tile):
-            return sum_ref[i, pl.ds(tile * C, C), :].astype(F32)
-
-        def store(tap, value):
-            if half == 0:
-                first_ref[9 * dx + tap] = value.T[:C]
-            else:
-                second_ref[26 - 9 * dx - tap] = value[:, :C]
-
-        unpack_grads(load, store)
-        done = (first_ref, first_hbm, 9 * dx) if half == 0 else (second_ref, second_hbm, 18 - 9 * dx)
-        taps = pl.ds(done[2], 9)
-        stores.append(pltpu.make_async_copy(done[0].at[taps], done[1].at[taps], out_sem.at[i]))
-        stores[-1].start()
+    )(position, count, *(pltpu.with_memory_space_constraint(a, pltpu.HBM) for a in (x, g, codes, first, second)))
+
+
+def finish_kernel(grad_ref, sum_ref, out_hbm, first_hbm, second_hbm, first_ref, second_ref, out_sem):
+    stores = [pltpu.make_async_copy(grad_ref, out_hbm, out_sem.at[6])]
+    stores[0].start()
+    for dx in (0, 1, 2):
+        for half in (0, 1):
+
+            def load(tile):
+                return sum_ref[pl.ds(half * HALF + dx * STRIP + tile * C, C), :].astype(F32)
+
+            def store(tap, value):
+                if half == 0:
+                    first_ref[9 * dx + tap] = value.T[:C]
+                else:
+                    second_ref[26 - 9 * dx - tap] = value[:, :C]
+
+            unpack_grads(load, store)
+            here, there, start = (first_ref, first_hbm, 9 * dx) if half == 0 else (second_ref, second_hbm, 18 - 9 * dx)
+            taps = pl.ds(start, 9)
+            stores.append(pltpu.make_async_copy(here.at[taps], there.at[taps], out_sem.at[2 * dx + half]))
+            stores[-1].start()
     for copy in stores:
         copy.wait()
-    keep.wait()
 
 
 def finish(grad, summed):
@@ -575,14 +602,15 @@
         out_shape=(
             jax.ShapeDtypeStruct((C, 512), BF),
             jax.ShapeDtypeStruct((27, C, C), F32), jax.ShapeDtypeStruct((27, C, C), F32)),
-        in_specs=[anywhere, anywhere],
+        in_specs=[VMEM, VMEM],
         out_specs=(anywhere,) * 3,
         scratch_shapes=[
-            pltpu.VMEM((6, STRIP, WIDE), BF), pltpu.VMEM((27, C, C), F32), pltpu.VMEM((27, C, C), F32),
-            pltpu.SemaphoreType.DMA((6,)), pltpu.SemaphoreType.DMA((7,))],
-        compiler_params=pltpu.CompilerParams(vmem_limit_bytes=60 * 2 ** 20),
+            pltpu.VMEM((27, C, C), F32), pltpu.VMEM((27, C, C), F32), pltpu.SemaphoreType.DMA((7,))],
+        compiler_params=pltpu.CompilerParams(vmem_limit_bytes=16 * 2 ** 20),
         name="finish",
-    )(grad, summed)
+    )(
+        pltpu.with_memory_space_constraint(grad, pltpu.VMEM),
+        pltpu.with_memory_space_constraint(summed, pltpu.VMEM))
 
 
 def shards(features, cotangent, first_weight, second_weight, slot_position, brick_count, column_code):

time: 67.9 us -> 66.2 us (0.975)
  Pallas kernels: 65.8 us -> 64.2 us
    pallas_call x1, Pallas kernels: 4.2 us -> 1.92 us  [finish(): pl.pallas_call(finish_kernel, out_shape=(jax.ShapeDtypeStruct((C, 512), B...]
where the time goes in v6:
time: 66.2 us; the launch traced here: 66.1 us
  Pallas kernels  64.2 us (97%)
  between operations  1.93 us (3%)
    pallas_call x1, Pallas kernels, whole(): pl.pallas_call(functools.partial(whole_kernel, scale), out_shape=(pltpu.V...  62.2 us
    pallas_call x1, Pallas kernels, finish(): pl.pallas_call(finish_kernel, out_shape=(jax.ShapeDtypeStruct((C, 512), B...  1.92 us

profile of v6, /device:TPU:1, one launch (start us, length us, event | category | flops | bytes accessed | tf_op | source)
XLA Modules:
  0.0 66.1 jit_solution(11950353291043441804)
XLA Ops:
  1.9 62.2 %whole.1 = (bf16[96,512]{1,0:T(8,128)(2,1)S(1)}, bf16[4096,128]{1,0:T(8,128)(2,1)S(1)}) custom-call(s32[1]{0:T(128)} %bitcast.6.position_ref, s32[1]{0:T(128)} %bitcast.7.count_ref, bf16[96,512]{1,0:T(8,128)(2,1)} %bitcast.8, bf16[96,512]{1,0:T(8,128)(2,1)} %bitcast.9, s32[1,64]{1,0:T(1,128)} %bitcast.10, bf16[27,96,96]{2,1,0:T(8,128)(2,1)} %first_hbm.1, ...), custom_call_target="tpu_custom_call" | custom-call | tf_op jit(solution)/shard_map/whole/pallas_call | solution.py:542
  64.2 1.9 %finish.1 = (bf16[96,512]{1,0:T(8,128)(2,1)}, f32[27,96,96]{2,1,0:T(8,128)}, f32[27,96,96]{2,1,0:T(8,128)}) custom-call(bf16[96,512]{1,0:T(8,128)(2,1)S(1)} %get-tuple-element.8.grad_ref, bf16[4096,128]{1,0:T(8,128)(2,1)S(1)} %get-tuple-element.9.sum_ref), custom_call_target="tpu_custom_call" | custom-call | tf_op jit(solution)/shard_map/finish/pallas_call | solution.py:600

commit v7 on v5

--- a/solution.py
+++ b/solution.py
@@ -314,7 +314,7 @@
 def all_sum(fill_plane, fill_line, data_ref, sum_ref, gathered, half_out, half_in, total, plane_out, plane_in,
             near_src, near_in, line_in, own_part, swap_send, swap_recv, plane_send, plane_recv,
             near_send, near_recv, line_send, line_recv, plane_send2, plane_recv2,
-            join_send, join_recv, out_sem):
+            join_send, join_recv):
     core, x, y, mate, plane_peer, near_peer, line_peer = places()
     u = lax.axis_index("gx")
     chip = x * 4 + y
@@ -404,18 +404,12 @@
         plane_arrive(t).wait_recv()
         joins.append(join_copy(t, own))
         joins[-1].start()
-    first_out = pltpu.make_async_copy(
-        gathered.at[pl.ds(own, HALF), :], sum_ref.at[pl.ds(own, HALF), :], out_sem.at[0])
-    first_out.start()
+    sum_ref[pl.ds(own, HALF), :] = gathered[pl.ds(own, HALF), :]
     for t in [0, *reversed(PLANE)]:
         join_copy(t, other).wait_recv()
-    second_out = pltpu.make_async_copy(
-        gathered.at[pl.ds(other, HALF), :], sum_ref.at[pl.ds(other, HALF), :], out_sem.at[1])
-    second_out.start()
+    sum_ref[pl.ds(other, HALF), :] = gathered[pl.ds(other, HALF), :]
     for copy in [*swaps, *plane_copies, *near_copies, *line_copies, *backs, *joins]:
         copy.wait_send()
-    first_out.wait()
-    second_out.wait()
 
 
 SHARERS = 1 + 15 + 15
@@ -507,9 +501,9 @@
     anywhere = pl.BlockSpec(memory_space=pl.ANY)
     return pl.pallas_call(
         functools.partial(whole_kernel, scale),
-        out_shape=(jax.ShapeDtypeStruct((C, 512), BF), jax.ShapeDtypeStruct((ROWS, WIDE), BF)),
+        out_shape=(pltpu.VMEM((C, 512), BF), pltpu.VMEM((ROWS, WIDE), BF)),
         in_specs=[SMEM, SMEM] + [anywhere] * 5,
-        out_specs=(VMEM, anywhere),
+        out_specs=(VMEM, VMEM),
         scratch_shapes=[
             pltpu.VMEM((C, 512), BF), pltpu.VMEM((C, 512), BF), pltpu.VMEM((1, 64), jnp.int32),
             pltpu.VMEM((27, C, C), BF), pltpu.VMEM((27, C, C), BF), sems(5),
@@ -528,44 +522,36 @@
             pltpu.VMEM((4, CELL, WIDE), F32), pltpu.VMEM((16, CELL, WIDE), BF),
             pltpu.VMEM((PART, WIDE), BF),
             sems(3), sems(3), sems(16), sems(16), sems(4), sems(4), sems(16), sems(16),
-            sems(16), sems(16), sems(16), sems(16), sems(2),
+            sems(16), sems(16), sems(16), sems(16),
         ],
         compiler_params=pltpu.CompilerParams(
-            collective_id=1, has_side_effects=True, vmem_limit_bytes=60 * 2 ** 20),
+            collective_id=1, has_side_effects=True, vmem_limit_bytes=48 * 2 ** 20),
         name="whole",
-    )(position, count, x, g, codes, first, second)
-
-
-def finish_kernel(grad_hbm, sum_hbm, out_hbm, first_hbm, second_hbm, sum_ref, first_ref, second_ref, in_sem, out_sem):
-    keep = pltpu.make_async_copy(grad_hbm, out_hbm, out_sem.at[6])
-    keep.start()
-    strips = [(half, dx) for dx in (0, 1, 2) for half in (0, 1)]
-    loads = []
-    for i, (half, dx) in enumerate(strips):
-        rows = pl.ds(half * HALF + dx * STRIP, STRIP)
-        loads.append(pltpu.make_async_copy(sum_hbm.at[rows, :], sum_ref.at[i], in_sem.at[i]))
-        loads[-1].start()
-    stores = []
-    for i, (half, dx) in enumerate(strips):
-        loads[i].wait()
-
-        def load(tile):
-            return sum_ref[i, pl.ds(tile * C, C), :].astype(F32)
-
-        def store(tap, value):
-            if half == 0:
-                first_ref[9 * dx + tap] = value.T[:C]
-            else:
-                second_ref[26 - 9 * dx - tap] = value[:, :C]
-
-        unpack_grads(load, store)
-        done = (first_ref, first_hbm, 9 * dx) if half == 0 else (second_ref, second_hbm, 18 - 9 * dx)
-        taps = pl.ds(done[2], 9)
-        stores.append(pltpu.make_async_copy(done[0].at[taps], done[1].at[taps], out_sem.at[i]))
-        stores[-1].start()
+    )(position, count, *(pltpu.with_memory_space_constraint(a, pltpu.HBM) for a in (x, g, codes, first, second)))
+
+
+def finish_kernel(grad_ref, sum_ref, out_hbm, first_hbm, second_hbm, first_ref, second_ref, out_sem):
+    stores = [pltpu.make_async_copy(grad_ref, out_hbm, out_sem.at[6])]
+    stores[0].start()
+    for dx in (0, 1, 2):
+        for half in (0, 1):
+
+            def load(tile):
+                return sum_ref[pl.ds(half * HALF + dx * STRIP + tile * C, C), :].astype(F32)
+
+            def store(tap, value):
+                if half == 0:
+                    first_ref[9 * dx + tap] = value.T[:C]
+                else:
+                    second_ref[26 - 9 * dx - tap] = value[:, :C]
+
+            unpack_grads(load, store)
+            here, there, start = (first_ref, first_hbm, 9 * dx) if half == 0 else (second_ref, second_hbm, 18 - 9 * dx)
+            taps = pl.ds(start, 9)
+            stores.append(pltpu.make_async_copy(here.at[taps], there.at[taps], out_sem.at[2 * dx + half]))
+            stores[-1].start()
     for copy in stores:
         copy.wait()
-    keep.wait()
 
 
 def finish(grad, summed):
@@ -575,14 +561,15 @@
         out_shape=(
             jax.ShapeDtypeStruct((C, 512), BF),
             jax.ShapeDtypeStruct((27, C, C), F32), jax.ShapeDtypeStruct((27, C, C), F32)),
-        in_specs=[anywhere, anywhere],
+        in_specs=[VMEM, VMEM],
         out_specs=(anywhere,) * 3,
         scratch_shapes=[
-            pltpu.VMEM((6, STRIP, WIDE), BF), pltpu.VMEM((27, C, C), F32), pltpu.VMEM((27, C, C), F32),
-            pltpu.SemaphoreType.DMA((6,)), pltpu.SemaphoreType.DMA((7,))],
-        compiler_params=pltpu.CompilerParams(vmem_limit_bytes=60 * 2 ** 20),
+            pltpu.VMEM((27, C, C), F32), pltpu.VMEM((27, C, C), F32), pltpu.SemaphoreType.DMA((7,))],
+        compiler_params=pltpu.CompilerParams(vmem_limit_bytes=16 * 2 ** 20),
         name="finish",
-    )(grad, summed)
+    )(
+        pltpu.with_memory_space_constraint(grad, pltpu.VMEM),
+        pltpu.with_memory_space_constraint(summed, pltpu.VMEM))
 
 
 def shards(features, cotangent, first_weight, second_weight, slot_position, brick_count, column_code):

time: 67.9 us -> 64.3 us (0.947)
  Pallas kernels: 65.8 us -> 62.2 us
    pallas_call x1, Pallas kernels: 4.2 us -> 1.92 us  [finish(): pl.pallas_call(finish_kernel, out_shape=(jax.ShapeDtypeStruct((C, 512), B...]
    pallas_call x1, Pallas kernels: 61.6 us -> 60.3 us  [whole(): pl.pallas_call(functools.partial(whole_kernel, scale), out_shape=(pltpu.V...]
where the time goes in v7:
time: 64.3 us; the launch traced here: 64.2 us
  Pallas kernels  62.2 us (97%)
  between operations  1.93 us (3%)
    pallas_call x1, Pallas kernels, whole(): pl.pallas_call(functools.partial(whole_kernel, scale), out_shape=(pltpu.V...  60.3 us
    pallas_call x1, Pallas kernels, finish(): pl.pallas_call(finish_kernel, out_shape=(jax.ShapeDtypeStruct((C, 512), B...  1.92 us

profile of v7, /device:TPU:1, one launch (start us, length us, event | category | flops | bytes accessed | tf_op | source)
XLA Modules:
  0.0 64.2 jit_solution(5735374426727882830)
XLA Ops:
  1.9 60.3 %whole.1 = (bf16[96,512]{1,0:T(8,128)(2,1)S(1)}, bf16[4096,128]{1,0:T(8,128)(2,1)S(1)}) custom-call(s32[1]{0:T(128)} %bitcast.6.position_ref, s32[1]{0:T(128)} %bitcast.7.count_ref, bf16[96,512]{1,0:T(8,128)(2,1)} %bitcast.8, bf16[96,512]{1,0:T(8,128)(2,1)} %bitcast.9, s32[1,64]{1,0:T(1,128)} %bitcast.10, bf16[27,96,96]{2,1,0:T(8,128)(2,1)} %first_hbm.1, ...), custom_call_target="tpu_custom_call" | custom-call | tf_op jit(solution)/shard_map/whole/pallas_call | solution.py:502
  62.2 1.9 %finish.1 = (bf16[96,512]{1,0:T(8,128)(2,1)}, f32[27,96,96]{2,1,0:T(8,128)}, f32[27,96,96]{2,1,0:T(8,128)}) custom-call(bf16[96,512]{1,0:T(8,128)(2,1)S(1)} %get-tuple-element.8.grad_ref, bf16[4096,128]{1,0:T(8,128)(2,1)S(1)} %get-tuple-element.9.sum_ref), custom_call_target="tpu_custom_call" | custom-call | tf_op jit(solution)/shard_map/finish/pallas_call | solution.py:559

commit v8 on v7

--- a/solution.py
+++ b/solution.py
@@ -415,16 +415,11 @@
 SHARERS = 1 + 15 + 15
 
 
-def whole_kernel(scale, position_ref, count_ref, x_hbm, g_hbm, code_hbm, first_hbm, second_hbm,
-                 out_ref, sum_ref, x_ref, g_ref, code_ref, first_ref, second_ref, load_sem,
-                 wide_ref, rows_ref, msg_ref, into_ref, back_msg_ref, back_into_ref,
-                 x_weight_ref, g_weight_ref, back_weight_ref, level_ref, x_patch_ref, g_patch_ref,
-                 back_level_ref, back_patch_ref, grads_ref, data_ref, delta_ref,
-                 send_sem, recv_sem, back_send_sem, back_recv_sem, *reduce_refs):
+def halo_kernel(position_ref, count_ref, x_hbm, g_hbm, code_hbm, first_hbm, second_hbm,
+                rows_ref, halo_ref, x_weight_ref, g_weight_ref, x_ref, g_ref, code_ref, first_ref, second_ref, load_sem,
+                wide_ref, msg_ref, into_ref, send_sem, recv_sem):
     q = lax.axis_index("gz")
-    position = position_ref[0]
     barrier = pltpu.get_barrier_semaphore()
-    greet_sharers(barrier)
     greet_neighbours(barrier)
     loads = [
         pltpu.make_async_copy(src, dst, load_sem.at[i])
@@ -434,9 +429,9 @@
         load.start()
     for load in loads[:3]:
         load.wait()
-    pack_rows(position, count_ref[0], x_ref, g_ref, code_ref, wide_ref, rows_ref)
+    pack_rows(position_ref[0], count_ref[0], x_ref, g_ref, code_ref, wide_ref, rows_ref)
     pack_messages(wide_ref, msg_ref, q)
-    pl.semaphore_wait(barrier, 17 + SHARERS)
+    pl.semaphore_wait(barrier, 17)
     copies = halo_copies(msg_ref, into_ref, send_sem, recv_sem)
     for copy in copies:
         copy.start()
@@ -446,6 +441,44 @@
     lay_weights(second_ref, g_weight_ref, True)
     for copy in copies:
         copy.wait()
+    halo_ref[...] = into_ref[...]
+
+
+def halo(position, count, x, g, codes, first, second):
+    sems = lambda n: pltpu.SemaphoreType.DMA((n,))
+    taps = 9 * WIDE
+    anywhere = pl.BlockSpec(memory_space=pl.ANY)
+    return pl.pallas_call(
+        halo_kernel,
+        out_shape=(
+            pltpu.VMEM((512, 2 * WIDE), BF), pltpu.VMEM((MSG, 2 * WIDE), BF),
+            pltpu.VMEM((3, taps, WIDE), BF), pltpu.VMEM((3, taps, WIDE), BF)),
+        in_specs=[SMEM, SMEM] + [anywhere] * 5,
+        out_specs=(VMEM,) * 4,
+        scratch_shapes=[
+            pltpu.VMEM((C, 512), BF), pltpu.VMEM((C, 512), BF), pltpu.VMEM((1, 64), jnp.int32),
+            pltpu.VMEM((27, C, C), BF), pltpu.VMEM((27, C, C), BF), sems(5),
+            pltpu.VMEM((2, 512, WIDE), F32), pltpu.VMEM((MSG, 2 * WIDE), BF), pltpu.VMEM((MSG, 2 * WIDE), BF),
+            sems(17), sems(17),
+        ],
+        compiler_params=pltpu.CompilerParams(
+            collective_id=2, has_side_effects=True, vmem_limit_bytes=24 * 2 ** 20),
+        name="halo",
+    )(position, count, *(pltpu.with_memory_space_constraint(a, pltpu.HBM) for a in (x, g, codes, first, second)))
+
+
+def whole_kernel(scale, position_ref, first_hbm, rows_ref, into_ref, x_weight_ref, g_weight_ref,
+                 out_ref, sum_ref, first_ref, load_sem, wide_ref, back_msg_ref, back_into_ref,
+                 back_weight_ref, level_ref, x_patch_ref, g_patch_ref,
+                 back_level_ref, back_patch_ref, grads_ref, data_ref, delta_ref,
+                 back_send_sem, back_recv_sem, *reduce_refs):
+    q = lax.axis_index("gz")
+    position = position_ref[0]
+    barrier = pltpu.get_barrier_semaphore()
+    greet_sharers(barrier)
+    greet_neighbours(barrier)
+    load = pltpu.make_async_copy(first_hbm, first_ref, load_sem.at[0])
+    load.start()
 
     rows = rows_ref[...].astype(F32)
     picked = pick_messages(position, into_ref)
@@ -476,12 +509,15 @@
                 data_ref[pl.ds(half * HALF + dx * STRIP + tile * C, C), :] = value
 
             pack_grads(block, store)
+        if dx == 0:
+            pl.semaphore_wait(barrier, 17 + SHARERS)
         start_swap(dx, data_ref, *reduce_refs[1:3], *reduce_refs[10:12])
 
     def fill_plane():
-        pack_messages(wide_ref.at[pl.ds(0, 1)], back_msg_ref, q)
+        pack_messages(wide_ref, back_msg_ref, q)
         for copy in back_copies:
             copy.start()
+        load.wait()
         lay_weights(first_ref, back_weight_ref, True)
 
     def fill_line():
@@ -495,26 +531,22 @@
     all_sum(fill_plane, fill_line, data_ref, sum_ref, *reduce_refs)
 
 
-def whole(scale, position, count, x, g, codes, first, second):
+def whole(scale, position, first, rows, into, x_weight, g_weight):
     sems = lambda n: pltpu.SemaphoreType.DMA((n,))
     taps = 9 * WIDE
     anywhere = pl.BlockSpec(memory_space=pl.ANY)
     return pl.pallas_call(
         functools.partial(whole_kernel, scale),
         out_shape=(pltpu.VMEM((C, 512), BF), pltpu.VMEM((ROWS, WIDE), BF)),
-        in_specs=[SMEM, SMEM] + [anywhere] * 5,
+        in_specs=[SMEM, anywhere] + [VMEM] * 4,
         out_specs=(VMEM, VMEM),
         scratch_shapes=[
-            pltpu.VMEM((C, 512), BF), pltpu.VMEM((C, 512), BF), pltpu.VMEM((1, 64), jnp.int32),
-            pltpu.VMEM((27, C, C), BF), pltpu.VMEM((27, C, C), BF), sems(5),
-            pltpu.VMEM((2, 512, WIDE), F32), pltpu.VMEM((512, 2 * WIDE), BF),
-            pltpu.VMEM((MSG, 2 * WIDE), BF), pltpu.VMEM((MSG, 2 * WIDE), BF),
-            pltpu.VMEM((MSG, WIDE), BF), pltpu.VMEM((MSG, WIDE), BF),
-            pltpu.VMEM((3, taps, WIDE), BF), pltpu.VMEM((3, taps, WIDE), BF), pltpu.VMEM((3, taps, WIDE), BF),
+            pltpu.VMEM((27, C, C), BF), sems(1), pltpu.VMEM((1, 512, WIDE), F32),
+            pltpu.VMEM((MSG, WIDE), BF), pltpu.VMEM((MSG, WIDE), BF), pltpu.VMEM((3, taps, WIDE), BF),
             pltpu.VMEM((800, 2 * WIDE), F32), pltpu.VMEM((640, taps), BF), pltpu.VMEM((640, taps), BF),
             pltpu.VMEM((800, WIDE), F32), pltpu.VMEM((640, taps), BF),
             pltpu.VMEM((2, C, taps), F32), pltpu.VMEM((ROWS, WIDE), F32), pltpu.VMEM((512, WIDE), BF),
-            sems(17), sems(17), sems(17), sems(17),
+            sems(17), sems(17),
             pltpu.VMEM((ROWS, WIDE), BF),
             pltpu.VMEM((HALF, WIDE), F32), pltpu.VMEM((HALF, WIDE), F32),
             pltpu.VMEM((HALF, WIDE), F32), pltpu.VMEM((HALF, WIDE), BF),
@@ -527,7 +559,9 @@
         compiler_params=pltpu.CompilerParams(
             collective_id=1, has_side_effects=True, vmem_limit_bytes=48 * 2 ** 20),
         name="whole",
-    )(position, count, *(pltpu.with_memory_space_constraint(a, pltpu.HBM) for a in (x, g, codes, first, second)))
+    )(
+        position, pltpu.with_memory_space_constraint(first, pltpu.HBM),
+        *(pltpu.with_memory_space_constraint(a, pltpu.VMEM) for a in (rows, into, x_weight, g_weight)))
 
 
 def finish_kernel(grad_ref, sum_ref, out_hbm, first_hbm, second_hbm, first_ref, second_ref, out_sem):
@@ -575,9 +609,11 @@
 def shards(features, cotangent, first_weight, second_weight, slot_position, brick_count, column_code):
     devices = lax.axis_size("gx") * lax.axis_size("gy") * lax.axis_size("gz")
     scale = float(devices ** -0.5 / 8.0)
-    grad, summed = whole(
-        scale, slot_position.reshape(1), brick_count.reshape(1), features.reshape(C, 512),
-        cotangent.reshape(C, 512), column_code.reshape(1, 64), first_weight, second_weight)
+    position = slot_position.reshape(1)
+    handed = halo(
+        position, brick_count.reshape(1), features.reshape(C, 512), cotangent.reshape(C, 512),
+        column_code.reshape(1, 64), first_weight, second_weight)
+    grad, summed = whole(scale, position, first_weight, *handed)
     grad_input, first_grad, second_grad = finish(grad, summed)
     return grad_input.reshape(1, 1, 1, 1, C, 512), first_grad, second_grad
 

time: 64.3 us -> 64.4 us (level)
    pallas_call x0 -> x1, Pallas kernels: none -> 19.3 us  [halo(): pl.pallas_call(halo_kernel, out_shape=(pltpu.VMEM((512, 2 * WIDE), BF), p...]
    pallas_call x1, Pallas kernels: 60.3 us -> 41.1 us  [whole(): pl.pallas_call(functools.partial(whole_kernel, scale), out_shape=(pltpu.V...]
where the time goes in v8:
time: 64.4 us; the launch traced here: 64.2 us
  Pallas kernels  62.3 us (97%)
  between operations  1.94 us (3%)
    pallas_call x1, Pallas kernels, whole(): pl.pallas_call(functools.partial(whole_kernel, scale), out_shape=(pltpu.V...  41.1 us
    pallas_call x1, Pallas kernels, halo(): pl.pallas_call(halo_kernel, out_shape=(pltpu.VMEM((512, 2 * WIDE), BF), p...  19.3 us
    pallas_call x1, Pallas kernels, finish(): pl.pallas_call(finish_kernel, out_shape=(jax.ShapeDtypeStruct((C, 512), B...  1.92 us

profile of v8, /device:TPU:1, one launch (start us, length us, event | category | flops | bytes accessed | tf_op | source)
XLA Modules:
  0.0 64.2 jit_solution(15262247539481839003)
XLA Ops:
  1.9 19.3 %halo.1 = (bf16[512,256]{1,0:T(8,128)(2,1)S(1)}, bf16[512,256]{1,0:T(8,128)(2,1)S(1)}, bf16[3,1152,128]{2,1,0:T(8,128)(2,1)S(1)}, bf16[3,1152,128]{2,1,0:T(8,128)(2,1)S(1)}) custom-call(s32[1]{0:T(128)} %bitcast.6.position_ref, s32[1]{0:T(128)} %bitcast.8.count_ref, bf16[96,512]{1,0:T(8,128)(2,1)} %bitcast.9, bf16[96,512]{1,0:T(8,128)(2,1)} %bitcast.10, ...), custom_call_target="tpu_custom_call" | custom-call | tf_op jit(solution)/shard_map/halo/pallas_call | solution.py:451
  21.2 41.1 %whole.1 = (bf16[96,512]{1,0:T(8,128)(2,1)S(1)}, bf16[4096,128]{1,0:T(8,128)(2,1)S(1)}) custom-call(s32[1]{0:T(128)} %bitcast.7.position_ref, bf16[27,96,96]{2,1,0:T(8,128)(2,1)} %first_hbm.3, bf16[512,256]{1,0:T(8,128)(2,1)S(1)} %get-tuple-element.12.rows_ref, bf16[512,256]{1,0:T(8,128)(2,1)S(1)} %get-tuple-element.13.into_ref, ...), custom_call_target="tpu_custom_call" | custom-call | tf_op jit(solution)/shard_map/whole/pallas_call | solution.py:538
  62.3 1.9 %finish.1 = (bf16[96,512]{1,0:T(8,128)(2,1)}, f32[27,96,96]{2,1,0:T(8,128)}, f32[27,96,96]{2,1,0:T(8,128)}) custom-call(bf16[96,512]{1,0:T(8,128)(2,1)S(1)} %get-tuple-element.16.grad_ref, bf16[4096,128]{1,0:T(8,128)(2,1)S(1)} %get-tuple-element.17.sum_ref), custom_call_target="tpu_custom_call" | custom-call | tf_op jit(solution)/shard_map/finish/pallas_call | solution.py:593

commit v9 on v8

--- a/solution.py
+++ b/solution.py
@@ -311,7 +311,7 @@
     swap_copy(strip, half_out, half_in, swap_send, swap_recv).start()
 
 
-def all_sum(fill_plane, fill_line, data_ref, sum_ref, gathered, half_out, half_in, total, plane_out, plane_in,
+def all_sum(fill_plane, fill_line, data_ref, spread, gathered, half_out, half_in, total, plane_out, plane_in,
             near_src, near_in, line_in, own_part, swap_send, swap_recv, plane_send, plane_recv,
             near_send, near_recv, line_send, line_recv, plane_send2, plane_recv2,
             join_send, join_recv):
@@ -404,10 +404,10 @@
         plane_arrive(t).wait_recv()
         joins.append(join_copy(t, own))
         joins[-1].start()
-    sum_ref[pl.ds(own, HALF), :] = gathered[pl.ds(own, HALF), :]
+    spread(core)
     for t in [0, *reversed(PLANE)]:
         join_copy(t, other).wait_recv()
-    sum_ref[pl.ds(other, HALF), :] = gathered[pl.ds(other, HALF), :]
+    spread(1 - core)
     for copy in [*swaps, *plane_copies, *near_copies, *line_copies, *backs, *joins]:
         copy.wait_send()
 
@@ -468,7 +468,7 @@
 
 
 def whole_kernel(scale, position_ref, first_hbm, rows_ref, into_ref, x_weight_ref, g_weight_ref,
-                 out_ref, sum_ref, first_ref, load_sem, wide_ref, back_msg_ref, back_into_ref,
+                 out_ref, first_out_ref, second_out_ref, first_ref, load_sem, wide_ref, back_msg_ref, back_into_ref,
                  back_weight_ref, level_ref, x_patch_ref, g_patch_ref,
                  back_level_ref, back_patch_ref, grads_ref, data_ref, delta_ref,
                  back_send_sem, back_recv_sem, *reduce_refs):
@@ -509,9 +509,11 @@
                 data_ref[pl.ds(half * HALF + dx * STRIP + tile * C, C), :] = value
 
             pack_grads(block, store)
-        if dx == 0:
+        if dx == 1:
             pl.semaphore_wait(barrier, 17 + SHARERS)
-        start_swap(dx, data_ref, *reduce_refs[1:3], *reduce_refs[10:12])
+            start_swap(0, data_ref, *reduce_refs[1:3], *reduce_refs[10:12])
+        if dx > 0:
+            start_swap(dx, data_ref, *reduce_refs[1:3], *reduce_refs[10:12])
 
     def fill_plane():
         pack_messages(wide_ref, back_msg_ref, q)
@@ -528,7 +530,25 @@
         grad = convolve(rows_ref[:, WIDE:].astype(F32), back_patch_ref, back_weight_ref)
         out_ref[...] = (grad * mask).T[:C].astype(BF)
 
-    all_sum(fill_plane, fill_line, data_ref, sum_ref, *reduce_refs)
+    def spread(half):
+        for which in (0, 1):
+
+            @pl.when(half == which)
+            def _():
+                for dx in (0, 1, 2):
+
+                    def load(tile):
+                        return reduce_refs[0][pl.ds(which * HALF + dx * STRIP + tile * C, C), :].astype(F32)
+
+                    def store(tap, value):
+                        if which == 0:
+                            first_out_ref[9 * dx + tap] = value.T[:C]
+                        else:
+                            second_out_ref[26 - 9 * dx - tap] = value[:, :C]
+
+                    unpack_grads(load, store)
+
+    all_sum(fill_plane, fill_line, data_ref, spread, *reduce_refs)
 
 
 def whole(scale, position, first, rows, into, x_weight, g_weight):
@@ -537,9 +557,9 @@
     anywhere = pl.BlockSpec(memory_space=pl.ANY)
     return pl.pallas_call(
         functools.partial(whole_kernel, scale),
-        out_shape=(pltpu.VMEM((C, 512), BF), pltpu.VMEM((ROWS, WIDE), BF)),
+        out_shape=(pltpu.VMEM((C, 512), BF), pltpu.VMEM((27, C, C), F32), pltpu.VMEM((27, C, C), F32)),
         in_specs=[SMEM, anywhere] + [VMEM] * 4,
-        out_specs=(VMEM, VMEM),
+        out_specs=(VMEM,) * 3,
         scratch_shapes=[
             pltpu.VMEM((27, C, C), BF), sems(1), pltpu.VMEM((1, 512, WIDE), F32),
             pltpu.VMEM((MSG, WIDE), BF), pltpu.VMEM((MSG, WIDE), BF), pltpu.VMEM((3, taps, WIDE), BF),
@@ -564,46 +584,33 @@
         *(pltpu.with_memory_space_constraint(a, pltpu.VMEM) for a in (rows, into, x_weight, g_weight)))
 
 
-def finish_kernel(grad_ref, sum_ref, out_hbm, first_hbm, second_hbm, first_ref, second_ref, out_sem):
-    stores = [pltpu.make_async_copy(grad_ref, out_hbm, out_sem.at[6])]
-    stores[0].start()
-    for dx in (0, 1, 2):
-        for half in (0, 1):
-
-            def load(tile):
-                return sum_ref[pl.ds(half * HALF + dx * STRIP + tile * C, C), :].astype(F32)
-
-            def store(tap, value):
-                if half == 0:
-                    first_ref[9 * dx + tap] = value.T[:C]
-                else:
-                    second_ref[26 - 9 * dx - tap] = value[:, :C]
-
-            unpack_grads(load, store)
-            here, there, start = (first_ref, first_hbm, 9 * dx) if half == 0 else (second_ref, second_hbm, 18 - 9 * dx)
-            taps = pl.ds(start, 9)
-            stores.append(pltpu.make_async_copy(here.at[taps], there.at[taps], out_sem.at[2 * dx + half]))
-            stores[-1].start()
-    for copy in stores:
+def finish_kernel(grad_ref, first_ref, second_ref, grad_hbm, first_hbm, second_hbm, out_sem):
+    stores = []
+    for start in (0, 9, 18):
+        taps = pl.ds(start, 9)
+        stores.append((first_ref.at[taps], first_hbm.at[taps]))
+        stores.append((second_ref.at[taps], second_hbm.at[taps]))
+    stores.append((grad_ref, grad_hbm))
+    copies = [pltpu.make_async_copy(here, there, out_sem.at[i]) for i, (here, there) in enumerate(stores)]
+    for copy in copies:
+        copy.start()
+    for copy in copies:
         copy.wait()
 
 
-def finish(grad, summed):
+def finish(grad, first, second):
     anywhere = pl.BlockSpec(memory_space=pl.ANY)
     return pl.pallas_call(
         finish_kernel,
         out_shape=(
             jax.ShapeDtypeStruct((C, 512), BF),
             jax.ShapeDtypeStruct((27, C, C), F32), jax.ShapeDtypeStruct((27, C, C), F32)),
-        in_specs=[VMEM, VMEM],
+        in_specs=[VMEM] * 3,
         out_specs=(anywhere,) * 3,
-        scratch_shapes=[
-            pltpu.VMEM((27, C, C), F32), pltpu.VMEM((27, C, C), F32), pltpu.SemaphoreType.DMA((7,))],
+        scratch_shapes=[pltpu.SemaphoreType.DMA((7,))],
         compiler_params=pltpu.CompilerParams(vmem_limit_bytes=16 * 2 ** 20),
         name="finish",
-    )(
-        pltpu.with_memory_space_constraint(grad, pltpu.VMEM),
-        pltpu.with_memory_space_constraint(summed, pltpu.VMEM))
+    )(*(pltpu.with_memory_space_constraint(a, pltpu.VMEM) for a in (grad, first, second)))
 
 
 def shards(features, cotangent, first_weight, second_weight, slot_position, brick_count, column_code):
@@ -613,8 +620,7 @@
     handed = halo(
         position, brick_count.reshape(1), features.reshape(C, 512), cotangent.reshape(C, 512),
         column_code.reshape(1, 64), first_weight, second_weight)
-    grad, summed = whole(scale, position, first_weight, *handed)
-    grad_input, first_grad, second_grad = finish(grad, summed)
+    grad_input, first_grad, second_grad = finish(*whole(scale, position, first_weight, *handed))
     return grad_input.reshape(1, 1, 1, 1, C, 512), first_grad, second_grad
 
 

time: 64.4 us -> 64.2 us (level)
  no operation moved by 1% of the time
where the time goes in v9:
time: 64.2 us; the launch traced here: 64 us
  Pallas kernels  62 us (97%)
  between operations  1.94 us (3%)
    pallas_call x1, Pallas kernels, whole(): pl.pallas_call(functools.partial(whole_kernel, scale), out_shape=(pltpu.V...  41.2 us
    pallas_call x1, Pallas kernels, halo(): pl.pallas_call(halo_kernel, out_shape=(pltpu.VMEM((512, 2 * WIDE), BF), p...  19.3 us
    pallas_call x1, Pallas kernels, finish(): pl.pallas_call(finish_kernel, out_shape=(jax.ShapeDtypeStruct((C, 512), B...  1.58 us

profile of v9, /device:TPU:1, one launch (start us, length us, event | category | flops | bytes accessed | tf_op | source)
XLA Modules:
  0.0 64.0 jit_solution(3914924398720962128)
XLA Ops:
  1.9 19.3 %halo.1 = (bf16[512,256]{1,0:T(8,128)(2,1)S(1)}, bf16[512,256]{1,0:T(8,128)(2,1)S(1)}, bf16[3,1152,128]{2,1,0:T(8,128)(2,1)S(1)}, bf16[3,1152,128]{2,1,0:T(8,128)(2,1)S(1)}) custom-call(s32[1]{0:T(128)} %bitcast.6.position_ref, s32[1]{0:T(128)} %bitcast.8.count_ref, bf16[96,512]{1,0:T(8,128)(2,1)} %bitcast.9, bf16[96,512]{1,0:T(8,128)(2,1)} %bitcast.10, ...), custom_call_target="tpu_custom_call" | custom-call | tf_op jit(solution)/shard_map/halo/pallas_call | solution.py:451
  21.2 41.2 %whole.1 = (bf16[96,512]{1,0:T(8,128)(2,1)S(1)}, f32[27,96,96]{2,1,0:T(8,128)S(1)}, f32[27,96,96]{2,1,0:T(8,128)S(1)}) custom-call(s32[1]{0:T(128)} %bitcast.7.position_ref, bf16[27,96,96]{2,1,0:T(8,128)(2,1)} %first_hbm.3, bf16[512,256]{1,0:T(8,128)(2,1)S(1)} %get-tuple-element.13.rows_ref, bf16[512,256]{1,0:T(8,128)(2,1)S(1)} %get-tuple-element.14.into_ref, ...), custom_call_target="tpu_custom_call" | custom-call | tf_op jit(solution)/shard_map/whole/pallas_call | solution.py:558
  62.4 1.6 %finish.1 = (bf16[96,512]{1,0:T(8,128)(2,1)}, f32[27,96,96]{2,1,0:T(8,128)}, f32[27,96,96]{2,1,0:T(8,128)}) custom-call(bf16[96,512]{1,0:T(8,128)(2,1)S(1)} %get-tuple-element.17.grad_ref, f32[27,96,96]{2,1,0:T(8,128)S(1)} %get-tuple-element.18.first_ref, f32[27,96,96]{2,1,0:T(8,128)S(1)} %get-tuple-element.19.second_ref), custom_call_target="tpu_custom_call" | custom-call | tf_op jit(solution)/shard_map/finish/pallas_call | solution.py:603

commit v10 on v9

--- a/solution.py
+++ b/solution.py
@@ -321,26 +321,33 @@
     own = pl.multiple_of(core * HALF, HALF)
     other = pl.multiple_of((1 - core) * HALF, HALF)
 
+    def plane_copy(t):
+        there, device = plane_peer(t)
+        rows = pl.ds(pl.multiple_of(there * PART, PART), PART)
+        return remote(plane_out.at[rows, :], plane_in.at[t], plane_send, plane_recv, t, device)
+
+    plane_copies = [plane_copy(t) for t in PLANE]
+    early = 2 * STRIP // PART
     swaps = [swap_copy(strip, half_out, half_in, swap_send, swap_recv) for strip in range(3)]
-    for strip in range(3):
+
+    def join_strip(strip):
         rows = pl.ds(strip * STRIP, STRIP)
         swaps[strip].wait_recv()
         mine = data_ref[pl.ds(pl.multiple_of(own + strip * STRIP, 16), STRIP), :]
         both = mine + half_in[rows, :]
         total[rows, :] = both
         plane_out[rows, :] = both.astype(BF)
+
+    join_strip(0)
+    join_strip(1)
+    for t, copy in zip(PLANE, plane_copies):
+        pl.when(plane_peer(t)[0] < early)(copy.start)
+    join_strip(2)
     rest = pl.ds(3 * STRIP, HALF - 3 * STRIP)
     total[rest, :] = jnp.zeros((HALF - 3 * STRIP, WIDE), F32)
     plane_out[rest, :] = jnp.zeros((HALF - 3 * STRIP, WIDE), BF)
-
-    def plane_copy(t):
-        there, device = plane_peer(t)
-        rows = pl.ds(pl.multiple_of(there * PART, PART), PART)
-        return remote(plane_out.at[rows, :], plane_in.at[t], plane_send, plane_recv, t, device)
-
-    plane_copies = [plane_copy(t) for t in PLANE]
-    for copy in plane_copies:
-        copy.start()
+    for t, copy in zip(PLANE, plane_copies):
+        pl.when(plane_peer(t)[0] >= early)(copy.start)
     fill_plane()
     part = pl.multiple_of(chip * PART, PART)
     part_sum = total[pl.ds(part, PART), :]

time: 64.2 us -> 64.5 us (level)
  no operation moved by 1% of the time
where the time goes in v10:
time: 64.5 us; the launch traced here: 64.4 us
  Pallas kernels  62.4 us (97%)
  between operations  1.94 us (3%)
    pallas_call x1, Pallas kernels, whole(): pl.pallas_call(functools.partial(whole_kernel, scale), out_shape=(pltpu.V...  41.6 us
    pallas_call x1, Pallas kernels, halo(): pl.pallas_call(halo_kernel, out_shape=(pltpu.VMEM((512, 2 * WIDE), BF), p...  19.3 us
    pallas_call x1, Pallas kernels, finish(): pl.pallas_call(finish_kernel, out_shape=(jax.ShapeDtypeStruct((C, 512), B...  1.58 us

profile of v10, /device:TPU:1, one launch (start us, length us, event | category | flops | bytes accessed | tf_op | source)
XLA Modules:
  0.0 64.4 jit_solution(6705929413098546030)
XLA Ops:
  1.9 19.3 %halo.1 = (bf16[512,256]{1,0:T(8,128)(2,1)S(1)}, bf16[512,256]{1,0:T(8,128)(2,1)S(1)}, bf16[3,1152,128]{2,1,0:T(8,128)(2,1)S(1)}, bf16[3,1152,128]{2,1,0:T(8,128)(2,1)S(1)}) custom-call(s32[1]{0:T(128)} %bitcast.6.position_ref, s32[1]{0:T(128)} %bitcast.8.count_ref, bf16[96,512]{1,0:T(8,128)(2,1)} %bitcast.9, bf16[96,512]{1,0:T(8,128)(2,1)} %bitcast.10, ...), custom_call_target="tpu_custom_call" | custom-call | tf_op jit(solution)/shard_map/halo/pallas_call | solution.py:458
  21.2 41.6 %whole.1 = (bf16[96,512]{1,0:T(8,128)(2,1)S(1)}, f32[27,96,96]{2,1,0:T(8,128)S(1)}, f32[27,96,96]{2,1,0:T(8,128)S(1)}) custom-call(s32[1]{0:T(128)} %bitcast.7.position_ref, bf16[27,96,96]{2,1,0:T(8,128)(2,1)} %first_hbm.3, bf16[512,256]{1,0:T(8,128)(2,1)S(1)} %get-tuple-element.13.rows_ref, bf16[512,256]{1,0:T(8,128)(2,1)S(1)} %get-tuple-element.14.into_ref, ...), custom_call_target="tpu_custom_call" | custom-call | tf_op jit(solution)/shard_map/whole/pallas_call | solution.py:565
  62.8 1.6 %finish.1 = (bf16[96,512]{1,0:T(8,128)(2,1)}, f32[27,96,96]{2,1,0:T(8,128)}, f32[27,96,96]{2,1,0:T(8,128)}) custom-call(bf16[96,512]{1,0:T(8,128)(2,1)S(1)} %get-tuple-element.17.grad_ref, f32[27,96,96]{2,1,0:T(8,128)S(1)} %get-tuple-element.18.first_ref, f32[27,96,96]{2,1,0:T(8,128)S(1)} %get-tuple-element.19.second_ref), custom_call_target="tpu_custom_call" | custom-call | tf_op jit(solution)/shard_map/finish/pallas_call | solution.py:610

commit v11 on v9

--- a/solution.py
+++ b/solution.py
@@ -441,7 +441,7 @@
     lay_weights(second_ref, g_weight_ref, True)
     for copy in copies:
         copy.wait()
-    halo_ref[...] = into_ref[...]
+    halo_ref[...] = pick_messages(position_ref[0], into_ref)
 
 
 def halo(position, count, x, g, codes, first, second):
@@ -451,7 +451,7 @@
     return pl.pallas_call(
         halo_kernel,
         out_shape=(
-            pltpu.VMEM((512, 2 * WIDE), BF), pltpu.VMEM((MSG, 2 * WIDE), BF),
+            pltpu.VMEM((512, 2 * WIDE), BF), pltpu.VMEM((256, 2 * WIDE), BF),
             pltpu.VMEM((3, taps, WIDE), BF), pltpu.VMEM((3, taps, WIDE), BF)),
         in_specs=[SMEM, SMEM] + [anywhere] * 5,
         out_specs=(VMEM,) * 4,
@@ -481,7 +481,7 @@
     load.start()
 
     rows = rows_ref[...].astype(F32)
-    picked = pick_messages(position, into_ref)
+    picked = into_ref[...]
     sender = picked[:, :WIDE].astype(F32).T[C : C + 8].astype(jnp.int32)
     code = halo_codes(position, sender)[:1]
     build_patch(rows, picked, code, level_ref, (x_patch_ref, g_patch_ref))

time: 64.2 us -> 64.2 us (level)
  no operation moved by 1% of the time
where the time goes in v11:
time: 64.2 us; the launch traced here: 64 us
  Pallas kernels  62.1 us (97%)
  between operations  1.94 us (3%)
    pallas_call x1, Pallas kernels, whole(): pl.pallas_call(functools.partial(whole_kernel, scale), out_shape=(pltpu.V...  41.2 us
    pallas_call x1, Pallas kernels, halo(): pl.pallas_call(halo_kernel, out_shape=(pltpu.VMEM((512, 2 * WIDE), BF), p...  19.3 us
    pallas_call x1, Pallas kernels, finish(): pl.pallas_call(finish_kernel, out_shape=(jax.ShapeDtypeStruct((C, 512), B...  1.58 us

profile of v11, /device:TPU:1, one launch (start us, length us, event | category | flops | bytes accessed | tf_op | source)
XLA Modules:
  0.0 64.0 jit_solution(10571957389042463767)
XLA Ops:
  1.9 19.3 %halo.1 = (bf16[512,256]{1,0:T(8,128)(2,1)S(1)}, bf16[256,256]{1,0:T(8,128)(2,1)S(1)}, bf16[3,1152,128]{2,1,0:T(8,128)(2,1)S(1)}, bf16[3,1152,128]{2,1,0:T(8,128)(2,1)S(1)}) custom-call(s32[1]{0:T(128)} %bitcast.6.position_ref, s32[1]{0:T(128)} %bitcast.8.count_ref, bf16[96,512]{1,0:T(8,128)(2,1)} %bitcast.9, bf16[96,512]{1,0:T(8,128)(2,1)} %bitcast.10, ...), custom_call_target="tpu_custom_call" | custom-call | tf_op jit(solution)/shard_map/halo/pallas_call | solution.py:451
  21.2 41.2 %whole.1 = (bf16[96,512]{1,0:T(8,128)(2,1)S(1)}, f32[27,96,96]{2,1,0:T(8,128)S(1)}, f32[27,96,96]{2,1,0:T(8,128)S(1)}) custom-call(s32[1]{0:T(128)} %bitcast.7.position_ref, bf16[27,96,96]{2,1,0:T(8,128)(2,1)} %first_hbm.3, bf16[512,256]{1,0:T(8,128)(2,1)S(1)} %get-tuple-element.13.rows_ref, bf16[256,256]{1,0:T(8,128)(2,1)S(1)} %get-tuple-element.14.into_ref, ...), custom_call_target="tpu_custom_call" | custom-call | tf_op jit(solution)/shard_map/whole/pallas_call | solution.py:558
  62.4 1.6 %finish.1 = (bf16[96,512]{1,0:T(8,128)(2,1)}, f32[27,96,96]{2,1,0:T(8,128)}, f32[27,96,96]{2,1,0:T(8,128)}) custom-call(bf16[96,512]{1,0:T(8,128)(2,1)S(1)} %get-tuple-element.17.grad_ref, f32[27,96,96]{2,1,0:T(8,128)S(1)} %get-tuple-element.18.first_ref, f32[27,96,96]{2,1,0:T(8,128)S(1)} %get-tuple-element.19.second_ref), custom_call_target="tpu_custom_call" | custom-call | tf_op jit(solution)/shard_map/finish/pallas_call | solution.py:603
